TPU v7x, 32 devices: a whole 2x2x4 slice. The times are simulated.
32 devices in a mesh: dp: 4 (over y, x), fsdp: 8 (over z, core).
Axes of the slice: x: 2, y: 2, z: 4, core: 2. Of those that a mesh axis runs over, the one named last changes fastest.
Arguments:
- text_ids: int32 [32, 128], P(('dp', 'fsdp')), may hold values from 0 to 15999
- text_segments: int32 [32, 128], P(('dp', 'fsdp')), may hold values from 0 to 1, never falling along the last dimension, each value on 1 to 127 neighbouring positions
- codes: int32 [64, 256], P(('dp', 'fsdp')), may hold values from 0 to 8191
- caption_of: int32 [64], P(('dp', 'fsdp')), may hold values from 0 to 1
- mix_in: float32 [3, 1024, 3072], P(None, ('dp', 'fsdp')), may hold values from -0.1875 to 0.1875
- mix_out: float32 [3, 1024, 1024], P(None, ('dp', 'fsdp')), may hold values from -1.5 to 1.5
- ffn_up: float32 [2, 1024, 4096], P(None, ('dp', 'fsdp')), may hold values from -0.1875 to 0.1875
- ffn_down: float32 [2, 4096, 1024], P(None, ('dp', 'fsdp')), may hold values from -0.09375 to 0.09375
- norm_gains: float32 [7, 1024], P(None, ('dp', 'fsdp')), may hold values from 0 to 3, as said below
- text_table: float32 [16000, 1024], P(('dp', 'fsdp')), may hold values from -0.1875 to 0.1875
- code_table: float32 [8192, 1024], P('fsdp', 'dp'), may hold values from -2 to 2
- mix_in_first: float32 [3, 1024, 3072], P(None, ('dp', 'fsdp')), may hold values from -3.8146973e-05 to 3.8146973e-05
- mix_out_first: float32 [3, 1024, 1024], P(None, ('dp', 'fsdp')), may hold values from -3.8146973e-05 to 3.8146973e-05
- ffn_up_first: float32 [2, 1024, 4096], P(None, ('dp', 'fsdp')), may hold values from -3.8146973e-05 to 3.8146973e-05
- ffn_down_first: float32 [2, 4096, 1024], P(None, ('dp', 'fsdp')), may hold values from -3.8146973e-05 to 3.8146973e-05
- gains_first: float32 [7, 1024], P(None, ('dp', 'fsdp')), may hold values from -0.00015258789 to 0.00015258789
- text_first: float32 [16000, 1024], P(('dp', 'fsdp')), may hold values from -3.8146973e-05 to 3.8146973e-05
- code_first: float32 [8192, 1024], P('fsdp', 'dp'), may hold values from -3.8146973e-05 to 3.8146973e-05
- mix_in_second: float32 [3, 1024, 3072], P(None, ('dp', 'fsdp')), may hold values from 7.3e-12 to 2.9e-11
- mix_out_second: float32 [3, 1024, 1024], P(None, ('dp', 'fsdp')), may hold values from 7.3e-12 to 2.9e-11
- ffn_up_second: float32 [2, 1024, 4096], P(None, ('dp', 'fsdp')), may hold values from 7.3e-12 to 2.9e-11
- ffn_down_second: float32 [2, 4096, 1024], P(None, ('dp', 'fsdp')), may hold values from 7.3e-12 to 2.9e-11
- gains_second: float32 [7, 1024], P(None, ('dp', 'fsdp')), may hold values from 1.2e-10 to 4.8e-10
- text_second: float32 [16000, 1024], P(('dp', 'fsdp')), may hold values from 7.3e-12 to 2.9e-11
- code_second: float32 [8192, 1024], P('fsdp', 'dp'), may hold values from 7.3e-12 to 2.9e-11
Outputs:
- loss_sum: float32 [], replicated
- grad_norm: float32 [], replicated
- mix_in_new: float32 [3, 1024, 3072], P(None, ('dp', 'fsdp'))
- mix_out_new: float32 [3, 1024, 1024], P(None, ('dp', 'fsdp'))
- ffn_up_new: float32 [2, 1024, 4096], P(None, ('dp', 'fsdp'))
- ffn_down_new: float32 [2, 4096, 1024], P(None, ('dp', 'fsdp'))
- gains_new: float32 [7, 1024], P(None, ('dp', 'fsdp'))
- text_new: float32 [16000, 1024], P(('dp', 'fsdp'))
- code_new: float32 [8192, 1024], P('fsdp', 'dp')
- mix_in_first_new: float32 [3, 1024, 3072], P(None, ('dp', 'fsdp'))
- mix_out_first_new: float32 [3, 1024, 1024], P(None, ('dp', 'fsdp'))
- ffn_up_first_new: float32 [2, 1024, 4096], P(None, ('dp', 'fsdp'))
- ffn_down_first_new: float32 [2, 4096, 1024], P(None, ('dp', 'fsdp'))
- gains_first_new: float32 [7, 1024], P(None, ('dp', 'fsdp'))
- text_first_new: float32 [16000, 1024], P(('dp', 'fsdp'))
- code_first_new: float32 [8192, 1024], P('fsdp', 'dp')
- mix_in_second_new: float32 [3, 1024, 3072], P(None, ('dp', 'fsdp'))
- mix_out_second_new: float32 [3, 1024, 1024], P(None, ('dp', 'fsdp'))
- ffn_up_second_new: float32 [2, 1024, 4096], P(None, ('dp', 'fsdp'))
- ffn_down_second_new: float32 [2, 4096, 1024], P(None, ('dp', 'fsdp'))
- gains_second_new: float32 [7, 1024], P(None, ('dp', 'fsdp'))
- text_second_new: float32 [16000, 1024], P(('dp', 'fsdp'))
- code_second_new: float32 [8192, 1024], P('fsdp', 'dp')
Inputs may be any that keep to these rules, and one draw needn't show every extreme that they name: `text_segments`: in each row the segment numbers run 0 to 1 in order, every one present. Image i reads segment caption_of[i] of caption row i // 2. `norm_gains`: positive gains.
All inputs are finite; a program needn't handle non-finite values.
Results may differ from a plain program's by a relative error of at most 0.017.
Values may be sent and summed in bfloat16 or wider, within the bound.
A program may use at most 512 MiB of HBM per device.

v0:
```python
from functools import partial
import math

import jax
import jax.numpy as jnp
from jax import lax
from jax.sharding import PartitionSpec as P

D = 1024
HEADS = 16
HEAD = 64
VOCAB = 8192
TVOC = 16000
IMG_LEN = 256
TXT_LEN = 128
STEP = 5


SMOOTH = 0.1
BETA_ONE = 0.5
BETA_TWO = 0.5
WEIGHT_DECAY = 0.1
ADAM_EPS = 1e-08
CLIP_NORM = 0.02
MASKED = -1e30
STEP_RATES = (0.02, 0.15, 0.02, 0.01, 0.3, 0.02, 0.03)


def combined_all(x, axis, join):
    gathered = jax.tree.map(
        lambda a, kind: lax.all_gather(a.astype(kind), axis), x, (jnp.bfloat16, jnp.bfloat16)
    )

    def take(source):
        return jax.tree.map(
            lambda a, own: lax.dynamic_index_in_dim(a, source, 0, False).astype(own.dtype),
            gathered,
            x,
        )

    return lax.fori_loop(
        1, lax.axis_size(axis), lambda source, state: join(state, take(source)), take(0)
    )


def layer_norm(stream, gain):
    centred = stream - jnp.mean(stream, axis=-1, keepdims=True)
    return centred * lax.rsqrt(jnp.mean(centred * centred, axis=-1, keepdims=True) + 1e-05) * gain


def norm_back(stream, gain, grad_out):
    _, pullback = jax.vjp(layer_norm, stream, gain)
    return pullback(grad_out)


def positions(length, width):
    position = jnp.arange(length, dtype=jnp.float32)[:, None]
    speeds = jnp.exp(
        -math.log(10000.0) * 2.0 * jnp.arange(width // 2, dtype=jnp.float32)[None, :] / width
    )
    return jnp.concatenate([jnp.sin(position * speeds), jnp.cos(position * speeds)], axis=1)


def matmul(first_op, second_op):
    return jnp.dot(first_op, second_op, preferred_element_type=jnp.float32)


def across(first_op, second_op):
    return lax.dot_general(
        first_op, second_op, (((0,), (0,)), ((), ())), preferred_element_type=jnp.float32
    )


def against(first_op, second_op):
    return lax.dot_general(
        first_op, second_op, (((1,), (1,)), ((), ())), preferred_element_type=jnp.float32
    )


def head_split(matrix):
    return matrix.reshape(matrix.shape[0], HEADS, HEAD)


def score_block(queries, keys_in, visible):
    scores = jnp.einsum(
        "qhd,khd->hqk", head_split(queries), head_split(keys_in), preferred_element_type=jnp.float32
    ) * HEAD ** (-0.5)
    return jnp.where(visible[None], scores, MASKED)


def attend_block(inputs):
    queries, keys_in, values, visible = inputs
    scores = score_block(queries, keys_in, visible)
    top_score = jnp.max(scores, axis=-1, keepdims=True)
    weights = jnp.exp(scores - top_score)
    totals = jnp.sum(weights, axis=-1, keepdims=True)
    shares = (weights / totals).astype(jnp.bfloat16)
    attended = jnp.einsum(
        "hqk,khd->qhd", shares, head_split(values), preferred_element_type=jnp.float32
    )
    return (
        attended.reshape(queries.shape).astype(jnp.bfloat16),
        top_score[..., 0] + jnp.log(totals[..., 0]),
    )


def attend_back(inputs):
    queries, keys_in, values, visible, log_total, grad_mixed = inputs
    scores = score_block(queries, keys_in, visible)
    shares = jnp.exp(scores - log_total[..., None])
    grad_heads = head_split(grad_mixed)
    grad_shares = jnp.einsum(
        "qhd,khd->hqk", grad_heads, head_split(values), preferred_element_type=jnp.float32
    )
    grad_scores = (
        shares * (grad_shares - jnp.sum(shares * grad_shares, axis=-1, keepdims=True))
    ).astype(jnp.bfloat16)
    grad_query = jnp.einsum(
        "hqk,khd->qhd", grad_scores, head_split(keys_in), preferred_element_type=jnp.float32
    ) * HEAD ** (-0.5)
    grad_keys = jnp.einsum(
        "hqk,qhd->khd", grad_scores, head_split(queries), preferred_element_type=jnp.float32
    ) * HEAD ** (-0.5)
    grad_values = jnp.einsum(
        "hqk,qhd->khd", shares.astype(jnp.bfloat16), grad_heads, preferred_element_type=jnp.float32
    )
    return (
        grad_query.reshape(queries.shape),
        grad_keys.reshape(keys_in.shape),
        grad_values.reshape(values.shape),
    )


def attention(queries, keys_in, values, visible):
    blocks = visible.shape[0]
    attended, log_total = lax.map(
        attend_block, (queries.reshape(blocks, -1, queries.shape[1]), keys_in, values, visible)
    )
    return (attended.reshape(queries.shape), log_total)


def attention_back(queries, keys_in, values, visible, log_total, grad_mixed):
    blocks = visible.shape[0]
    width = queries.shape[1]
    grad_query, grad_keys, grad_values = lax.map(
        attend_back,
        (
            queries.reshape(blocks, -1, width),
            keys_in,
            values,
            visible,
            log_total,
            grad_mixed.reshape(blocks, -1, width),
        ),
    )
    return (grad_query.reshape(queries.shape), grad_keys, grad_values)


def gather_layer(stack_in, stack_out, up_one, down_one, gains_part):
    return (
        lax.all_gather(stack_in.astype(jnp.bfloat16), ("dp", "fsdp"), axis=1, tiled=True),
        lax.all_gather(stack_out.astype(jnp.bfloat16), ("dp", "fsdp"), axis=1, tiled=True),
        lax.all_gather(up_one.astype(jnp.bfloat16), ("dp", "fsdp"), axis=0, tiled=True),
        lax.all_gather(down_one.astype(jnp.bfloat16), ("dp", "fsdp"), axis=0, tiled=True),
        lax.all_gather(gains_part.astype(jnp.bfloat16), ("dp", "fsdp"), axis=1, tiled=True),
    )


def backward_weights(stack_in, stack_out, up_one, down_one, gains_part):
    return (
        lax.all_gather(stack_in.astype(jnp.bfloat16), ("dp", "fsdp"), axis=1, tiled=True),
        lax.all_gather(stack_out.astype(jnp.bfloat16), ("dp", "fsdp"), axis=1, tiled=True),
        lax.all_gather(up_one.astype(jnp.bfloat16), ("dp", "fsdp"), axis=0, tiled=True),
        lax.all_gather(down_one.astype(jnp.bfloat16), ("dp", "fsdp"), axis=0, tiled=True),
        lax.all_gather(gains_part.astype(jnp.bfloat16), ("dp", "fsdp"), axis=1, tiled=True),
    )


def reduce_grads(gradients):
    return (
        lax.psum_scatter(gradients[0], ("dp", "fsdp"), scatter_dimension=1, tiled=True),
        lax.psum_scatter(gradients[1], ("dp", "fsdp"), scatter_dimension=1, tiled=True),
        lax.psum_scatter(gradients[2], ("dp", "fsdp"), scatter_dimension=0, tiled=True),
        lax.psum_scatter(gradients[3], ("dp", "fsdp"), scatter_dimension=0, tiled=True),
        lax.psum_scatter(gradients[4], ("dp", "fsdp"), scatter_dimension=1, tiled=True),
    )


def layer_forward(stream, weights, self_visible, memory, cross_visible):
    mix_in, mix_out, ffn_up, ffn_down, gain_rows = weights
    gain_rows = gain_rows.astype(jnp.float32)
    width = stream.shape[1]
    blocks = self_visible.shape[0]
    stored = {"stream": stream}
    normed = layer_norm(stream, gain_rows[0]).astype(jnp.bfloat16)
    project = matmul(normed, mix_in[0]).astype(jnp.bfloat16)
    queries, keys_in, values = jnp.split(project, 3, axis=1)
    keys_in = keys_in.reshape(blocks, -1, width)
    values = values.reshape(blocks, -1, width)
    attended, log_total = attention(queries, keys_in, values, self_visible)
    stream = stream + matmul(attended, mix_out[0])
    stored.update(
        normed=normed,
        queries=queries,
        keys_in=keys_in,
        values=values,
        attended=attended,
        log_total=log_total,
        after_self=stream,
    )
    if memory is not None:
        cross_in = layer_norm(stream, gain_rows[1]).astype(jnp.bfloat16)
        cross_query = matmul(cross_in, mix_in[1][:, :width]).astype(jnp.bfloat16)
        memory_kv = matmul(memory, mix_in[1][:, width:]).astype(jnp.bfloat16)
        memory_keys, memory_values = jnp.split(memory_kv, 2, axis=1)
        stacked_shape = (blocks,) + memory_keys.shape
        memory_keys = jnp.broadcast_to(memory_keys, stacked_shape)
        memory_values = jnp.broadcast_to(memory_values, stacked_shape)
        cross_mixed, cross_total = attention(cross_query, memory_keys, memory_values, cross_visible)
        stream = stream + matmul(cross_mixed, mix_out[1])
        stored.update(
            cross_in=cross_in,
            cross_query=cross_query,
            memory_keys=memory_keys,
            memory_values=memory_values,
            cross_mixed=cross_mixed,
            cross_total=cross_total,
        )
    stored["before_ffn"] = stream
    ffn_in = layer_norm(stream, gain_rows[-2]).astype(jnp.bfloat16)
    hidden_pre = matmul(ffn_in, ffn_up)
    hidden = jax.nn.gelu(hidden_pre, approximate=True).astype(jnp.bfloat16)
    stream = stream + matmul(hidden, ffn_down)
    stored.update(ffn_in=ffn_in, hidden_pre=hidden_pre, hidden=hidden, before_final=stream)
    return (layer_norm(stream, gain_rows[-1]).astype(jnp.bfloat16), stored)


def layer_backward(grad_final, weights, stored, self_visible, memory, cross_visible):
    mix_in, mix_out, ffn_up, ffn_down, gain_rows = weights
    gain_rows = gain_rows.astype(jnp.float32)
    width = grad_final.shape[1]
    gain_grads = [None] * gain_rows.shape[0]
    grad_stream, gain_grads[-1] = norm_back(stored["before_final"], gain_rows[-1], grad_final)
    grad_low = grad_stream.astype(jnp.bfloat16)
    grad_down = across(stored["hidden"], grad_low)
    grad_hidden = against(grad_low, ffn_down)
    _, gelu_pull = jax.vjp(partial(jax.nn.gelu, approximate=True), stored["hidden_pre"])
    grad_pre = gelu_pull(grad_hidden)[0].astype(jnp.bfloat16)
    grad_up = across(stored["ffn_in"], grad_pre)
    grad_normed, gain_grads[-2] = norm_back(
        stored["before_ffn"], gain_rows[-2], against(grad_pre, ffn_up)
    )
    grad_stream = grad_stream + grad_normed
    in_grads = []
    out_grads = []
    grad_memory = None
    if memory is not None:
        grad_low = grad_stream.astype(jnp.bfloat16)
        out_grads.append(across(stored["cross_mixed"], grad_low))
        grad_mixed = against(grad_low, mix_out[1]).astype(jnp.bfloat16)
        grad_query, grad_keys, grad_values = attention_back(
            stored["cross_query"],
            stored["memory_keys"],
            stored["memory_values"],
            cross_visible,
            stored["cross_total"],
            grad_mixed,
        )
        grad_query = grad_query.astype(jnp.bfloat16)
        grad_memory_kv = jnp.concatenate(
            [jnp.sum(grad_keys, axis=0), jnp.sum(grad_values, axis=0)], axis=1
        ).astype(jnp.bfloat16)
        in_grads.append(
            jnp.concatenate(
                [across(stored["cross_in"], grad_query), across(memory, grad_memory_kv)], axis=1
            )
        )
        grad_memory = against(grad_memory_kv, mix_in[1][:, width:])
        grad_normed, gain_grads[1] = norm_back(
            stored["after_self"], gain_rows[1], against(grad_query, mix_in[1][:, :width])
        )
        grad_stream = grad_stream + grad_normed
    grad_low = grad_stream.astype(jnp.bfloat16)
    out_grads.insert(0, across(stored["attended"], grad_low))
    grad_mixed = against(grad_low, mix_out[0]).astype(jnp.bfloat16)
    grad_query, grad_keys, grad_values = attention_back(
        stored["queries"],
        stored["keys_in"],
        stored["values"],
        self_visible,
        stored["log_total"],
        grad_mixed,
    )
    grad_project = jnp.concatenate(
        [grad_query, grad_keys.reshape(-1, width), grad_values.reshape(-1, width)], axis=1
    ).astype(jnp.bfloat16)
    in_grads.insert(0, across(stored["normed"], grad_project))
    grad_normed, gain_grads[0] = norm_back(
        stored["stream"], gain_rows[0], against(grad_project, mix_in[0])
    )
    grad_stream = grad_stream + grad_normed
    return (
        grad_stream,
        grad_memory,
        (jnp.stack(in_grads), jnp.stack(out_grads), grad_up, grad_down, jnp.stack(gain_grads)),
    )


def combine_stats(earlier, latter):
    top_score = jnp.maximum(earlier[0], latter[0])
    summed = earlier[1] * jnp.exp(earlier[0] - top_score) + latter[1] * jnp.exp(
        latter[0] - top_score
    )
    return (top_score, summed)


def adam_step(weight, moment_one, second, gradient, rate):
    moment_one = BETA_ONE * moment_one + (1.0 - BETA_ONE) * gradient
    second = BETA_TWO * second + (1.0 - BETA_TWO) * gradient * gradient
    first_hat = moment_one / (1.0 - BETA_ONE**STEP)
    second_hat = second / (1.0 - BETA_TWO**STEP)
    weight = weight - rate * (first_hat / (jnp.sqrt(second_hat) + ADAM_EPS) + WEIGHT_DECAY * weight)
    return (weight, moment_one, second)


def on_device(
    text_ids,
    text_segments,
    codes,
    caption_of,
    mix_in,
    mix_out,
    ffn_up,
    ffn_down,
    norm_gains,
    text_table,
    code_table,
    mix_in_first,
    mix_out_first,
    ffn_up_first,
    ffn_down_first,
    gains_first,
    text_first,
    code_first,
    mix_in_second,
    mix_out_second,
    ffn_up_second,
    ffn_down_second,
    gains_second,
    text_second,
    code_second,
):
    image_count = codes.shape[0]
    token_total = image_count * IMG_LEN * lax.axis_size("dp") * lax.axis_size("fsdp")
    inverse = 1.0 / token_total
    scale_in = math.sqrt(D)
    segments = text_segments[0]
    text_visible = (segments[:, None] == segments[None, :])[None]
    blocks = image_count // 2
    rows_block = 2 * IMG_LEN
    position = jnp.arange(rows_block)
    image_of = position // IMG_LEN
    self_one = (image_of[:, None] == image_of[None, :]) & (position[None, :] <= position[:, None])
    self_visible = jnp.broadcast_to(self_one, (blocks, rows_block, rows_block))
    wanted = jnp.repeat(caption_of, IMG_LEN).reshape(blocks, rows_block)
    cross_visible = segments[None, None, :] == wanted[:, :, None]
    text_full = lax.all_gather(text_table.astype(jnp.bfloat16), ("dp", "fsdp"), axis=0, tiled=True)
    text_in = text_full[text_ids[0]].astype(jnp.float32) * scale_in + positions(TXT_LEN, D)
    enc_weights = gather_layer(mix_in[0:1], mix_out[0:1], ffn_up[0], ffn_down[0], norm_gains[0:3])
    memory, enc_stored = layer_forward(text_in, enc_weights, text_visible, None, None)
    code_cols = lax.all_gather(code_table.astype(jnp.bfloat16), "dp", axis=1, tiled=True)
    code_full = lax.all_gather(code_cols, "fsdp", axis=0, tiled=True)
    looked = code_full[codes].astype(jnp.float32) * scale_in
    shifted = jnp.concatenate([jnp.zeros_like(looked[:, :1]), looked[:, :-1]], axis=1)
    image_in = (shifted + positions(IMG_LEN, D)[None]).reshape(-1, D)
    dec_weights = gather_layer(mix_in[1:3], mix_out[1:3], ffn_up[1], ffn_down[1], norm_gains[3:7])
    final_out, dec_stored = layer_forward(
        image_in, dec_weights, self_visible, memory, cross_visible
    )
    targets = codes.reshape(-1)
    group_rows = lax.all_gather(final_out, "fsdp", axis=0, tiled=True)
    group_targets = lax.all_gather(targets, "fsdp", axis=0, tiled=True)
    columns = lax.axis_index("fsdp") * code_cols.shape[0] + jnp.arange(code_cols.shape[0])
    target_hit = group_targets[:, None] == columns[None, :]
    logits = against(group_rows, code_cols)
    top_local = jnp.max(logits, axis=1)
    statistics = combined_all(
        (top_local, jnp.sum(jnp.exp(logits - top_local[:, None]), axis=1)), "fsdp", combine_stats
    )
    log_total = statistics[0] + jnp.log(statistics[1])
    own_total = lax.dynamic_slice_in_dim(
        log_total, lax.axis_index("fsdp") * targets.shape[0], targets.shape[0]
    )
    own_final = final_out.astype(jnp.float32)
    picked = jnp.sum(own_final * code_full[targets].astype(jnp.float32), axis=1)
    column_sum = matmul(jnp.ones((1, code_full.shape[0]), jnp.bfloat16), code_full)[0]
    logit_sum = jnp.sum(own_final * column_sum[None, :], axis=1)
    loss_part = jnp.sum(own_total - (1.0 - SMOOTH) * picked - SMOOTH * logit_sum / VOCAB)
    grad_logits = (
        (
            jnp.exp(logits - log_total[:, None])
            - jnp.where(target_hit, 1.0 - SMOOTH, 0.0)
            - SMOOTH / VOCAB
        )
        * inverse
    ).astype(jnp.bfloat16)
    grad_final = lax.psum_scatter(
        matmul(grad_logits, code_cols).astype(jnp.bfloat16), "fsdp", scatter_dimension=0, tiled=True
    ).astype(jnp.float32)
    head_grad = across(grad_logits, group_rows)
    grad_image, grad_memory, dec_grads = layer_backward(
        grad_final,
        backward_weights(mix_in[1:3], mix_out[1:3], ffn_up[1], ffn_down[1], norm_gains[3:7]),
        dec_stored,
        self_visible,
        memory,
        cross_visible,
    )
    dec_grads = reduce_grads(dec_grads)
    grad_looked = grad_image.reshape(image_count, IMG_LEN, D)[:, 1:] * scale_in
    lookup = jnp.zeros((VOCAB, D), jnp.float32).at[codes[:, :-1]].add(grad_looked)
    rows_grad = lax.psum_scatter(
        lookup.astype(jnp.bfloat16), "fsdp", scatter_dimension=0, tiled=True
    ).astype(jnp.float32)
    rows_grad = rows_grad + head_grad
    code_grad = lax.psum_scatter(
        rows_grad.astype(jnp.bfloat16), "dp", scatter_dimension=1, tiled=True
    ).astype(jnp.float32)
    grad_text, _, enc_grads = layer_backward(
        grad_memory,
        backward_weights(mix_in[0:1], mix_out[0:1], ffn_up[0], ffn_down[0], norm_gains[0:3]),
        enc_stored,
        text_visible,
        None,
        None,
    )
    enc_grads = reduce_grads(enc_grads)
    text_lookup = jnp.zeros((TVOC, D), jnp.float32).at[text_ids[0]].add(grad_text * scale_in)
    text_grad = lax.psum_scatter(text_lookup, ("dp", "fsdp"), scatter_dimension=0, tiled=True)
    gradients = (
        jnp.concatenate([enc_grads[0], dec_grads[0]], axis=0),
        jnp.concatenate([enc_grads[1], dec_grads[1]], axis=0),
        jnp.stack([enc_grads[2], dec_grads[2]]),
        jnp.stack([enc_grads[3], dec_grads[3]]),
        jnp.concatenate([enc_grads[4], dec_grads[4]], axis=0),
        text_grad,
        code_grad,
    )
    square_part = sum((jnp.sum(gradient * gradient) for gradient in gradients))
    loss_sum, square_sum = lax.psum((loss_part, square_part), ("dp", "fsdp"))
    grad_norm = jnp.sqrt(square_sum)
    factor = CLIP_NORM / jnp.maximum(grad_norm, CLIP_NORM)
    params = (mix_in, mix_out, ffn_up, ffn_down, norm_gains, text_table, code_table)
    firsts = (
        mix_in_first,
        mix_out_first,
        ffn_up_first,
        ffn_down_first,
        gains_first,
        text_first,
        code_first,
    )
    seconds = (
        mix_in_second,
        mix_out_second,
        ffn_up_second,
        ffn_down_second,
        gains_second,
        text_second,
        code_second,
    )
    updated = [
        adam_step(
            params[index],
            firsts[index],
            seconds[index],
            gradients[index] * factor,
            STEP_RATES[index],
        )
        for index in range(7)
    ]
    return (
        loss_sum,
        grad_norm,
        updated[0][0],
        updated[1][0],
        updated[2][0],
        updated[3][0],
        updated[4][0],
        updated[5][0],
        updated[6][0],
        updated[0][1],
        updated[1][1],
        updated[2][1],
        updated[3][1],
        updated[4][1],
        updated[5][1],
        updated[6][1],
        updated[0][2],
        updated[1][2],
        updated[2][2],
        updated[3][2],
        updated[4][2],
        updated[5][2],
        updated[6][2],
    )


def solution(mesh):
    return jax.shard_map(
        on_device,
        mesh=mesh,
        in_specs=(
            P(("dp", "fsdp"), None),
            P(("dp", "fsdp"), None),
            P(("dp", "fsdp"), None),
            P(("dp", "fsdp")),
            P(None, ("dp", "fsdp"), None),
            P(None, ("dp", "fsdp"), None),
            P(None, ("dp", "fsdp"), None),
            P(None, ("dp", "fsdp"), None),
            P(None, ("dp", "fsdp")),
            P(("dp", "fsdp"), None),
            P("fsdp", "dp"),
            P(None, ("dp", "fsdp"), None),
            P(None, ("dp", "fsdp"), None),
            P(None, ("dp", "fsdp"), None),
            P(None, ("dp", "fsdp"), None),
            P(None, ("dp", "fsdp")),
            P(("dp", "fsdp"), None),
            P("fsdp", "dp"),
            P(None, ("dp", "fsdp"), None),
            P(None, ("dp", "fsdp"), None),
            P(None, ("dp", "fsdp"), None),
            P(None, ("dp", "fsdp"), None),
            P(None, ("dp", "fsdp")),
            P(("dp", "fsdp"), None),
            P("fsdp", "dp"),
        ),
        out_specs=(
            P(),
            P(),
            P(None, ("dp", "fsdp"), None),
            P(None, ("dp", "fsdp"), None),
            P(None, ("dp", "fsdp"), None),
            P(None, ("dp", "fsdp"), None),
            P(None, ("dp", "fsdp")),
            P(("dp", "fsdp"), None),
            P("fsdp", "dp"),
            P(None, ("dp", "fsdp"), None),
            P(None, ("dp", "fsdp"), None),
            P(None, ("dp", "fsdp"), None),
            P(None, ("dp", "fsdp"), None),
            P(None, ("dp", "fsdp")),
            P(("dp", "fsdp"), None),
            P("fsdp", "dp"),
            P(None, ("dp", "fsdp"), None),
            P(None, ("dp", "fsdp"), None),
            P(None, ("dp", "fsdp"), None),
            P(None, ("dp", "fsdp"), None),
            P(None, ("dp", "fsdp")),
            P(("dp", "fsdp"), None),
            P("fsdp", "dp"),
        ),
        check_vma=False,
    )
```

profile of v0, /device:TPU:0, one launch (start us, length us, event | category | flops | bytes accessed | tf_op | source)
XLA Modules:
  0.0 3554.7 jit_solution(7385021680921752330)
XLA Ops:
  11.3 37.1 %all-gather.23.cloned.1.call-done = bf16[1024,1024]{1,0:T(8,128)(2,1)} async-done(((bf16[1024,256]{1,0:T(8,128)(2,1)}), bf16[1024,1024]{1,0:T(8,128)(2,1)}) %all-gather.23.cloned.1.call-update) | async-done | bytes 2097168 | tf_op jit(solution)/shard_map/all_gather | solution.py:371
  60.2 41.0 %all-gather.6 = bf16[32,32,4]{1,2,0:T(4,128)(2,1)S(1)} all-gather(bf16[1,32,4]{1,2,0:T(4,128)(2,1)S(1)} %slice_bitcast_fusion.21), channel_id=1, replica_groups=mesh['dp'=4,'fsdp'=8] {'dp','fsdp'}, dimensions={0}, use_global_device_ids=true | all-gather | bytes 8448 | tf_op jit(solution)/shard_map/all_gather | solution.py:165
  101.2 37.1 %all-gather.8 = bf16[32,32,3]{1,2,0:T(4,128)(2,1)S(1)} all-gather(bf16[1,32,3]{1,2,0:T(4,128)(2,1)S(1)} %slice_bitcast_fusion.20), channel_id=1, replica_groups=mesh['dp'=4,'fsdp'=8] {'dp','fsdp'}, dimensions={0}, use_global_device_ids=true | all-gather | bytes 6336 | tf_op jit(solution)/shard_map/all_gather | solution.py:165
  139.0 9.1 all-gather.27.cloned.1.call-done
  148.2 5.8 slice_bitcast_fusion
  154.0 145.4 %all-gather.25.cloned.1.call-done = bf16[8192,1024]{1,0:T(8,128)(2,1)} async-done(((bf16[1024,1024]{1,0:T(8,128)(2,1)}), bf16[8192,1024]{1,0:T(8,128)(2,1)}) %all-gather.25.cloned.1.call-update) | async-done | bytes 16777232 | tf_op jit(solution)/shard_map/all_gather | solution.py:372
  299.4 10.9 gather_fusion
  312.9 6.5 fusion.38
  327.6 8.5 fusion.189
  336.1 8.2 fusion.3
  344.9 8.1 fusion.88
  353.1 10.0 all-gather.29.cloned.1.call-done
  371.7 12.4 gather_fusion.2
  384.1 8.1 fusion.137
  392.3 165.3 %all-gather.45.cloned.1.call-done = bf16[32,500,1024]{2,1,0:T(8,128)(2,1)} async-done(((bf16[1,500,1024]{2,1,0:T(8,128)(2,1)}), bf16[32,500,1024]{2,1,0:T(8,128)(2,1)}) %all-gather.45.cloned.1.call-update) | async-done | bytes 32768016 | tf_op jit(solution)/shard_map/all_gather | solution.py:367
  557.5 28.6 reshape.787
  588.8 39.9 %all-gather.31.cloned.1.call-done = bf16[1,1024,3072]{2,1,0:T(8,128)(2,1)} async-done(((bf16[1,32,3072]{2,1,0:T(8,128)(2,1)}), bf16[1,1024,3072]{2,1,0:T(8,128)(2,1)}) %all-gather.31.cloned.1.call-update) | async-done | bytes 6291472 | tf_op jit(solution)/shard_map/all_gather | solution.py:161
  634.9 51.8 %all-gather.33.cloned.1.call-done = bf16[1,1024,1024]{2,1,0:T(8,128)(2,1)} async-done(((bf16[1,32,1024]{2,1,0:T(8,128)(2,1)}), bf16[1,1024,1024]{2,1,0:T(8,128)(2,1)}) %all-gather.33.cloned.1.call-update) | async-done | bytes 2097168 | tf_op jit(solution)/shard_map/all_gather | solution.py:162
  689.0 77.3 %all-gather.37.cloned.1.call-done = bf16[1,1024,4096]{2,1,0:T(8,128)(2,1)} async-done(((bf16[1,32,4096]{2,1,0:T(8,128)(2,1)}), bf16[1,1024,4096]{2,1,0:T(8,128)(2,1)}) %all-gather.37.cloned.1.call-update) | async-done | bytes 8388624 | tf_op jit(solution)/shard_map/all_gather | solution.py:163
  771.1 74.8 %all-gather.39.cloned.1.call-done = bf16[1,4096,1024]{2,1,0:T(8,128)(2,1)} async-done(((bf16[1,128,1024]{2,1,0:T(8,128)(2,1)}), bf16[1,4096,1024]{2,1,0:T(8,128)(2,1)}) %all-gather.39.cloned.1.call-update) | async-done | bytes 8388624 | tf_op jit(solution)/shard_map/all_gather | solution.py:164
  863.5 61.8 %all-gather.41.cloned.1.call-done = bf16[1,1024,4096]{2,1,0:T(8,128)(2,1)} async-done(((bf16[1,32,4096]{2,1,0:T(8,128)(2,1)}), bf16[1,1024,4096]{2,1,0:T(8,128)(2,1)}) %all-gather.41.cloned.1.call-update) | async-done | bytes 8388624 | tf_op jit(solution)/shard_map/all_gather | solution.py:163
  925.2 10.5 fusion.20
  935.7 69.1 %all-gather.43.cloned.1.call-done = bf16[1,4096,1024]{2,1,0:T(8,128)(2,1)} async-done(((bf16[1,128,1024]{2,1,0:T(8,128)(2,1)}), bf16[1,4096,1024]{2,1,0:T(8,128)(2,1)}) %all-gather.43.cloned.1.call-update) | async-done | bytes 8388624 | tf_op jit(solution)/shard_map/all_gather | solution.py:164
  1004.8 11.6 fusion.196
  1020.1 12.8 all-gather.9
  1032.9 67.9 %all-gather.35.cloned.1.call-done = bf16[4096,1024]{1,0:T(8,128)(2,1)} async-done(((bf16[512,1024]{1,0:T(8,128)(2,1)}), bf16[4096,1024]{1,0:T(8,128)(2,1)}) %all-gather.35.cloned.1.call-update) | async-done | bytes 8388624 | tf_op jit(solution)/shard_map/all_gather | solution.py:381
  1100.8 16.1 fusion.197
  1116.9 14.4 all-gather.4
  1131.3 8.0 exponential_reduce_fusion
  1139.4 14.0 all-gather.5
  1154.0 17.4 convolution_convert_fusion
  1174.2 85.4 %reduce-scatter.20.cloned.1.call-done = bf16[512,1024]{1,0:T(8,128)(2,1)} async-done(((bf16[4096,1024]{1,0:T(8,128)(2,1)}), bf16[512,1024]{1,0:T(8,128)(2,1)}) %reduce-scatter.20.cloned.1.call-update) | async-done | bytes 1048592 | tf_op jit(solution)/shard_map/reduce_scatter | solution.py:407
  1263.3 16.0 fusion.11
  1279.3 7.6 multiply_reduce_fusion.3
  1311.9 9.6 fusion.94
  1321.5 13.9 multiply_reduce_fusion
  1335.5 10.3 multiply_convert_fusion
  1345.8 6.2 multiply_convert_fusion.4
  1354.3 6.8 multiply_reduce_fusion.2
  1364.9 18.8 scatter_custom_fusion.1
  1383.8 17.6 convert_element_type.370
  1413.4 7.3 fusion.63
  1429.0 6.0 multiply_reduce_fusion.17
  1450.1 6.5 convolution_bitcast_fusion.1
  1457.2 5.4 fusion.164
  1467.2 10.9 maximum_bitcast_fusion
  1478.1 5.5 convolution_bitcast_fusion
  1483.9 9.2 pad_maximum_fusion
  1493.8 13.4 fusion.165
  1508.4 8.2 fusion.163
  1517.2 15.7 fusion.162
  1533.4 9.8 fusion.161
  1544.7 21.1 broadcast_in_dim.278
  1565.8 18.4 scatter_fusion
  1584.1 16.9 add_convert_fusion
  1601.1 951.2 %fusion = f32[512,1024]{1,0:T(8,128)S(1)} fusion(f32[16000,1024]{1,0:T(8,128)} %scatter_fusion), kind=kCustom, calls=%all-reduce-scatter | all-reduce-scatter fusion | flops 16777216 | bytes 67633152
  2559.0 10.2 concatenate.43
  2575.6 122.3 %reduce-scatter.24.cloned.1.call-done = f32[2,32,3072]{2,1,0:T(8,128)} async-done(((f32[2,1024,3072]{2,1,0:T(8,128)}), f32[2,32,3072]{2,1,0:T(8,128)}) %reduce-scatter.24.cloned.1.call-update) | async-done | bytes 786448 | tf_op jit(solution)/shard_map/reduce_scatter | solution.py:181
  2701.3 185.1 %reduce-scatter.32.cloned.1.call-done = f32[32,4096]{1,0:T(8,128)} async-done(((f32[1024,4096]{1,0:T(8,128)}), f32[32,4096]{1,0:T(8,128)}) %reduce-scatter.32.cloned.1.call-update) | async-done | bytes 524304 | tf_op jit(solution)/shard_map/reduce_scatter | solution.py:183
  2886.4 186.7 %reduce-scatter.30.cloned.1.call-done = f32[32,4096]{1,0:T(8,128)} async-done(((f32[1024,4096]{1,0:T(8,128)}), f32[32,4096]{1,0:T(8,128)}) %reduce-scatter.30.cloned.1.call-update) | async-done | bytes 524304 | tf_op jit(solution)/shard_map/reduce_scatter | solution.py:183
  3075.8 184.0 %reduce-scatter.36.cloned.1.call-done = f32[128,1024]{1,0:T(8,128)} async-done(((f32[4096,1024]{1,0:T(8,128)}), f32[128,1024]{1,0:T(8,128)}) %reduce-scatter.36.cloned.1.call-update) | async-done | bytes 524304 | tf_op jit(solution)/shard_map/reduce_scatter | solution.py:184
  3259.8 186.5 %reduce-scatter.34.cloned.1.call-done = f32[128,1024]{1,0:T(8,128)} async-done(((f32[4096,1024]{1,0:T(8,128)}), f32[128,1024]{1,0:T(8,128)}) %reduce-scatter.34.cloned.1.call-update) | async-done | bytes 524304 | tf_op jit(solution)/shard_map/reduce_scatter | solution.py:184
  3450.5 31.8 reduce-scatter.40.cloned.1.call-done
  3484.8 39.8 %all-reduce.3 = (f32[]{:T(128)}, f32[]{:T(128)}) all-reduce(f32[]{:T(128)} %subtract_reduce_fusion, f32[]{:T(128)S(6)} %add.482), channel_id=1, replica_groups=mesh['dp'=4,'fsdp'=8] {'dp','fsdp'}, use_global_device_ids=true, to_apply=%region_27.28 | all-reduce | flops 2 | bytes 16 | tf_op jit(solution)/shard_map/psum | solution.py:450
  (644 shorter events, 198.2 us)
Async XLA Ops:
  7.2 52.7 %copy-start = (s32[2]{0:T(128)S(1)}, s32[2]{0:T(128)}, u32[]{:S(2)}) copy-start(s32[2]{0:T(128)} %param.30) | copy-start | bytes 28
  7.2 41.1 %all-gather.23.cloned.1.call-start = ((), (), s32[]{:S(2)}) async-start(), calls=%async_computation.13 | async-start | bytes 2621440 | tf_op jit(solution)/shard_map/all_gather | solution.py:371
  9.4 39.0 %copy-start.67 = (f32[3,32,1024]{2,1,0:T(8,128)S(1)}, f32[3,32,1024]{2,1,0:T(8,128)}, u32[]{:S(2)}) copy-start(f32[3,32,1024]{2,1,0:T(8,128)} %param.32) | copy-start | bytes 1179652
  9.5 138.7 %all-gather.27.cloned.1.call-start = ((), (), s32[]{:S(2)}) async-start(), calls=%async_computation.15 | async-start | bytes 12976128 | tf_op jit(solution)/shard_map/all_gather | solution.py:161
  10.4 38.8 %copy-start.36 = (f32[500,1024]{1,0:T(8,128)S(1)}, f32[500,1024]{1,0:T(8,128)}, u32[]{:S(2)}) copy-start(f32[500,1024]{1,0:T(8,128)} %param.36) | copy-start | bytes 6144004
  11.2 288.1 %all-gather.25.cloned.1.call-start = ((), (), s32[]{:S(2)}) async-start(), calls=%async_computation.14 | async-start | bytes 18874368 | tf_op jit(solution)/shard_map/all_gather | solution.py:372
  48.4 314.7 %all-gather.29.cloned.1.call-start = ((), (), s32[]{:S(2)}) async-start(), calls=%async_computation.16 | async-start | bytes 4325376 | tf_op jit(solution)/shard_map/all_gather | solution.py:162
  49.2 508.3 %all-gather.45.cloned.1.call-start = ((), (), s32[]{:S(2)}) async-start(), calls=%async_computation.35 | async-start | bytes 34062336 | tf_op jit(solution)/shard_map/all_gather | solution.py:367
  50.4 578.2 %all-gather.31.cloned.1.call-start = ((), (), s32[]{:S(2)}) async-start(), calls=%async_computation.17 | async-start | bytes 6488064 | tf_op jit(solution)/shard_map/all_gather | solution.py:161
  52.2 634.5 %all-gather.33.cloned.1.call-start = ((), (), s32[]{:S(2)}) async-start(), calls=%async_computation.18 | async-start | bytes 2162688 | tf_op jit(solution)/shard_map/all_gather | solution.py:162
  52.9 713.4 %all-gather.37.cloned.1.call-start = ((), (), s32[]{:S(2)}) async-start(), calls=%async_computation.31 | async-start | bytes 8650752 | tf_op jit(solution)/shard_map/all_gather | solution.py:163
  53.9 792.0 %all-gather.39.cloned.1.call-start = ((), (), s32[]{:S(2)}) async-start(), calls=%async_computation.32 | async-start | bytes 8650752 | tf_op jit(solution)/shard_map/all_gather | solution.py:164
  54.9 870.3 %all-gather.41.cloned.1.call-start = ((), (), s32[]{:S(2)}) async-start(), calls=%async_computation.33 | async-start | bytes 8650752 | tf_op jit(solution)/shard_map/all_gather | solution.py:163
  55.5 949.3 %all-gather.43.cloned.1.call-start = ((), (), s32[]{:S(2)}) async-start(), calls=%async_computation.34 | async-start | bytes 8650752 | tf_op jit(solution)/shard_map/all_gather | solution.py:164
  56.2 1044.6 %all-gather.35.cloned.1.call-start = ((), (), s32[]{:S(2)}) async-start(), calls=%async_computation.19 | async-start | bytes 9437184 | tf_op jit(solution)/shard_map/all_gather | solution.py:381
  59.9 78.6 %copy-start.167 = (s32[128]{0:T(128)}, s32[128]{0:T(128)S(1)}, u32[]{:S(2)}) copy-start(s32[128]{0:T(128)S(1)} %fusion.149) | copy-start | bytes 1540
  138.4 490.2 %copy-start.105 = (f32[1,1024]{1,0:T(1,128)}, f32[1,1024]{1,0:T(1,128)S(1)}, u32[]{:S(2)}) copy-start(f32[1,1024]{1,0:T(1,128)S(1)} %get-tuple-element.402) | copy-start | bytes 12292
  138.4 627.9 %copy-start.101 = (f32[1,1024]{1,0:T(1,128)}, f32[1,1024]{1,0:T(1,128)S(1)}, u32[]{:S(2)}) copy-start(f32[1,1024]{1,0:T(1,128)S(1)} %get-tuple-element.401) | copy-start | bytes 12292
  138.4 712.8 %copy-start.107 = (f32[1,1024]{1,0:T(1,128)}, f32[1,1024]{1,0:T(1,128)S(1)}, u32[]{:S(2)}) copy-start(f32[1,1024]{1,0:T(1,128)S(1)} %get-tuple-element.400) | copy-start | bytes 12292
  138.6 174.0 %copy-start.113 = (f32[1,1024]{1,0:T(1,128)}, f32[1,1024]{1,0:T(1,128)S(1)}, u32[]{:S(2)}) copy-start(f32[1,1024]{1,0:T(1,128)S(1)} %get-tuple-element.399) | copy-start | bytes 12292
  138.6 228.6 %copy-start.137 = (f32[1,1024]{1,0:T(1,128)}, f32[1,1024]{1,0:T(1,128)S(1)}, u32[]{:S(2)}) copy-start(f32[1,1024]{1,0:T(1,128)S(1)} %get-tuple-element.398) | copy-start | bytes 12292
  138.6 1148.4 %copy-start.135 = (f32[1,1024]{1,0:T(1,128)}, f32[1,1024]{1,0:T(1,128)S(1)}, u32[]{:S(2)}) copy-start(f32[1,1024]{1,0:T(1,128)S(1)} %get-tuple-element.396) | copy-start | bytes 12292
  311.0 52.0 %copy-start.6 = (f32[2,256,1024]{2,1,0:T(8,128)}, f32[2,256,1024]{2,1,0:T(8,128)S(1)}, u32[]{:S(2)}) copy-start(f32[2,256,1024]{2,1,0:T(8,128)S(1)} %get-tuple-element.380) | copy-start | bytes 6291460
  588.5 98.1 %copy-start.12 = (f32[128,1024]{1,0:T(8,128)}, f32[128,1024]{1,0:T(8,128)S(1)}, u32[]{:S(2)}) copy-start(f32[128,1024]{1,0:T(8,128)S(1)} %get-tuple-element.378) | copy-start | bytes 1572868
  588.5 44.0 %copy-start.140 = (f32[128]{0:T(128)}, f32[128]{0:T(128)S(1)}, u32[]{:S(2)}) copy-start(f32[128]{0:T(128)S(1)} %broadcast_multiply_fusion.6) | copy-start | bytes 1540
  588.7 43.8 %copy-start.169 = (f32[128]{0:T(128)}, f32[128]{0:T(128)S(1)}, u32[]{:S(2)}) copy-start(f32[128]{0:T(128)S(1)} %multiply_reduce_fusion.25) | copy-start | bytes 1540
  588.8 43.7 %copy-start.142 = (f32[128]{0:T(128)}, f32[128]{0:T(128)S(1)}, u32[]{:S(2)}) copy-start(f32[128]{0:T(128)S(1)} %fusion.150) | copy-start | bytes 1540
  634.8 131.5 %copy-start.73 = (bf16[16,64,128]{2,1,0:T(8,128)(2,1)}, bf16[16,64,128]{2,1,0:T(8,128)(2,1)S(1)}, u32[]{:S(2)}) copy-start(bf16[16,64,128]{2,1,0:T(8,128)(2,1)S(1)} %convolution_convert_fusion.2) | copy-start | bytes 786436
  688.8 157.2 %copy-start.10 = (f32[128,1024]{1,0:T(8,128)}, f32[128,1024]{1,0:T(8,128)S(1)}, u32[]{:S(2)}) copy-start(f32[128,1024]{1,0:T(8,128)S(1)} %get-tuple-element.416) | copy-start | bytes 1572868
  688.8 82.3 %copy-start.118 = (f32[128]{0:T(128)}, f32[128]{0:T(128)S(1)}, u32[]{:S(2)}) copy-start(f32[128]{0:T(128)S(1)} %broadcast_multiply_fusion.5) | copy-start | bytes 1540
  689.0 82.1 %copy-start.171 = (f32[128]{0:T(128)}, f32[128]{0:T(128)S(1)}, u32[]{:S(2)}) copy-start(f32[128]{0:T(128)S(1)} %multiply_reduce_fusion.24) | copy-start | bytes 1540
  689.0 82.0 %copy-start.122 = (f32[128]{0:T(128)}, f32[128]{0:T(128)S(1)}, u32[]{:S(2)}) copy-start(f32[128]{0:T(128)S(1)} %fusion.151) | copy-start | bytes 1540
  771.1 79.9 %copy-start.19 = (f32[128,4096]{1,0:T(8,128)}, f32[128,4096]{1,0:T(8,128)S(1)}, u32[]{:S(2)}) copy-start(f32[128,4096]{1,0:T(8,128)S(1)} %fusion.28) | copy-start | bytes 6291460
  863.1 72.7 %copy-start.29 = (f32[512,1024]{1,0:T(8,128)}, f32[512,1024]{1,0:T(8,128)S(1)}, u32[]{:S(2)}) copy-start(f32[512,1024]{1,0:T(8,128)S(1)} %get-tuple-element.424) | copy-start | bytes 6291460
  863.1 423.9 %copy-start.126 = (f32[512]{0:T(512)}, f32[512]{0:T(512)S(1)}, u32[]{:S(2)}) copy-start(f32[512]{0:T(512)S(1)} %broadcast_multiply_fusion.1) | copy-start | bytes 6148
  863.4 423.5 %copy-start.149 = (f32[512]{0:T(512)}, f32[512]{0:T(512)S(1)}, u32[]{:S(2)}) copy-start(f32[512]{0:T(512)S(1)} %fusion.145) | copy-start | bytes 6148
  1020.0 239.7 %reduce-scatter.20.cloned.1.call-start = ((), (), s32[]{:S(2)}) async-start(), calls=%async_computation.20 | async-start | bytes 9437184 | tf_op jit(solution)/shard_map/reduce_scatter | solution.py:407
  1032.9 121.1 %copy-start.133 = (s32[8,1,512]{2,1,0:T(1,128)}, s32[8,1,512]{2,1,0:T(1,128)S(1)}, u32[]{:S(2)}) copy-start(s32[8,1,512]{2,1,0:T(1,128)S(1)} %all-gather.9) | copy-start | bytes 49156
  1032.9 121.1 %copy-start.163 = (s32[1024]{0:T(1024)}, s32[1024]{0:T(1024)S(1)}, u32[]{:S(2)}) copy-start(s32[1024]{0:T(1024)S(1)} %iota_add_fusion) | copy-start | bytes 12292
  1171.5 412.6 %reduce-scatter.38.cloned.1.call-start = ((), (), s32[]{:S(2)}) async-start(), calls=%async_computation.29 | async-start | bytes 18874368 | tf_op jit(solution)/shard_map/reduce_scatter | solution.py:422
  1174.2 123.7 %copy-start.97 = (f32[16,512]{1,0:T(8,128)}, f32[16,512]{1,0:T(8,128)S(1)}, u32[]{:S(2)}) copy-start(f32[16,512]{1,0:T(8,128)S(1)} %log_add_fusion.1) | copy-start | bytes 98308
  1263.2 24.5 copy-start.34
  1263.2 24.5 copy-start.151
  1311.9 23.5 slice-start
  1311.9 23.5 slice-start.1
  1401.4 1155.3 %reduce-scatter.42.cloned.1.call-start = ((), (), s32[]{:S(2)}) async-start(), calls=%async_computation.36 | async-start | bytes 540672
  1436.0 1121.5 %reduce-scatter.44.cloned.1.call-start = ((), (), s32[]{:S(2)}) async-start(), calls=%async_computation.37 | async-start | bytes 540672
  1437.4 1134.6 %reduce-scatter.26.cloned.1.call-start = ((), (), s32[]{:S(2)}) async-start(), calls=%async_computation.23 | async-start | bytes 4325376 | tf_op jit(solution)/shard_map/reduce_scatter | solution.py:182
  1440.1 1132.8 %reduce-scatter.28.cloned.1.call-start = ((), (), s32[]{:S(2)}) async-start(), calls=%async_computation.24 | async-start | bytes 8650752 | tf_op jit(solution)/shard_map/reduce_scatter | solution.py:182
  1449.0 1125.6 %reduce-scatter.22.cloned.1.call-start = ((), (), s32[]{:S(2)}) async-start(), calls=%async_computation.21 | async-start | bytes 12976128 | tf_op jit(solution)/shard_map/reduce_scatter | solution.py:181
  1456.6 1241.3 %reduce-scatter.24.cloned.1.call-start = ((), (), s32[]{:S(2)}) async-start(), calls=%async_computation.22 | async-start | bytes 25952256 | tf_op jit(solution)/shard_map/reduce_scatter | solution.py:181
  1493.1 1393.3 %reduce-scatter.32.cloned.1.call-start = ((), (), s32[]{:S(2)}) async-start(), calls=%async_computation.26 | async-start | bytes 17301504 | tf_op jit(solution)/shard_map/reduce_scatter | solution.py:183
  1507.2 1565.9 %reduce-scatter.30.cloned.1.call-start = ((), (), s32[]{:S(2)}) async-start(), calls=%async_computation.25 | async-start | bytes 17301504 | tf_op jit(solution)/shard_map/reduce_scatter | solution.py:183
  1516.6 1743.2 %reduce-scatter.36.cloned.1.call-start = ((), (), s32[]{:S(2)}) async-start(), calls=%async_computation.28 | async-start | bytes 17301504 | tf_op jit(solution)/shard_map/reduce_scatter | solution.py:184
  1533.0 1913.3 %reduce-scatter.34.cloned.1.call-start = ((), (), s32[]{:S(2)}) async-start(), calls=%async_computation.27 | async-start | bytes 17301504 | tf_op jit(solution)/shard_map/reduce_scatter | solution.py:184
  1543.2 1939.0 %reduce-scatter.40.cloned.1.call-start = ((), (), s32[]{:S(2)}) async-start(), calls=%async_computation.30 | async-start | bytes 2621440 | tf_op jit(solution)/shard_map/reduce_scatter | solution.py:426
  1544.7 21.1 copy-start.168
  1565.8 18.4 copy-start.134
  2553.6 5.4 collective-permute-start
  2699.0 826.3 %copy-start.132 = (f32[7,32]{1,0:T(8,128)S(1)}, f32[7,32]{1,0:T(8,128)}, u32[]{:S(2)}) copy-start(f32[7,32]{1,0:T(8,128)} %param.35) | copy-start | bytes 2692
  2699.0 826.3 %copy-start.162 = (f32[7,32]{1,0:T(8,128)S(1)}, f32[7,32]{1,0:T(8,128)}, u32[]{:S(2)}) copy-start(f32[7,32]{1,0:T(8,128)} %param.42) | copy-start | bytes 2692
  2699.1 827.8 %copy-start.68 = (f32[3,32,1024]{2,1,0:T(8,128)S(1)}, f32[3,32,1024]{2,1,0:T(8,128)}, u32[]{:S(2)}) copy-start(f32[3,32,1024]{2,1,0:T(8,128)} %param.32) | copy-start | bytes 1179652
  3446.3 82.9 %copy-start.50 = (f32[2,128,1024]{2,1,0:T(8,128)S(1)}, f32[2,128,1024]{2,1,0:T(8,128)}, u32[]{:S(2)}) copy-start(f32[2,128,1024]{2,1,0:T(8,128)} %param.34) | copy-start | bytes 3145732
  3446.3 82.9 %copy-start.63 = (f32[128,1024]{1,0:T(8,128)S(1)}, f32[128,1024]{1,0:T(8,128)}, u32[]{:S(2)}) copy-start(f32[128,1024]{1,0:T(8,128)} %reduce-scatter.36.cloned.1.call-done) | copy-start | bytes 1572868
  (152 other events, 647.3 us)
Sparse Core Ops, SparseCore 0:
  10.5 37.8 all-gather.22
  52.0 96.1 all-gather.26
  149.8 149.5 all-gather.24
  302.8 60.1 all-gather.28
  366.5 190.9 all-gather.44
  560.9 67.6 all-gather.30
  631.6 54.9 all-gather.32
  690.2 76.1 all-gather.36
  769.9 75.9 all-gather.38
  849.3 75.8 all-gather.40
  928.8 75.9 all-gather.42
  1020.1 80.6 all-gather.34
  1171.6 87.9 reduce-scatter.19
  1401.5 166.6 reduce-scatter.37
  1570.9 136.2 reduce-scatter.41
  1709.9 135.5 reduce-scatter.43
  1847.7 153.7 reduce-scatter.25
  2003.7 182.8 reduce-scatter.27
  2192.6 206.0 reduce-scatter.21
  2406.1 291.6 reduce-scatter.23
  2700.1 186.2 reduce-scatter.31
  2888.7 184.3 reduce-scatter.29
  3075.4 184.3 reduce-scatter.35
  3261.9 184.3 reduce-scatter.33
  3449.3 32.8 reduce-scatter.39
where the time goes:
time: 3560 us; the launch traced here: 3550 us
  waiting for transfers between devices  1790 us (50%)
  blocking collectives  1110 us (31%)
  matrix products  311 us (9%)
  other arithmetic  162 us (5%)
  local copies, waits for them, and re-layouts  151 us (4%)
    unnamed x1, blocking collectives  951 us
    reduce_scatter x2, waiting for transfers between devices, reduce_grads(): lax.psum_scatter(gradients[2], ('dp', 'fsdp'), scatter_dimension=0, tiled...  372 us
    reduce_scatter x2, waiting for transfers between devices, reduce_grads(): lax.psum_scatter(gradients[3], ('dp', 'fsdp'), scatter_dimension=0, tiled...  370 us
    all_gather x1, waiting for transfers between devices, on_device(): lax.all_gather(text_table.astype(jnp.bfloat16), ('dp', 'fsdp'), axis=0, t...  165 us
    all_gather x1, waiting for transfers between devices, on_device(): code_full = lax.all_gather(code_cols, 'fsdp', axis=0, tiled=True)  145 us
    all_gather x2, waiting for transfers between devices, gather_layer(): lax.all_gather(down_one.astype(jnp.bfloat16), ('dp', 'fsdp'), axis=0, til...  144 us
    all_gather x2, waiting for transfers between devices, gather_layer(): lax.all_gather(up_one.astype(jnp.bfloat16), ('dp', 'fsdp'), axis=0, tiled...  139 us
    reduce_scatter x2, waiting for transfers between devices, reduce_grads(): lax.psum_scatter(gradients[0], ('dp', 'fsdp'), scatter_dimension=1, tiled...  122 us
  transfers between devices with their start and end apart: 26, of which 19 were waited for; matrix products, arithmetic and copies ran while one was open for 38% of the time, Pallas kernels for 0%

commit v1 on v0

v1 whole, which is shorter than its diff:
```python
from functools import partial
import math

import jax
import jax.numpy as jnp
from jax import lax
from jax.experimental import pallas as pl
from jax.experimental.pallas import tpu as pltpu
from jax.sharding import PartitionSpec as P

D = 1024
HEADS = 16
HEAD = 64
VOCAB = 8192
TVOC = 16000
IMG_LEN = 256
TXT_LEN = 128
STEP = 5


SMOOTH = 0.1
BETA_ONE = 0.5
BETA_TWO = 0.5
WEIGHT_DECAY = 0.1
ADAM_EPS = 1e-08
CLIP_NORM = 0.02
MASKED = -1e30
STEP_RATES = (0.02, 0.15, 0.02, 0.01, 0.3, 0.02, 0.03)

BF = jnp.bfloat16
F32 = jnp.float32
AXES = ("dp", "fsdp")
MESH = pl.DeviceIdType.MESH
LAG = 2


def sum_kernel(
    units, Z, p_ref, out_ref, own, from_core, held, from_x, from_y, all_x, all_y, kept, from_line,
    own_sem, core_send, core_recv, one_send, one_recv, two_send, two_recv, line_send, line_recv,
):
    depth = 2 * LAG
    dp, fs = lax.axis_index("dp"), lax.axis_index("fsdp")
    z, core = fs // 2, fs % 2
    x_mate, y_mate = dp + 1 - 2 * (dp % 2), (dp + 2) % 4
    across_dp = (x_mate + 2) % 4
    core_dev, x_dev, y_dev = (dp, fs + 1 - 2 * core), (x_mate, fs), (y_mate, fs)
    up_dev, down_dev = (dp, fs + 2), (dp, fs - 2)
    has_up, has_down = z < Z - 1, z > 0

    barrier = pltpu.get_barrier_semaphore()
    for device in (core_dev, x_dev, y_dev):
        pl.semaphore_signal(barrier, inc=1, device_id=device, device_id_type=MESH)

    @pl.when(has_up)
    def _():
        pl.semaphore_signal(barrier, inc=1, device_id=up_dev, device_id_type=MESH)

    @pl.when(has_down)
    def _():
        pl.semaphore_signal(barrier, inc=1, device_id=down_dev, device_id_type=MESH)

    pl.semaphore_wait(barrier, 3 + has_up.astype(jnp.int32) + has_down.astype(jnp.int32))
    half = Z // 2
    own_slots, held_slots, kept_slots = own.shape[0], held.shape[0], kept.shape[0]

    def add(a, b):
        return (a.astype(F32) + b.astype(F32)).astype(BF)

    def remote(src, dst, send, recv, device):
        return pltpu.make_async_remote_copy(
            src_ref=src, dst_ref=dst, send_sem=send, recv_sem=recv, device_id=device, device_id_type=MESH
        )

    def own_copy(k):
        return pltpu.make_async_copy(
            p_ref.at[k, :, :, core], own.at[k % own_slots], own_sem.at[k % own_slots]
        )

    def core_copy(k):
        s = k % depth
        return remote(
            p_ref.at[k, :, :, 1 - core], from_core.at[s], core_send.at[s], core_recv.at[s], core_dev
        )

    def one_copies(k):
        s, block = k % depth, held.at[k % held_slots, across_dp]
        return (
            remote(block.at[pl.ds(0, half)], from_x.at[s], one_send.at[0, s], one_recv.at[0, s], x_dev),
            remote(block.at[pl.ds(half, Z - half)], from_y.at[s], one_send.at[1, s], one_recv.at[1, s], y_dev),
        )

    def two_copies(k):
        s, h = k % depth, k % held_slots
        return (
            remote(held.at[h, x_mate], all_x.at[s], two_send.at[0, s], two_recv.at[0, s], x_dev),
            remote(held.at[h, y_mate], all_y.at[s], two_send.at[1, s], two_recv.at[1, s], y_dev),
        )

    def up_block(step):
        return jnp.minimum(z + Z - step, Z - 1)

    def down_block(step):
        return jnp.maximum(z - Z + step, 0)

    def up_copy(k, step):
        s = k % depth
        return remote(
            kept.at[k % kept_slots, up_block(step)], from_line.at[0, step - 1, s],
            line_send.at[0, step - 1, s], line_recv.at[0, step - 1, s], up_dev,
        )

    def down_copy(k, step):
        s = k % depth
        return remote(
            kept.at[k % kept_slots, down_block(step)], from_line.at[1, step - 1, s],
            line_send.at[1, step - 1, s], line_recv.at[1, step - 1, s], down_dev,
        )

    def line_start(k, step):
        @pl.when(has_up)
        def _():
            up_copy(k, step).start()

        @pl.when(has_down)
        def _():
            down_copy(k, step).start()

    def line_wait(k, step):
        @pl.when(has_down)
        def _():
            up_copy(k, step).wait_recv()
            down_copy(k, step).wait_send()

        @pl.when(has_up)
        def _():
            down_copy(k, step).wait_recv()
            up_copy(k, step).wait_send()

    def begin(k):
        own_copy(k).start()
        core_copy(k).start()

    def after_core(k):
        own_copy(k).wait()
        core_copy(k).wait()

        def one(block, carry):
            for q in range(Z):
                held[k % held_slots, block, q] = add(
                    own[k % own_slots, block, q], from_core[k % depth, block, q]
                )
            return carry

        lax.fori_loop(0, 4, one, 0)
        for copy in one_copies(k):
            copy.start()

    def after_one(k):
        s, h = k % depth, k % held_slots
        for copy in one_copies(k):
            copy.wait()
        for q in range(half):
            held[h, y_mate, q] = add(held[h, y_mate, q], from_x[s, q])
        for q in range(Z - half):
            held[h, x_mate, half + q] = add(held[h, x_mate, half + q], from_y[s, q])
        for copy in two_copies(k):
            copy.start()

    def after_two(k):
        s, h = k % depth, k % held_slots
        for copy in two_copies(k):
            copy.wait()
        for q in range(Z):
            kept[k % kept_slots, q] = (
                held[h, dp, q].astype(F32) + all_x[s, q].astype(F32) + all_y[s, q].astype(F32)
            ).astype(BF)
        line_start(k, 1)

    def along_line(step):
        def run(k):
            s, h = k % depth, k % kept_slots
            line_wait(k, step - 1)

            @pl.when(has_down & (z + Z - step <= Z - 1))
            def _():
                kept[h, up_block(step)] = add(kept[h, up_block(step)], from_line[0, step - 2, s])

            @pl.when(has_up & (z - Z + step >= 0))
            def _():
                kept[h, down_block(step)] = add(kept[h, down_block(step)], from_line[1, step - 2, s])

            line_start(k, step)

        return run

    def finish(k):
        s = k % depth
        line_wait(k, Z - 1)
        out_ref[k] = kept[k % kept_slots, z].astype(F32)

        @pl.when(has_down)
        def _():
            out_ref[k] = out_ref[k] + from_line[0, Z - 2, s].astype(F32)

        @pl.when(has_up)
        def _():
            out_ref[k] = out_ref[k] + from_line[1, Z - 2, s].astype(F32)

    stages = [begin, after_core, after_one, after_two]
    stages += [along_line(step) for step in range(2, Z)] + [finish]

    def loop_step(j, carry):
        for place in reversed(range(len(stages))):
            k = j - place * LAG

            @pl.when((k >= 0) & (k < units))
            def _(k=k, run=stages[place]):
                run(k)

        return carry

    lax.fori_loop(0, units + (len(stages) - 1) * LAG, loop_step, 0)


def sum_units(partial_sums, call_id):
    units, devices, m, n = partial_sums.shape
    Z = lax.axis_size("fsdp") // 2
    if lax.axis_size("dp") != 4 or Z != 4 or m % 16:
        return lax.psum_scatter(
            partial_sums, AXES, scatter_dimension=1, tiled=True
        ).reshape(units, m, n).astype(F32)
    depth, half = 2 * LAG, Z // 2
    own_slots, held_slots, kept_slots = LAG + 1, 2 * LAG + 1, Z * LAG + 1
    dma = pltpu.SemaphoreType.DMA
    return pl.pallas_call(
        partial(sum_kernel, units, Z),
        out_shape=jax.ShapeDtypeStruct((units, m, n), F32),
        in_specs=[pl.BlockSpec(memory_space=pl.ANY)],
        out_specs=pl.BlockSpec(memory_space=pltpu.VMEM),
        scratch_shapes=[
            pltpu.VMEM((own_slots, 4, Z, m, n), BF),
            pltpu.VMEM((depth, 4, Z, m, n), BF),
            pltpu.VMEM((held_slots, 4, Z, m, n), BF),
            pltpu.VMEM((depth, half, m, n), BF),
            pltpu.VMEM((depth, Z - half, m, n), BF),
            pltpu.VMEM((depth, Z, m, n), BF),
            pltpu.VMEM((depth, Z, m, n), BF),
            pltpu.VMEM((kept_slots, Z, m, n), BF),
            pltpu.VMEM((2, Z - 1, depth, m, n), BF),
            dma((own_slots,)),
            dma((depth,)),
            dma((depth,)),
            dma((2, depth)),
            dma((2, depth)),
            dma((2, depth)),
            dma((2, depth)),
            dma((2, Z - 1, depth)),
            dma((2, Z - 1, depth)),
        ],
        compiler_params=pltpu.CompilerParams(
            collective_id=call_id, has_side_effects=True, vmem_limit_bytes=48 << 20
        ),
    )(partial_sums.reshape(units, 4, Z, 2, m, n))


def layer_norm(stream, gain):
    centred = stream - jnp.mean(stream, axis=-1, keepdims=True)
    return centred * lax.rsqrt(jnp.mean(centred * centred, axis=-1, keepdims=True) + 1e-05) * gain


def norm_back(stream, gain, grad_out):
    _, pullback = jax.vjp(layer_norm, stream, gain)
    return pullback(grad_out)


def positions(length, width):
    position = jnp.arange(length, dtype=jnp.float32)[:, None]
    speeds = jnp.exp(
        -math.log(10000.0) * 2.0 * jnp.arange(width // 2, dtype=jnp.float32)[None, :] / width
    )
    return jnp.concatenate([jnp.sin(position * speeds), jnp.cos(position * speeds)], axis=1)


def matmul(first_op, second_op):
    return jnp.dot(first_op, second_op, preferred_element_type=jnp.float32)


def across(first_op, second_op):
    return lax.dot_general(
        first_op, second_op, (((0,), (0,)), ((), ())), preferred_element_type=jnp.float32
    )


def against(first_op, second_op):
    return lax.dot_general(
        first_op, second_op, (((1,), (1,)), ((), ())), preferred_element_type=jnp.float32
    )


def heads_first(matrix, blocks):
    return matrix.reshape(blocks, -1, HEADS, HEAD).transpose(0, 2, 1, 3)


def heads_last(array):
    return array.transpose(0, 2, 1, 3).reshape(-1, HEADS * HEAD)


def attention(queries, keys_in, values, visible):
    scores = jnp.einsum(
        "bhqd,bhkd->bhqk", queries, keys_in, preferred_element_type=F32
    ) * HEAD ** (-0.5)
    scores = jnp.where(visible[:, None], scores, MASKED)
    weights = jnp.exp(scores - jnp.max(scores, axis=-1, keepdims=True))
    shares = weights / jnp.sum(weights, axis=-1, keepdims=True)
    low = shares.astype(BF)
    attended = jnp.einsum("bhqk,bhkd->bhqd", low, values, preferred_element_type=F32)
    return heads_last(attended.astype(BF)), low


def attention_back(queries, keys_in, values, shares, grad_mixed):
    grad_heads = heads_first(grad_mixed, queries.shape[0])
    grad_shares = jnp.einsum(
        "bhqd,bhkd->bhqk", grad_heads, values, preferred_element_type=F32
    )
    wide = shares.astype(F32)
    grad_scores = (
        wide * (grad_shares - jnp.sum(wide * grad_shares, axis=-1, keepdims=True))
    ).astype(BF)
    grad_query = jnp.einsum(
        "bhqk,bhkd->bhqd", grad_scores, keys_in, preferred_element_type=F32
    ) * HEAD ** (-0.5)
    grad_keys = jnp.einsum(
        "bhqk,bhqd->bhkd", grad_scores, queries, preferred_element_type=F32
    ) * HEAD ** (-0.5)
    grad_values = jnp.einsum(
        "bhqk,bhqd->bhkd", shares, grad_heads, preferred_element_type=F32
    )
    return grad_query, grad_keys, grad_values


def layer_forward(stream, weights, gains, self_visible, memory, cross_visible):
    project, mix_out, cross, cross_out, ffn_up, ffn_down = weights
    blocks = self_visible.shape[0]
    stored = {"stream": stream}
    normed = layer_norm(stream, gains[0]).astype(BF)
    queries, keys_in, values = [
        heads_first(matmul(normed, project[i]).astype(BF), blocks) for i in range(3)
    ]
    attended, shares = attention(queries, keys_in, values, self_visible)
    stream = stream + matmul(attended, mix_out)
    stored.update(
        normed=normed, self_attention=(queries, keys_in, values, shares), attended=attended, after_self=stream
    )
    if memory is not None:
        cross_in = layer_norm(stream, gains[1]).astype(BF)
        cross_query = heads_first(matmul(cross_in, cross[0]).astype(BF), 1)
        memory_keys = heads_first(matmul(memory, cross[1]).astype(BF), 1)
        memory_values = heads_first(matmul(memory, cross[2]).astype(BF), 1)
        cross_mixed, cross_shares = attention(cross_query, memory_keys, memory_values, cross_visible)
        stream = stream + matmul(cross_mixed, cross_out)
        stored.update(
            cross_in=cross_in,
            cross_attention=(cross_query, memory_keys, memory_values, cross_shares),
            cross_mixed=cross_mixed,
        )
    stored["before_ffn"] = stream
    ffn_in = layer_norm(stream, gains[-2]).astype(BF)
    hidden_pre = [matmul(ffn_in, up) for up in ffn_up]
    hidden = [jax.nn.gelu(pre, approximate=True).astype(BF) for pre in hidden_pre]
    for low, down in zip(hidden, ffn_down):
        stream = stream + matmul(low, down)
    stored.update(ffn_in=ffn_in, hidden_pre=hidden_pre, hidden=hidden, before_final=stream)
    return layer_norm(stream, gains[-1]).astype(BF), stored


def layer_backward(grad_final, weights, gains, stored, memory):
    project, mix_out, cross, cross_out, ffn_up, ffn_down = weights
    gain_grads = [None] * len(gains)
    grad_stream, gain_grads[-1] = norm_back(stored["before_final"], gains[-1], grad_final)
    grad_low = grad_stream.astype(BF)
    up_pairs, down_pairs = [], []
    grad_ffn = 0.0
    for pre, low, up, down in zip(stored["hidden_pre"], stored["hidden"], ffn_up, ffn_down):
        down_pairs.append((low, grad_low))
        _, gelu_pull = jax.vjp(partial(jax.nn.gelu, approximate=True), pre)
        grad_pre = gelu_pull(against(grad_low, down))[0].astype(BF)
        up_pairs.append((stored["ffn_in"], grad_pre))
        grad_ffn = grad_ffn + against(grad_pre, up)
    grad_normed, gain_grads[-2] = norm_back(stored["before_ffn"], gains[-2], grad_ffn)
    grad_stream = grad_stream + grad_normed
    cross_pairs, cross_out_pairs = [], []
    grad_memory = None
    if memory is not None:
        grad_low = grad_stream.astype(BF)
        cross_out_pairs.append((stored["cross_mixed"], grad_low))
        grad_mixed = against(grad_low, cross_out).astype(BF)
        grads = [
            heads_last(grad.astype(BF)) for grad in attention_back(*stored["cross_attention"], grad_mixed)
        ]
        cross_pairs = [(stored["cross_in"], grads[0]), (memory, grads[1]), (memory, grads[2])]
        grad_memory = against(grads[1], cross[1]) + against(grads[2], cross[2])
        grad_normed, gain_grads[1] = norm_back(
            stored["after_self"], gains[1], against(grads[0], cross[0])
        )
        grad_stream = grad_stream + grad_normed
    grad_low = grad_stream.astype(BF)
    out_pairs = [(stored["attended"], grad_low)]
    grad_mixed = against(grad_low, mix_out).astype(BF)
    grads = [
        heads_last(grad.astype(BF)) for grad in attention_back(*stored["self_attention"], grad_mixed)
    ]
    project_pairs = [(stored["normed"], grad) for grad in grads]
    grad_normed, gain_grads[0] = norm_back(
        stored["stream"],
        gains[0],
        sum(against(grads[i], project[i]) for i in range(3)),
    )
    grad_stream = grad_stream + grad_normed
    pairs = (project_pairs, out_pairs, cross_pairs, cross_out_pairs, up_pairs, down_pairs)
    return grad_stream, grad_memory, gain_grads, pairs


def adam_step(weight, moment_one, second, gradient, rate):
    moment_one = BETA_ONE * moment_one + (1.0 - BETA_ONE) * gradient
    second = BETA_TWO * second + (1.0 - BETA_TWO) * gradient * gradient
    first_hat = moment_one / (1.0 - BETA_ONE**STEP)
    second_hat = second / (1.0 - BETA_TWO**STEP)
    weight = weight - rate * (first_hat / (jnp.sqrt(second_hat) + ADAM_EPS) + WEIGHT_DECAY * weight)
    return (weight, moment_one, second)


def column_units(matrix):
    return matrix.reshape(matrix.shape[0], -1, D).transpose(1, 0, 2)


def from_column_units(units):
    return units.transpose(1, 0, 2).reshape(units.shape[1], -1)


def hidden_units(matrix, devices):
    rows, width = matrix.shape
    return (
        matrix.reshape(rows, devices, 4, width // devices // 4)
        .transpose(2, 0, 1, 3)
        .reshape(4, rows, width // 4)
    )


def from_hidden_units(units, devices):
    quarters, rows, width = units.shape
    return (
        units.reshape(quarters, rows, devices, width // devices)
        .transpose(1, 2, 0, 3)
        .reshape(rows, quarters * width)
    )


def on_device(
    text_ids,
    text_segments,
    codes,
    caption_of,
    mix_in,
    mix_out,
    ffn_up,
    ffn_down,
    norm_gains,
    text_table,
    code_table,
    mix_in_first,
    mix_out_first,
    ffn_up_first,
    ffn_down_first,
    gains_first,
    text_first,
    code_first,
    mix_in_second,
    mix_out_second,
    ffn_up_second,
    ffn_down_second,
    gains_second,
    text_second,
    code_second,
):
    image_count = codes.shape[0]
    dp_size, fsdp_size = lax.axis_size("dp"), lax.axis_size("fsdp")
    devices = dp_size * fsdp_size
    me = lax.axis_index("dp") * fsdp_size + lax.axis_index("fsdp")
    token_total = image_count * IMG_LEN * devices
    inverse = 1.0 / token_total
    scale_in = math.sqrt(D)
    rows = mix_in.shape[1]
    segments = text_segments[0]
    text_visible = (segments[:, None] == segments[None, :])[None]
    place = jnp.arange(IMG_LEN)
    self_visible = jnp.broadcast_to(
        place[None, :] <= place[:, None], (image_count, IMG_LEN, IMG_LEN)
    )
    wanted = jnp.repeat(caption_of, IMG_LEN)
    cross_visible = (segments[None, :] == wanted[:, None])[None]

    small = jnp.concatenate([text_ids[0].astype(F32), norm_gains.reshape(-1)])
    small = lax.all_gather(small, AXES)
    all_ids = small[:, :TXT_LEN].astype(jnp.int32).reshape(-1)
    gains = small[:, TXT_LEN:].reshape(devices, 7, -1).transpose(1, 0, 2).reshape(7, D)
    gains = gains.astype(BF).astype(F32)

    def gather(units):
        return lax.all_gather(units.astype(BF), AXES, axis=1, tiled=True)

    code_cols = lax.all_gather(code_table.astype(BF), "dp", axis=1, tiled=True)
    code_full = lax.all_gather(code_cols, "fsdp", axis=0, tiled=True)

    def layer_units(which):
        return [
            column_units(mix_in[which]),
            mix_out[which][None],
            hidden_units(ffn_up[min(which, 1)], devices),
            ffn_down[min(which, 1)].reshape(4, rows, D),
        ]

    enc_units = gather(jnp.concatenate(layer_units(0)))
    self_units = gather(jnp.concatenate(layer_units(1)[:2]))
    late_units = gather(jnp.concatenate(layer_units(2)))
    enc_weights = (enc_units[:3], enc_units[3], None, None, enc_units[4:8], enc_units[8:])
    dec_weights = (
        self_units[:3], self_units[3], late_units[:3], late_units[3], late_units[4:8], late_units[8:]
    )

    base = me * text_table.shape[0]
    owned = (all_ids[:, None] - base == jnp.arange(text_table.shape[0])[None, :]).astype(BF)
    looked = matmul(owned, text_table.astype(BF)).astype(BF)
    looked = looked.reshape(devices, TXT_LEN // rows, rows, D).transpose(1, 0, 2, 3)
    text_in = sum_units(looked, 0).reshape(TXT_LEN, D) * scale_in + positions(TXT_LEN, D)
    enc_gains = [gains[i] for i in range(3)]
    dec_gains = [gains[i] for i in range(3, 7)]
    memory, enc_stored = layer_forward(text_in, enc_weights, enc_gains, text_visible, None, None)

    image_rows = code_full[codes].astype(F32) * scale_in
    shifted = jnp.concatenate([jnp.zeros_like(image_rows[:, :1]), image_rows[:, :-1]], axis=1)
    image_in = (shifted + positions(IMG_LEN, D)[None]).reshape(-1, D)
    final_out, dec_stored = layer_forward(
        image_in, dec_weights, dec_gains, self_visible, memory, cross_visible
    )

    targets = codes.reshape(-1)
    logits = against(final_out, code_full)
    hit = targets[:, None] == jnp.arange(VOCAB)[None, :]
    top = jnp.max(logits, axis=1, keepdims=True)
    log_total = top + jnp.log(jnp.sum(jnp.exp(logits - top), axis=1, keepdims=True))
    weighted = jnp.sum(
        logits * jnp.where(hit, 1.0 - SMOOTH + SMOOTH / VOCAB, SMOOTH / VOCAB), axis=1, keepdims=True
    )
    loss_part = jnp.sum(log_total - weighted)
    grad_logits = (
        (jnp.exp(logits - log_total) - jnp.where(hit, 1.0 - SMOOTH, 0.0) - SMOOTH / VOCAB) * inverse
    ).astype(BF)
    grad_final = matmul(grad_logits, code_full)

    grad_image, grad_memory, dec_gain_grads, dec_pairs = layer_backward(
        grad_final, dec_weights, dec_gains, dec_stored, memory
    )
    grad_text, _, enc_gain_grads, enc_pairs = layer_backward(
        grad_memory, enc_weights, enc_gains, enc_stored, None
    )
    gain_part = jnp.stack(enc_gain_grads + dec_gain_grads)

    grad_rows = lax.all_gather((grad_text * scale_in).astype(BF), AXES, axis=0, tiled=True)
    text_grad = across(owned, grad_rows)

    grad_looked = grad_image.reshape(image_count, IMG_LEN, D)[:, 1:] * scale_in
    grad_looked = jnp.pad(grad_looked, ((0, 0), (0, 1), (0, 0))).reshape(-1, D).astype(BF)
    code_part = across(
        jnp.concatenate([grad_logits, hit.astype(BF)]), jnp.concatenate([final_out, grad_looked])
    ).astype(BF)
    code_parts = 8
    code_part = (
        code_part.reshape(fsdp_size, code_parts, -1, dp_size, D // dp_size)
        .transpose(1, 3, 0, 2, 4)
        .reshape(code_parts, devices, -1, D // dp_size)
    )
    pairs = [pair for group in (*enc_pairs, *dec_pairs) for pair in group]
    weight_part = jnp.stack([across(*pair).astype(BF) for pair in pairs])
    weight_sum = sum_units(weight_part.reshape(len(pairs), devices, rows, D), 1)
    code_grad = sum_units(code_part, 2).reshape(code_table.shape)

    enc_sum, dec_sum = weight_sum[:12], weight_sum[12:]
    small_sum = lax.psum(jnp.concatenate([gain_part.reshape(-1), loss_part[None]]), AXES)
    loss_sum = small_sum[-1]
    gains_grad = lax.dynamic_slice_in_dim(small_sum[:-1].reshape(7, D), me * rows, rows, 1)
    gradients = (
        jnp.stack(
            [from_column_units(part) for part in (enc_sum[:3], dec_sum[:3], dec_sum[4:7])]
        ),
        jnp.stack([enc_sum[3], dec_sum[3], dec_sum[7]]),
        jnp.stack(
            [from_hidden_units(part, devices) for part in (enc_sum[4:8], dec_sum[8:12])]
        ),
        jnp.stack([part.reshape(-1, D) for part in (enc_sum[8:], dec_sum[12:])]),
        gains_grad,
        text_grad,
        code_grad,
    )
    square_part = sum((jnp.sum(gradient * gradient) for gradient in gradients))
    grad_norm = jnp.sqrt(lax.psum(square_part, AXES))
    factor = CLIP_NORM / jnp.maximum(grad_norm, CLIP_NORM)
    params = (mix_in, mix_out, ffn_up, ffn_down, norm_gains, text_table, code_table)
    firsts = (
        mix_in_first,
        mix_out_first,
        ffn_up_first,
        ffn_down_first,
        gains_first,
        text_first,
        code_first,
    )
    seconds = (
        mix_in_second,
        mix_out_second,
        ffn_up_second,
        ffn_down_second,
        gains_second,
        text_second,
        code_second,
    )
    updated = [
        adam_step(
            params[index],
            firsts[index],
            seconds[index],
            gradients[index] * factor,
            STEP_RATES[index],
        )
        for index in range(7)
    ]
    return (
        loss_sum,
        grad_norm,
        updated[0][0],
        updated[1][0],
        updated[2][0],
        updated[3][0],
        updated[4][0],
        updated[5][0],
        updated[6][0],
        updated[0][1],
        updated[1][1],
        updated[2][1],
        updated[3][1],
        updated[4][1],
        updated[5][1],
        updated[6][1],
        updated[0][2],
        updated[1][2],
        updated[2][2],
        updated[3][2],
        updated[4][2],
        updated[5][2],
        updated[6][2],
    )


def solution(mesh):
    return jax.shard_map(
        on_device,
        mesh=mesh,
        in_specs=(
            P(("dp", "fsdp"), None),
            P(("dp", "fsdp"), None),
            P(("dp", "fsdp"), None),
            P(("dp", "fsdp")),
            P(None, ("dp", "fsdp"), None),
            P(None, ("dp", "fsdp"), None),
            P(None, ("dp", "fsdp"), None),
            P(None, ("dp", "fsdp"), None),
            P(None, ("dp", "fsdp")),
            P(("dp", "fsdp"), None),
            P("fsdp", "dp"),
            P(None, ("dp", "fsdp"), None),
            P(None, ("dp", "fsdp"), None),
            P(None, ("dp", "fsdp"), None),
            P(None, ("dp", "fsdp"), None),
            P(None, ("dp", "fsdp")),
            P(("dp", "fsdp"), None),
            P("fsdp", "dp"),
            P(None, ("dp", "fsdp"), None),
            P(None, ("dp", "fsdp"), None),
            P(None, ("dp", "fsdp"), None),
            P(None, ("dp", "fsdp"), None),
            P(None, ("dp", "fsdp")),
            P(("dp", "fsdp"), None),
            P("fsdp", "dp"),
        ),
        out_specs=(
            P(),
            P(),
            P(None, ("dp", "fsdp"), None),
            P(None, ("dp", "fsdp"), None),
            P(None, ("dp", "fsdp"), None),
            P(None, ("dp", "fsdp"), None),
            P(None, ("dp", "fsdp")),
            P(("dp", "fsdp"), None),
            P("fsdp", "dp"),
            P(None, ("dp", "fsdp"), None),
            P(None, ("dp", "fsdp"), None),
            P(None, ("dp", "fsdp"), None),
            P(None, ("dp", "fsdp"), None),
            P(None, ("dp", "fsdp")),
            P(("dp", "fsdp"), None),
            P("fsdp", "dp"),
            P(None, ("dp", "fsdp"), None),
            P(None, ("dp", "fsdp"), None),
            P(None, ("dp", "fsdp"), None),
            P(None, ("dp", "fsdp"), None),
            P(None, ("dp", "fsdp")),
            P(("dp", "fsdp"), None),
            P("fsdp", "dp"),
        ),
        check_vma=False,
    )
```

time: 3560 us -> 1540 us (0.43)
  waiting for transfers between devices: 1790 us -> 316 us
  blocking collectives: 1110 us -> 119 us
  Pallas kernels: 0 us -> 425 us
  local copies, waits for them, and re-layouts: 151 us -> 246 us
  other arithmetic: 162 us -> 90.2 us
    reduce_scatter x11 -> x0, waiting for transfers between devices: 982 us -> none  [the longest x2 372 us: reduce_grads(): lax.psum_scatter(gradients[2], ('dp', 'fsdp'), scatter_dimension=0, tiled...]
    unnamed x1, blocking collectives: 951 us -> 40.5 us
    pallas_call x0 -> x3, Pallas kernels: none -> 425 us  [sum_units(): pl.pallas_call(partial(sum_kernel, units, Z), out_shape=jax.ShapeDtypeStr...]
    all_gather x11 -> x5, waiting for transfers between devices: 664 us -> 256 us  [the longest x3 220 us: gather(): return lax.all_gather(units.astype(BF), AXES, axis=1, tiled=True)]
    all_gather x5 -> x0, blocking collectives: 119 us -> none  [the longest x2 78.1 us: gather_layer(): lax.all_gather(gains_part.astype(jnp.bfloat16), ('dp', 'fsdp'), axis=1, t...]
    all_gather x1, waiting for transfers between devices: 145 us -> 60.3 us  [on_device(): code_full = lax.all_gather(code_cols, 'fsdp', axis=0, tiled=True)]
    reshape x0 -> x14, local copies, waits for them, and re-layouts: none -> 64.1 us  [the longest x2 43.2 us: on_device(): code_part.reshape(fsdp_size, code_parts, -1, dp_size, D // dp_size)]
    psum x1 -> x2, blocking collectives: 39.8 us -> 78.3 us  [the longest x1 39.4 us: on_device(): lax.psum(jnp.concatenate([gain_part.reshape(-1), loss_part[None]]), AXES)]
  transfers between devices with their start and end apart: 26 -> 6, of which waited for: 19 -> 4; matrix products, arithmetic and copies ran while one was open for 38% -> 22% of each run, Pallas kernels for 0% -> 28%
where the time goes in v1:
time: 1540 us; the launch traced here: 1530 us
  Pallas kernels  425 us (28%)
  waiting for transfers between devices  316 us (21%)
  matrix products  307 us (20%)
  local copies, waits for them, and re-layouts  246 us (16%)
  blocking collectives  119 us (8%)
  other arithmetic  90.2 us (6%)
  between operations  24.1 us (2%)
    pallas_call x3, Pallas kernels, sum_units(): pl.pallas_call(partial(sum_kernel, units, Z), out_shape=jax.ShapeDtypeStr...  425 us
    all_gather x3, waiting for transfers between devices, gather(): return lax.all_gather(units.astype(BF), AXES, axis=1, tiled=True)  220 us
    dot_general x30, matrix products, matmul(): return jnp.dot(first_op, second_op, preferred_element_type=jnp.float32)  101 us
    dot_general x29, matrix products, against(): lax.dot_general(first_op, second_op, (((1,), (1,)), ((), ())), preferred_...  101 us
    unnamed x458, local copies, waits for them, and re-layouts  89.2 us
    dot_general x30, matrix products, across(): lax.dot_general(first_op, second_op, (((0,), (0,)), ((), ())), preferred_...  76.8 us
    all_gather x1, waiting for transfers between devices, on_device(): code_full = lax.all_gather(code_cols, 'fsdp', axis=0, tiled=True)  60.3 us
    reshape x2, local copies, waits for them, and re-layouts, on_device(): code_part.reshape(fsdp_size, code_parts, -1, dp_size, D // dp_size)  43.2 us
  transfers between devices with their start and end apart: 6, of which 4 were waited for; matrix products, arithmetic and copies ran while one was open for 22% of the time, Pallas kernels for 28%

profile of v1, /device:TPU:0, one launch (start us, length us, event | category | flops | bytes accessed | tf_op | source)
XLA Modules:
  0.0 1528.1 jit_solution(10571203799927798460)
XLA Ops:
  12.2 36.1 %all-gather.10.cloned.1.call-done = bf16[1024,1024]{1,0:T(8,128)(2,1)} async-done(((bf16[1024,256]{1,0:T(8,128)(2,1)}), bf16[1024,1024]{1,0:T(8,128)(2,1)}) %all-gather.10.cloned.1.call-update) | async-done | bytes 2097168 | tf_op jit(solution)/shard_map/all_gather | solution.py:511
  57.1 40.5 %all-reduce.2 = f32[11264]{0:T(1024)S(1)} all-reduce(f32[11264]{0:T(1024)S(1)} %maximum_dynamic-update-slice_fusion), channel_id=2, replica_groups=mesh['dp'=4,'fsdp'=8] {'dp','fsdp'}, use_global_device_ids=true, to_apply=%add.2 | all-reduce | flops 11264 | bytes 90112
  98.3 6.8 fusion.15
  105.2 8.7 copy.131
  113.9 80.6 %shard_map.416 = f32[4,32,1024]{2,1,0:T(8,128)S(1)} custom-call(bf16[4,4,4,2,32,1024]{5,4,3,2,1,0:T(8,128)(2,1)} %bitcast.548), custom_call_target="tpu_custom_call" | custom-call | tf_op jit(solution)/shard_map/pallas_call | solution.py:235
  202.3 6.6 fusion.7
  209.0 27.0 %fusion.237 = (bf16[1,1024,1024]{2,0,1:T(2,128)(2,1)}, bf16[1,1024,1024]{2,0,1:T(2,128)(2,1)}, bf16[1,1024,1024]{2,0,1:T(2,128)(2,1)}, bf16[1,1024,1024]{2,0,1:T(2,128)(2,1)}) fusion(bf16[4,1024,1024]{2,0,1:T(4,128)(2,1)} %all-gather.14.cloned.1.call-done), kind=kLoop, calls=%fused_computation.522 | loop fusion | bytes 16777216 | tf_op jit(solution)/shard_map/slice | solution.py:527
  236.0 60.3 %all-gather.12.cloned.1.call-done = bf16[8192,1024]{1,0:T(8,128)(2,1)} async-done(((bf16[1024,1024]{1,0:T(8,128)(2,1)}), bf16[8192,1024]{1,0:T(8,128)(2,1)}) %all-gather.12.cloned.1.call-update) | async-done | bytes 16777232 | tf_op jit(solution)/shard_map/all_gather | solution.py:512
  296.3 10.7 gather_fusion
  315.9 4.8 convolution_convert_fusion.34
  323.3 3.8 convolution_convert_fusion.32
  330.1 6.6 fusion.152
  336.6 9.2 fusion.244
  357.0 95.0 %all-gather.8.cloned.1.call-done = bf16[12,1024,1024]{2,1,0:T(8,128)(2,1)} async-done(((bf16[12,32,1024]{2,1,0:T(8,128)(2,1)}), bf16[12,1024,1024]{2,1,0:T(8,128)(2,1)}) %all-gather.8.cloned.1.call-update) | async-done | bytes 25165840 | tf_op jit(solution)/shard_map/all_gather | solution.py:509
  483.0 125.0 %all-gather.16.cloned.1.call-done = bf16[12,1024,1024]{2,1,0:T(8,128)(2,1)} async-done(((bf16[12,32,1024]{2,1,0:T(8,128)(2,1)}), bf16[12,1024,1024]{2,1,0:T(8,128)(2,1)}) %all-gather.16.cloned.1.call-update) | async-done | bytes 25165840 | tf_op jit(solution)/shard_map/all_gather | solution.py:509
  610.4 3.9 fusion.111
  618.8 4.9 fusion.249
  623.7 2.8 divide_convert_fusion.1
  626.9 3.6 fusion.250
  631.3 3.2 fusion.106
  634.6 3.6 fusion.102
  638.2 3.6 fusion.98
  641.8 3.6 fusion.94
  645.5 3.8 fusion.104
  649.3 3.0 fusion.100
  652.3 3.0 fusion.96
  655.3 3.7 fusion.251
  660.7 16.0 %fusion.252 = (f32[512]{0:T(512)S(1)}, f32[512,8192]{1,0:T(8,128)}) fusion(bf16[512,1024]{1,0:T(8,128)(2,1)} %multiply_convert_fusion.4, bf16[8192,1024]{1,0:T(8,128)(2,1)} %all-gather.12.cloned.1.call-done), kind=kOutput, calls=%fused_computation.537 | convolution fusion | flops 8594128896 | bytes 34605056 | tf_op jit(solution)/shard_map/dot_general | solution.py:295
  676.7 10.3 multiply_reduce_fusion
  687.6 5.2 multiply_convert_fusion
  692.8 16.1 %multiply_reduce_fusion.2 = (f32[1024]{0:T(1024)S(1)}, f32[512]{0:T(512)S(1)}, f32[512,1024]{1,0:T(8,128)S(1)}) fusion(f32[512,1024]{1,0:T(8,128)S(1)} %get-tuple-element.138, f32[512]{0:T(512)S(1)} %fusion.206, f32[512]{0:T(512)S(1)} %broadcast_multiply_fusion.2, f32[1024]{0:T(1024)S(1)} %mul.1345, bf16[512,8192]{1,0:T(8,128)(2,1)S(1)} %multiply_convert_fusion, ...), kind=kOutput, calls=%fused_computation.119 | convolution fusion | flops 8593602560 | bytes 29374464 | tf_op jit(solution)/shard_map/dot_general | solution.py:285
  711.3 4.4 fusion.52
  715.7 4.4 fusion.45
  720.2 4.4 fusion.31
  724.6 4.4 fusion.38
  729.0 3.3 fusion.101
  732.3 2.9 fusion.93
  735.3 3.1 fusion.97
  738.4 3.6 multiply_reduce_fusion.3
  744.5 3.9 fusion.110
  763.4 2.7 fusion.171
  766.2 2.7 fusion.178
  782.1 3.2 fusion.135
  793.1 3.8 multiply_reduce_fusion.4
  805.5 3.7 fusion.113
  838.1 2.7 fusion.156
  843.0 2.7 fusion.157
  860.7 3.4 constant_dynamic-update-slice_fusion.26
  882.8 3.4 multiply_reduce_fusion.1
  887.9 3.4 constant_dynamic-update-slice_fusion.16
  945.1 256.3 %shard_map.417 = f32[28,32,1024]{2,1,0:T(8,128)S(1)} custom-call(bf16[28,4,4,2,32,1024]{5,4,3,2,1,0:T(8,128)(2,1)} %constant_dynamic-update-slice_fusion.p_ref), custom_call_target="tpu_custom_call" | custom-call | tf_op jit(solution)/shard_map/pallas_call | solution.py:235
  1212.0 4.7 copy.182
  1216.8 4.4 stack_reshape.24
  1223.2 4.7 copy.183
  1227.9 4.4 stack_reshape.25
  1233.0 39.4 %psum.14 = f32[7169]{0:T(1024)S(1)} all-reduce(f32[7169]{0:T(1024)S(1)} %pad_maximum_fusion.6), channel_id=1, replica_groups=mesh['dp'=4,'fsdp'=8] {'dp','fsdp'}, use_global_device_ids=true, to_apply=%region_44.45 | all-reduce | flops 7169 | bytes 57352 | tf_op jit(solution)/shard_map/psum | solution.py:588
  1277.2 23.7 %fusion.8 = bf16[8192,1024]{1,0:T(8,128)(2,1)} fusion(bf16[512,8192]{1,0:T(8,128)(2,1)} %fusion.7, bf16[512,8192]{1,0:T(8,128)(2,1)} %copy-done.20, bf16[512,1024]{1,0:T(8,128)(2,1)S(1)} %bitcast.628, bf16[512,1024]{1,0:T(8,128)(2,1)S(1)} %copy-done.92), kind=kOutput, calls=%fused_computation.13 | convolution fusion | flops 17226006528 | bytes 35651584 | tf_op jit(solution)/shard_map/dot_general | solution.py:289
  1300.9 27.9 %reshape.985 = bf16[8,8,128,4,256]{4,3,2,1,0:T(4,128)(2,1)} reshape(bf16[8192,1024]{1,0:T(8,128)(2,1)} %fusion.8) | data formatting | bytes 33554432 | tf_op jit(solution)/shard_map/reshape | solution.py:578
  1328.8 15.3 %copy.184 = bf16[8,8,128,4,256]{4,2,0,3,1:T(8,128)(2,1)} copy(bf16[8,8,128,4,256]{4,3,2,1,0:T(4,128)(2,1)} %reshape.985) | data formatting | bytes 33554432 | tf_op jit(solution)/shard_map/reshape | solution.py:578
  1344.1 88.5 %shard_map.418 = f32[8,128,256]{2,1,0:T(8,128)S(1)} custom-call(bf16[8,4,4,2,128,256]{5,4,3,2,1,0:T(8,128)(2,1)} %bitcast.545), custom_call_target="tpu_custom_call" | custom-call | tf_op jit(solution)/shard_map/pallas_call | solution.py:235
  1446.1 9.8 multiply_reduce_fusion.13
  1458.5 39.0 %psum.15 = f32[]{:T(128)} all-reduce(f32[]{:T(128)S(6)} %add.484), channel_id=1, replica_groups=mesh['dp'=4,'fsdp'=8] {'dp','fsdp'}, use_global_device_ids=true, to_apply=%region_56.57 | all-reduce | flops 1 | bytes 8 | tf_op jit(solution)/shard_map/psum | solution.py:605
  1499.5 4.4 multiply_subtract_fusion.1
  1513.6 4.1 multiply_subtract_fusion
  (715 shorter events, 299.1 us)
Async XLA Ops:
  7.2 187.5 %copy-start = (s32[2]{0:T(128)S(1)}, s32[2]{0:T(128)}, u32[]{:S(2)}) copy-start(s32[2]{0:T(128)} %param.28) | copy-start | bytes 28
  7.2 41.1 %all-gather.10.cloned.1.call-start = ((), (), s32[]{:S(2)}) async-start(), calls=%async_computation.1 | async-start | bytes 2621440 | tf_op jit(solution)/shard_map/all_gather | solution.py:511
  9.5 199.5 %all-gather.14.cloned.1.call-start = ((), (), s32[]{:S(2)}) async-start(), calls=%async_computation.3 | async-start | bytes 8650752 | tf_op jit(solution)/shard_map/all_gather | solution.py:509
  9.9 38.5 %copy-start.59 = (f32[2,128,1024]{2,1,0:T(8,128)S(1)}, f32[2,128,1024]{2,1,0:T(8,128)}, u32[]{:S(2)}) copy-start(f32[2,128,1024]{2,1,0:T(8,128)} %param.32) | copy-start | bytes 3145732
  12.2 36.4 %copy-start.57 = (f32[2,32,4096]{2,1,0:T(8,128)S(1)}, f32[2,32,4096]{2,1,0:T(8,128)}, u32[]{:S(2)}) copy-start(f32[2,32,4096]{2,1,0:T(8,128)} %param.31) | copy-start | bytes 3145732
  12.2 284.1 %all-gather.12.cloned.1.call-start = ((), (), s32[]{:S(2)}) async-start(), calls=%async_computation.2 | async-start | bytes 18874368 | tf_op jit(solution)/shard_map/all_gather | solution.py:512
  48.4 403.6 %all-gather.8.cloned.1.call-start = ((), (), s32[]{:S(2)}) async-start(), calls=%async_computation | async-start | bytes 25952256 | tf_op jit(solution)/shard_map/all_gather | solution.py:509
  53.1 554.9 %all-gather.16.cloned.1.call-start = ((), (), s32[]{:S(2)}) async-start(), calls=%async_computation.4 | async-start | bytes 25952256 | tf_op jit(solution)/shard_map/all_gather | solution.py:509
  55.4 42.9 %copy-start.78 = (f32[500,1024]{1,0:T(8,128)S(1)}, f32[500,1024]{1,0:T(8,128)}, u32[]{:S(2)}) copy-start(f32[500,1024]{1,0:T(8,128)} %param.34) | copy-start | bytes 6144004
  56.8 1389.3 %all-gather.18.cloned.1.call-start = ((), (), s32[]{:S(2)}) async-start(), calls=%async_computation.5 | async-start | bytes 8650752 | tf_op jit(solution)/shard_map/all_gather | solution.py:568
  98.2 209.8 %copy-start.152 = (f32[1024]{0:T(1024)}, f32[1024]{0:T(1024)S(1)}, u32[]{:S(2)}) copy-start(f32[1024]{0:T(1024)S(1)} %mul.1279) | copy-start | bytes 12292
  98.3 103.0 %copy-start.155 = (f32[1024]{0:T(1024)}, f32[1024]{0:T(1024)S(1)}, u32[]{:S(2)}) copy-start(f32[1024]{0:T(1024)S(1)} %mul.1266) | copy-start | bytes 12292
  98.3 6.8 copy-start.169
  194.6 269.4 %copy-start.157 = (f32[1024]{0:T(1024)}, f32[1024]{0:T(1024)S(1)}, u32[]{:S(2)}) copy-start(f32[1024]{0:T(1024)S(1)} %mul.1293) | copy-start | bytes 12292
  194.8 415.5 %copy-start.172 = (f32[1024]{0:T(1024)}, f32[1024]{0:T(1024)S(1)}, u32[]{:S(2)}) copy-start(f32[1024]{0:T(1024)S(1)} %mul.1287) | copy-start | bytes 12292
  201.5 255.1 %copy-start.49 = (bf16[4,32,1024]{2,1,0:T(8,128)(2,1)}, bf16[4,32,1024]{2,1,0:T(8,128)(2,1)S(1)}, u32[]{:S(2)}) copy-start(bf16[4,32,1024]{2,1,0:T(8,128)(2,1)S(1)} %get-tuple-element.106) | copy-start | bytes 786436
  307.6 46.2 %copy-start.6 = (f32[2,256,1024]{2,1,0:T(8,128)}, f32[2,256,1024]{2,1,0:T(8,128)S(1)}, u32[]{:S(2)}) copy-start(f32[2,256,1024]{2,1,0:T(8,128)S(1)} %get-tuple-element.84) | copy-start | bytes 6291460
  330.0 19.2 %copy-start.12 = (bf16[2,256,16,64]{1,0,3,2:T(2,128)(2,1)}, bf16[2,256,16,64]{1,0,3,2:T(2,128)(2,1)S(1)}, u32[]{:S(2)}) copy-start(bf16[2,256,16,64]{1,0,3,2:T(2,128)(2,1)S(1)} %reshape.946) | copy-start | bytes 3145732
  330.0 6.6 copy-start.154
  355.3 255.1 %copy-start.165 = (f32[512]{0:T(512)}, f32[512]{0:T(512)S(1)}, u32[]{:S(2)}) copy-start(f32[512]{0:T(512)S(1)} %broadcast_multiply_fusion.4) | copy-start | bytes 6148
  357.0 99.4 %copy-start.167 = (f32[512]{0:T(512)}, f32[512]{0:T(512)S(1)}, u32[]{:S(2)}) copy-start(f32[512]{0:T(512)S(1)} %multiply_reduce_fusion.11) | copy-start | bytes 6148
  357.0 253.3 %copy-start.174 = (f32[512]{0:T(512)}, f32[512]{0:T(512)S(1)}, u32[]{:S(2)}) copy-start(f32[512]{0:T(512)S(1)} %fusion.204) | copy-start | bytes 6148
  454.2 5.4 copy-start.71
  463.3 9.8 copy-start.34
  463.9 4.7 copy-start.188
  464.0 4.6 copy-start.182
  464.1 6.7 copy-start.39
  466.3 6.8 copy-start.140
  468.6 6.9 copy-start.137
  470.9 6.8 copy-start.134
  473.1 6.7 copy-start.131
  482.9 127.5 %copy-start.22 = (f32[512,1024]{1,0:T(8,128)S(1)}, f32[512,1024]{1,0:T(8,128)}, u32[]{:S(2)}) copy-start(f32[512,1024]{1,0:T(8,128)} %copy-done.21) | copy-start | bytes 6291460
  483.0 133.5 %copy-start.66 = (bf16[128,1024]{1,0:T(8,128)(2,1)}, bf16[128,1024]{1,0:T(8,128)(2,1)S(1)}, u32[]{:S(2)}) copy-start(bf16[128,1024]{1,0:T(8,128)(2,1)S(1)} %multiply_convert_fusion.13) | copy-start | bytes 786436
  618.8 4.9 copy-start.125
  631.3 10.5 copy-start.95
  634.6 20.7 %copy-start.75 = (f32[512,1024]{1,0:T(8,128)}, f32[512,1024]{1,0:T(8,128)S(1)}, u32[]{:S(2)}) copy-start(f32[512,1024]{1,0:T(8,128)S(1)} %fusion.106) | copy-start | bytes 6291460
  638.2 7.3 copy-start.191
  641.8 7.4 copy-start.194
  645.5 6.8 copy-start.197
  676.7 10.9 copy-start.5
  692.8 16.1 %copy-start.20 = (bf16[512,8192]{1,0:T(8,128)(2,1)}, bf16[512,8192]{1,0:T(8,128)(2,1)S(1)}, u32[]{:S(2)}) copy-start(bf16[512,8192]{1,0:T(8,128)(2,1)S(1)} %multiply_convert_fusion) | copy-start | bytes 25165828
  711.3 13.3 copy-start.115
  711.3 4.4 copy-start.192
  715.7 22.7 %copy-start.97 = (bf16[512,1024]{1,0:T(8,128)(2,1)}, bf16[512,1024]{1,0:T(8,128)(2,1)S(1)}, u32[]{:S(2)}) copy-start(bf16[512,1024]{1,0:T(8,128)(2,1)S(1)} %fusion.52) | copy-start | bytes 3145732
  720.2 8.8 copy-start.200
  724.6 7.7 copy-start.204
  729.0 6.3 copy-start.202
  751.9 5.2 copy-start.117
  754.6 5.1 copy-start.119
  763.4 8.1 copy-start.147
  766.1 8.0 copy-start.123
  768.9 7.7 copy-start.121
  771.6 7.5 copy-start.145
  782.1 5.0 copy-start.33
  782.1 6.5 copy-start.160
  802.8 6.4 copy-start.13
  805.5 5.4 slice-start
  873.6 7.4 copy-start.73
  873.6 7.4 copy-start.74
  1227.9 45.1 %copy-start.164 = (f32[1,2,2,128]{3,1,2,0:T(2,128)S(1)}, f32[1,2,2,128]{3,1,2,0:T(2,128)}, u32[]{:S(2)}) copy-start(f32[1,2,2,128]{3,1,2,0:T(2,128)} %copy-done.163) | copy-start | bytes 6148
  1344.1 90.4 %copy-start.83 = (f32[1,32,3072]{2,1,0:T(8,128)S(1)}, f32[1,32,3072]{2,1,0:T(8,128)}, u32[]{:S(2)}) copy-start(f32[1,32,3072]{2,1,0:T(8,128)} %stack_reshape.21) | copy-start | bytes 1179652
  1499.5 5.7 copy-start.128
  1505.8 7.7 copy-start.82
  1513.6 6.4 copy-start.1
  (150 other events, 387.9 us)
Sparse Core Ops, SparseCore 0:
  10.5 37.8 all-gather.9
  51.9 77.6 all-gather.13
  131.2 164.9 all-gather.11
  299.8 152.1 all-gather.7
  455.4 152.6 all-gather.15
  860.9 76.1 all-gather.17

commit v2 on v1

--- a/solution.py
+++ b/solution.py
@@ -34,10 +34,25 @@
 LAG = 2
 
 
+DEC_INPUTS = (0, 0, 0, 1, 2, 3, 4, 4, 4, 4, 5, 6, 7, 8)
+ENC_INPUTS = (0, 0, 1, 1, 1, 2, 3, 3, 3, 3, 4, 5, 6, 7)
+CODE_UNITS = 8
+
+
+def stepped(table, k):
+    rises = [i for i in range(1, len(table)) if table[i] > table[i - 1]]
+    return sum((k >= i).astype(jnp.int32) for i in rises)
+
+
 def sum_kernel(
-    units, Z, p_ref, out_ref, own, from_core, held, from_x, from_y, all_x, all_y, kept, from_line,
-    own_sem, core_send, core_recv, one_send, one_recv, two_send, two_recv, line_send, line_recv,
+    Z, dec_x, dec_g, enc_x, enc_g, code_x, code_g, out_ref,
+    dec_xs, dec_gs, enc_xs, enc_gs, code_xs, code_gs, to_core,
+    own, from_core, held, from_x, from_y, all_x, all_y, kept, from_line,
+    load_sem, code_sem, core_send, core_recv, one_send, one_recv, two_send, two_recv, line_send, line_recv,
 ):
+    dec_units, enc_units = len(DEC_INPUTS), len(ENC_INPUTS)
+    plain_units = dec_units + enc_units
+    units = plain_units + CODE_UNITS
     depth = 2 * LAG
     dp, fs = lax.axis_index("dp"), lax.axis_index("fsdp")
     z, core = fs // 2, fs % 2
@@ -71,15 +86,44 @@
             src_ref=src, dst_ref=dst, send_sem=send, recv_sem=recv, device_id=device, device_id_type=MESH
         )
 
-    def own_copy(k):
-        return pltpu.make_async_copy(
-            p_ref.at[k, :, :, core], own.at[k % own_slots], own_sem.at[k % own_slots]
-        )
+    def loads(k):
+        slot, e = k % 2, k - dec_units
+        dec_place, enc_place = stepped(DEC_INPUTS, k), stepped(ENC_INPUTS, e)
+
+        def three(x, g, xs, gs, x_place, g_place):
+            return [
+                pltpu.make_async_copy(x.at[x_place, :, side], xs.at[slot, own_side], load_sem.at[own_side, slot])
+                for own_side, side in ((0, core), (1, 1 - core))
+            ] + [pltpu.make_async_copy(g.at[g_place], gs.at[slot], load_sem.at[2, slot])]
+
+        return (
+            (k < dec_units, three(dec_x, dec_g, dec_xs, dec_gs, dec_place, jnp.minimum(k, 10))),
+            (
+                (k >= dec_units) & (k < plain_units),
+                three(enc_x, enc_g, enc_xs, enc_gs, enc_place, jnp.minimum(e, 10)),
+            ),
+        )
+
+    def start_loads(k):
+        for here, copies in loads(k):
+
+            @pl.when(here)
+            def _(copies=copies):
+                for copy in copies:
+                    copy.start()
+
+    code_loads = [
+        pltpu.make_async_copy(code_x, code_xs, code_sem.at[0]),
+        pltpu.make_async_copy(code_g, code_gs, code_sem.at[1]),
+    ]
+    for copy in code_loads:
+        copy.start()
+    start_loads(jnp.int32(0))
 
     def core_copy(k):
         s = k % depth
         return remote(
-            p_ref.at[k, :, :, 1 - core], from_core.at[s], core_send.at[s], core_recv.at[s], core_dev
+            to_core.at[k % own_slots], from_core.at[s], core_send.at[s], core_recv.at[s], core_dev
         )
 
     def one_copies(k):
@@ -136,12 +180,52 @@
             down_copy(k, step).wait_recv()
             up_copy(k, step).wait_send()
 
+    def product(xs, gs, slot, side, into):
+        def rows(block, carry):
+            value = xs[slot, side, pl.ds(block * Z, Z)].reshape(-1, xs.shape[-1])
+            result = jnp.dot(value, gs[slot], preferred_element_type=F32).astype(BF)
+            into[block] = result.reshape(into.shape[1:])
+            return carry
+
+        lax.fori_loop(0, 4, rows, 0)
+
+    def code_product(k, side, into):
+        value = code_gs[:, k - plain_units].reshape(-1, code_gs.shape[-1])
+        width = into.shape[-1]
+
+        def columns(place, carry):
+            start = pl.multiple_of((2 * place + side) * width, width)
+            result = jnp.dot(value, code_xs[:, pl.ds(start, width)], preferred_element_type=F32).astype(BF)
+            into[:, place] = result.reshape(4, -1, width)
+            return carry
+
+        lax.fori_loop(0, Z, columns, 0)
+
     def begin(k):
-        own_copy(k).start()
-        core_copy(k).start()
+        slot, o = k % 2, k % own_slots
+        for (here, copies), xs, gs in zip(loads(k), (dec_xs, enc_xs), (dec_gs, enc_gs)):
+
+            @pl.when(here)
+            def _(copies=copies, xs=xs, gs=gs):
+                for copy in copies:
+                    copy.wait()
+                start_loads(k + 1)
+                product(xs, gs, slot, 1, to_core.at[o])
+                core_copy(k).start()
+                product(xs, gs, slot, 0, own.at[o])
+
+        @pl.when(k == plain_units)
+        def _():
+            for copy in code_loads:
+                copy.wait()
+
+        @pl.when(k >= plain_units)
+        def _():
+            code_product(k, 1 - core, to_core.at[o])
+            core_copy(k).start()
+            code_product(k, core, own.at[o])
 
     def after_core(k):
-        own_copy(k).wait()
         core_copy(k).wait()
 
         def one(block, carry):
@@ -222,22 +306,37 @@
     lax.fori_loop(0, units + (len(stages) - 1) * LAG, loop_step, 0)
 
 
-def sum_units(partial_sums, call_id):
-    units, devices, m, n = partial_sums.shape
-    Z = lax.axis_size("fsdp") // 2
-    if lax.axis_size("dp") != 4 or Z != 4 or m % 16:
-        return lax.psum_scatter(
-            partial_sums, AXES, scatter_dimension=1, tiled=True
-        ).reshape(units, m, n).astype(F32)
+def sum_products(dec_x, dec_g, enc_x, enc_g, code_x, code_g, call_id):
+    dp_size, fsdp_size = lax.axis_size("dp"), lax.axis_size("fsdp")
+    devices, Z = dp_size * fsdp_size, fsdp_size // 2
+    m = D // devices
+    if dp_size != 4 or Z != 4 or m % 32:
+        products = [matmul(dec_x[i], dec_g[min(k, 10)]) for k, i in enumerate(DEC_INPUTS)]
+        products += [matmul(enc_x[i], enc_g[min(k, 10)]) for k, i in enumerate(ENC_INPUTS)]
+        plain = jnp.stack(products).astype(BF).reshape(len(products), devices, m, D)
+        code = matmul(code_g, code_x).astype(BF).reshape(dp_size, D // dp_size, fsdp_size, VOCAB // fsdp_size)
+        code = code.transpose(0, 2, 1, 3).reshape(devices, D // dp_size, VOCAB // fsdp_size)
+        plain = lax.psum_scatter(plain, AXES, scatter_dimension=1, tiled=True)
+        code = lax.psum_scatter(code, AXES, scatter_dimension=0, tiled=True)
+        return plain.reshape(-1, m, D).astype(F32), code.reshape(D // dp_size, -1).astype(F32)
+    n, units = D, len(DEC_INPUTS) + len(ENC_INPUTS) + CODE_UNITS
     depth, half = 2 * LAG, Z // 2
     own_slots, held_slots, kept_slots = LAG + 1, 2 * LAG + 1, Z * LAG + 1
+    dec_rows, enc_rows, code_rows = dec_x.shape[2], enc_x.shape[2], code_g.shape[1]
     dma = pltpu.SemaphoreType.DMA
-    return pl.pallas_call(
-        partial(sum_kernel, units, Z),
+    out = pl.pallas_call(
+        partial(sum_kernel, Z),
         out_shape=jax.ShapeDtypeStruct((units, m, n), F32),
-        in_specs=[pl.BlockSpec(memory_space=pl.ANY)],
+        in_specs=[pl.BlockSpec(memory_space=pl.ANY)] * 6,
         out_specs=pl.BlockSpec(memory_space=pltpu.VMEM),
         scratch_shapes=[
+            pltpu.VMEM((2, 2, 4 * Z, m, dec_rows), BF),
+            pltpu.VMEM((2, dec_rows, n), BF),
+            pltpu.VMEM((2, 2, 4 * Z, m, enc_rows), BF),
+            pltpu.VMEM((2, enc_rows, n), BF),
+            pltpu.VMEM(code_x.shape, BF),
+            pltpu.VMEM((4, CODE_UNITS, m, code_rows), BF),
+            pltpu.VMEM((own_slots, 4, Z, m, n), BF),
             pltpu.VMEM((own_slots, 4, Z, m, n), BF),
             pltpu.VMEM((depth, 4, Z, m, n), BF),
             pltpu.VMEM((held_slots, 4, Z, m, n), BF),
@@ -247,7 +346,8 @@
             pltpu.VMEM((depth, Z, m, n), BF),
             pltpu.VMEM((kept_slots, Z, m, n), BF),
             pltpu.VMEM((2, Z - 1, depth, m, n), BF),
-            dma((own_slots,)),
+            dma((3, 2)),
+            dma((2,)),
             dma((depth,)),
             dma((depth,)),
             dma((2, depth)),
@@ -258,9 +358,301 @@
             dma((2, Z - 1, depth)),
         ],
         compiler_params=pltpu.CompilerParams(
-            collective_id=call_id, has_side_effects=True, vmem_limit_bytes=48 << 20
+            collective_id=call_id, has_side_effects=True, vmem_limit_bytes=60 << 20
         ),
-    )(partial_sums.reshape(units, 4, Z, 2, m, n))
+    )(
+        dec_x.reshape(-1, 4 * Z, 2, m, dec_rows),
+        dec_g,
+        enc_x.reshape(-1, 4 * Z, 2, m, enc_rows),
+        enc_g,
+        code_x,
+        code_g.reshape(4, CODE_UNITS, m, code_rows),
+    )
+    return out[:-CODE_UNITS], out[-CODE_UNITS:].reshape(-1, n)
+
+
+def spread_kernel(
+    tables, units, Z, table_ref, unit_ref, table_out, unit_out,
+    own_sem, line_send, line_recv, square_send, square_recv, core_send, core_recv,
+):
+    dp, fs = lax.axis_index("dp"), lax.axis_index("fsdp")
+    z, core = fs // 2, fs % 2
+    x_mate, y_mate = dp + 1 - 2 * (dp % 2), (dp + 2) % 4
+    across_dp = (x_mate + 2) % 4
+    core_dev, x_dev, y_dev = (dp, fs + 1 - 2 * core), (x_mate, fs), (y_mate, fs)
+    up_dev, down_dev = (dp, fs + 2), (dp, fs - 2)
+    has_up, has_down = z < Z - 1, z > 0
+    total, half = tables + units, Z // 2
+    every = slice(None)
+    table_rows, table_columns = table_out.shape[2] // tables, table_out.shape[3] // 4
+
+    def at(is_table, k, dp_at, z_at, core_at, part=None):
+        if is_table:
+            size = table_rows if part is None else table_rows // 2
+            rows = pl.ds(k * table_rows + (part or 0) * size, size)
+            columns = every if isinstance(dp_at, slice) else pl.ds(dp_at * table_columns, table_columns)
+            return table_out.at[z_at, core_at, rows, columns]
+        if part is None:
+            return unit_out.at[k - tables, dp_at, z_at, core_at]
+        size = unit_out.shape[4] // 2
+        return unit_out.at[k - tables, dp_at, z_at, core_at, pl.ds(part * size, size)]
+
+    def remote(ref, send, recv, device):
+        return pltpu.make_async_remote_copy(
+            src_ref=ref, dst_ref=ref, send_sem=send, recv_sem=recv, device_id=device, device_id_type=MESH
+        )
+
+    own = (
+        pltpu.make_async_copy(
+            table_ref, table_out.at[z, core, :, pl.ds(dp * table_columns, table_columns)], own_sem.at[0]
+        ),
+        pltpu.make_async_copy(unit_ref, unit_out.at[:, dp, z, core], own_sem.at[1]),
+    )
+    for copy in own:
+        copy.start()
+
+    barrier = pltpu.get_barrier_semaphore()
+    for device in (core_dev, x_dev, y_dev):
+        pl.semaphore_signal(barrier, inc=1, device_id=device, device_id_type=MESH)
+
+    @pl.when(has_up)
+    def _():
+        pl.semaphore_signal(barrier, inc=1, device_id=up_dev, device_id_type=MESH)
+
+    @pl.when(has_down)
+    def _():
+        pl.semaphore_signal(barrier, inc=1, device_id=down_dev, device_id_type=MESH)
+
+    for copy in own:
+        copy.wait()
+    pl.semaphore_wait(barrier, 3 + has_up.astype(jnp.int32) + has_down.astype(jnp.int32))
+
+    def line_copies(view, k, step):
+        s = step - 1
+        return (
+            (remote(view(jnp.maximum(z - s, 0)), line_send.at[0, s, k], line_recv.at[0, s, k], up_dev),
+             has_up & (z >= s), has_down & (z >= s + 1)),
+            (remote(view(jnp.minimum(z + s, Z - 1)), line_send.at[1, s, k], line_recv.at[1, s, k], down_dev),
+             has_down & (z + s <= Z - 1), has_up & (z + s + 1 <= Z - 1)),
+        )
+
+    def line_start(view, k, step):
+        for copy, sends, _ in line_copies(view, k, step):
+            pl.when(sends)(copy.start)
+
+    def line_wait(view, k, step):
+        for copy, sends, receives in line_copies(view, k, step):
+            pl.when(sends)(copy.wait_send)
+            pl.when(receives)(copy.wait_recv)
+
+    def to_core(ref, k, slot):
+        return remote(ref, core_send.at[slot, k], core_recv.at[slot, k], core_dev)
+
+    def square_copy(ref, k, slot):
+        return remote(
+            ref, square_send.at[slot, k], square_recv.at[slot, k], x_dev if slot % 2 == 0 else y_dev
+        )
+
+    def line_first(is_table):
+        def view(k):
+            return lambda place: at(is_table, k, dp, place, core)
+
+        def row(k, dp_at):
+            return at(is_table, k, dp_at, every, core)
+
+        def ones(k):
+            return square_copy(row(k, dp), k, 0), square_copy(row(k, dp), k, 1)
+
+        def twos(k):
+            return (
+                square_copy(at(is_table, k, y_mate, pl.ds(0, half), core), k, 2),
+                square_copy(at(is_table, k, x_mate, pl.ds(half, Z - half), core), k, 3),
+            )
+
+        def line(step):
+            def run(k):
+                if step > 1:
+                    line_wait(view(k), k, step - 1)
+                if step < Z:
+                    line_start(view(k), k, step)
+                else:
+                    for copy in ones(k):
+                        copy.start()
+                    to_core(row(k, dp), k, 0).start()
+            return run
+
+        def after_one(k):
+            for copy in ones(k):
+                copy.wait()
+            for copy in twos(k):
+                copy.start()
+            to_core(row(k, x_mate), k, 1).start()
+            to_core(row(k, y_mate), k, 2).start()
+
+        def after_two(k):
+            for copy in twos(k):
+                copy.wait()
+            to_core(row(k, across_dp), k, 3).start()
+
+        def finish(k):
+            for slot in range(4):
+                to_core(row(k, dp), k, slot).wait()
+
+        return [line(step) for step in range(1, Z + 1)] + [after_one, after_two, finish]
+
+    def square_first(is_table):
+        def plane(k):
+            return lambda place: at(is_table, k, every, place, core)
+
+        def ones(k):
+            ref = at(is_table, k, dp, z, core)
+            return square_copy(ref, k, 0), square_copy(ref, k, 1)
+
+        def twos(k):
+            return (
+                square_copy(at(is_table, k, y_mate, z, core, 0), k, 2),
+                square_copy(at(is_table, k, x_mate, z, core, 1), k, 3),
+            )
+
+        def begin(k):
+            for copy in ones(k):
+                copy.start()
+
+        def after_one(k):
+            for copy in ones(k):
+                copy.wait()
+            for copy in twos(k):
+                copy.start()
+
+        def after_two(k):
+            for copy in twos(k):
+                copy.wait()
+            line_start(plane(k), k, 1)
+            to_core(plane(k)(z), k, z).start()
+
+        def line(step):
+            def run(k):
+                line_wait(plane(k), k, step)
+                if step + 1 < Z:
+                    line_start(plane(k), k, step + 1)
+
+                @pl.when(z - step >= 0)
+                def _():
+                    to_core(plane(k)(jnp.maximum(z - step, 0)), k, jnp.maximum(z - step, 0)).start()
+
+                @pl.when(z + step <= Z - 1)
+                def _():
+                    to_core(plane(k)(jnp.minimum(z + step, Z - 1)), k, jnp.minimum(z + step, Z - 1)).start()
+            return run
+
+        def finish(k):
+            for place in range(Z):
+                to_core(plane(k)(place), k, place).wait()
+
+        return [begin, after_one, after_two] + [line(step) for step in range(1, Z)] + [finish]
+
+    forms = [(is_table, first, form(is_table))
+             for is_table in (True, False) for first, form in ((True, line_first), (False, square_first))]
+    n_stages = Z + 3
+
+    def loop_step(j, carry):
+        for place in reversed(range(n_stages)):
+            k = j - place * LAG
+            turn = k % 9
+            by_line = (turn != 3) & (turn != 7)
+            for is_table, first, stages in forms:
+                here = (k >= 0) & (k < tables) if is_table else (k >= tables) & (k < total)
+                here = here & (by_line if first else jnp.logical_not(by_line))
+
+                @pl.when(here)
+                def _(k=k, run=stages[place]):
+                    run(k)
+
+        return carry
+
+    lax.fori_loop(0, total + (n_stages - 1) * LAG, loop_step, 0)
+
+
+def spread(table, units, call_id):
+    count, m, n = units.shape
+    Z = lax.axis_size("fsdp") // 2
+    if lax.axis_size("dp") != 4 or Z != 4 or m % 32:
+        whole = lax.all_gather(lax.all_gather(table, "dp", axis=1, tiled=True), "fsdp", axis=0, tiled=True)
+        return whole, lax.all_gather(units, AXES, axis=1, tiled=True)
+    tables, dma = 8, pltpu.SemaphoreType.DMA
+    total = tables + count
+    whole, units = pl.pallas_call(
+        partial(spread_kernel, tables, count, Z),
+        out_shape=(
+            jax.ShapeDtypeStruct((Z, 2, table.shape[0], 4 * table.shape[1]), BF),
+            jax.ShapeDtypeStruct((count, 4, Z, 2, m, n), BF),
+        ),
+        in_specs=[pl.BlockSpec(memory_space=pl.ANY)] * 2,
+        out_specs=[pl.BlockSpec(memory_space=pl.ANY)] * 2,
+        scratch_shapes=[
+            dma((2,)),
+            dma((2, Z - 1, total)),
+            dma((2, Z - 1, total)),
+            dma((4, total)),
+            dma((4, total)),
+            dma((4, total)),
+            dma((4, total)),
+        ],
+        compiler_params=pltpu.CompilerParams(collective_id=call_id, has_side_effects=True),
+    )(table, units)
+    return whole.reshape(-1, 4 * table.shape[1]), units.reshape(count, -1, n)
+
+
+def exchange_kernel(size, inner, in_ref, out_ref, send_sem, recv_sem):
+    me = lax.axis_index("dp") * inner + lax.axis_index("fsdp")
+
+    def peer(i):
+        other = lax.rem(me + i, size)
+        return other, (other // inner, lax.rem(other, inner))
+
+    barrier = pltpu.get_barrier_semaphore()
+
+    def greet(i, carry):
+        pl.semaphore_signal(barrier, inc=1, device_id=peer(i)[1], device_id_type=MESH)
+        return carry
+
+    def copy(i):
+        other, device = peer(i)
+        return pltpu.make_async_remote_copy(
+            src_ref=in_ref.at[other], dst_ref=out_ref.at[me], send_sem=send_sem.at[i],
+            recv_sem=recv_sem.at[i], device_id=device, device_id_type=MESH,
+        )
+
+    def begin(i, carry):
+        copy(i).start()
+        return carry
+
+    def end(i, carry):
+        copy(i).wait()
+        return carry
+
+    lax.fori_loop(1, size, greet, 0)
+    out_ref[me] = in_ref[me]
+    pl.semaphore_wait(barrier, size - 1)
+    lax.fori_loop(1, size, begin, 0)
+    lax.fori_loop(1, size, end, 0)
+
+
+def exchange(blocks, call_id):
+    size, inner = blocks.shape[0], lax.axis_size("fsdp")
+    return pl.pallas_call(
+        partial(exchange_kernel, size, inner),
+        out_shape=jax.ShapeDtypeStruct(blocks.shape, F32),
+        in_specs=[pl.BlockSpec(memory_space=pltpu.VMEM)],
+        out_specs=pl.BlockSpec(memory_space=pltpu.VMEM),
+        scratch_shapes=[pltpu.SemaphoreType.DMA((size,)), pltpu.SemaphoreType.DMA((size,))],
+        compiler_params=pltpu.CompilerParams(collective_id=call_id, has_side_effects=True),
+    )(blocks)
+
+
+def tiles(values, count):
+    padded = jnp.pad(values, ((0, 1024 - values.shape[0]),)).reshape(1, 8, 128)
+    return jnp.broadcast_to(padded, (count, 8, 128))
 
 
 def layer_norm(stream, gain):
@@ -377,47 +769,46 @@
     project, mix_out, cross, cross_out, ffn_up, ffn_down = weights
     gain_grads = [None] * len(gains)
     grad_stream, gain_grads[-1] = norm_back(stored["before_final"], gains[-1], grad_final)
-    grad_low = grad_stream.astype(BF)
-    up_pairs, down_pairs = [], []
+    ffn_low = grad_stream.astype(BF)
+    grad_pres = []
     grad_ffn = 0.0
-    for pre, low, up, down in zip(stored["hidden_pre"], stored["hidden"], ffn_up, ffn_down):
-        down_pairs.append((low, grad_low))
+    for pre, up, down in zip(stored["hidden_pre"], ffn_up, ffn_down):
         _, gelu_pull = jax.vjp(partial(jax.nn.gelu, approximate=True), pre)
-        grad_pre = gelu_pull(against(grad_low, down))[0].astype(BF)
-        up_pairs.append((stored["ffn_in"], grad_pre))
-        grad_ffn = grad_ffn + against(grad_pre, up)
+        grad_pres.append(gelu_pull(against(ffn_low, down))[0].astype(BF))
+        grad_ffn = grad_ffn + against(grad_pres[-1], up)
     grad_normed, gain_grads[-2] = norm_back(stored["before_ffn"], gains[-2], grad_ffn)
     grad_stream = grad_stream + grad_normed
-    cross_pairs, cross_out_pairs = [], []
+    cross_inputs, cross_grads, memory_grads = [], [], []
     grad_memory = None
     if memory is not None:
-        grad_low = grad_stream.astype(BF)
-        cross_out_pairs.append((stored["cross_mixed"], grad_low))
-        grad_mixed = against(grad_low, cross_out).astype(BF)
+        cross_low = grad_stream.astype(BF)
+        grad_mixed = against(cross_low, cross_out).astype(BF)
         grads = [
             heads_last(grad.astype(BF)) for grad in attention_back(*stored["cross_attention"], grad_mixed)
         ]
-        cross_pairs = [(stored["cross_in"], grads[0]), (memory, grads[1]), (memory, grads[2])]
+        cross_inputs = [stored["cross_in"], stored["cross_mixed"]]
+        cross_grads = [grads[0], cross_low]
+        memory_grads = grads[1:]
         grad_memory = against(grads[1], cross[1]) + against(grads[2], cross[2])
         grad_normed, gain_grads[1] = norm_back(
             stored["after_self"], gains[1], against(grads[0], cross[0])
         )
         grad_stream = grad_stream + grad_normed
-    grad_low = grad_stream.astype(BF)
-    out_pairs = [(stored["attended"], grad_low)]
-    grad_mixed = against(grad_low, mix_out).astype(BF)
+    self_low = grad_stream.astype(BF)
+    grad_mixed = against(self_low, mix_out).astype(BF)
     grads = [
         heads_last(grad.astype(BF)) for grad in attention_back(*stored["self_attention"], grad_mixed)
     ]
-    project_pairs = [(stored["normed"], grad) for grad in grads]
     grad_normed, gain_grads[0] = norm_back(
         stored["stream"],
         gains[0],
         sum(against(grads[i], project[i]) for i in range(3)),
     )
     grad_stream = grad_stream + grad_normed
-    pairs = (project_pairs, out_pairs, cross_pairs, cross_out_pairs, up_pairs, down_pairs)
-    return grad_stream, grad_memory, gain_grads, pairs
+    inputs = [stored["normed"], stored["attended"], *cross_inputs, stored["ffn_in"], *stored["hidden"]]
+    outputs = [*grads, self_low, *cross_grads, *grad_pres, ffn_low]
+    parts = (inputs, outputs) if memory is None else (inputs, outputs, memory_grads)
+    return grad_stream, grad_memory, gain_grads, parts
 
 
 def adam_step(weight, moment_one, second, gradient, rate):
@@ -499,17 +890,16 @@
     wanted = jnp.repeat(caption_of, IMG_LEN)
     cross_visible = (segments[None, :] == wanted[:, None])[None]
 
-    small = jnp.concatenate([text_ids[0].astype(F32), norm_gains.reshape(-1)])
-    small = lax.all_gather(small, AXES)
+    small = tiles(jnp.concatenate([text_ids[0].astype(F32), norm_gains.reshape(-1)]), devices)
+    small = exchange(small, 3).reshape(devices, 1024)[:, : TXT_LEN + 7 * norm_gains.shape[1]]
     all_ids = small[:, :TXT_LEN].astype(jnp.int32).reshape(-1)
     gains = small[:, TXT_LEN:].reshape(devices, 7, -1).transpose(1, 0, 2).reshape(7, D)
     gains = gains.astype(BF).astype(F32)
 
-    def gather(units):
-        return lax.all_gather(units.astype(BF), AXES, axis=1, tiled=True)
-
-    code_cols = lax.all_gather(code_table.astype(BF), "dp", axis=1, tiled=True)
-    code_full = lax.all_gather(code_cols, "fsdp", axis=0, tiled=True)
+    base = me * text_table.shape[0]
+    owned = (all_ids[:, None] - base == jnp.arange(text_table.shape[0])[None, :]).astype(BF)
+    looked = matmul(owned, text_table.astype(BF)).astype(BF)
+    text_rows = lax.psum_scatter(looked, AXES, scatter_dimension=0, tiled=True)
 
     def layer_units(which):
         return [
@@ -519,19 +909,15 @@
             ffn_down[min(which, 1)].reshape(4, rows, D),
         ]
 
-    enc_units = gather(jnp.concatenate(layer_units(0)))
-    self_units = gather(jnp.concatenate(layer_units(1)[:2]))
-    late_units = gather(jnp.concatenate(layer_units(2)))
+    shards = layer_units(0) + layer_units(1)[:2] + layer_units(2)
+    code_full, units = spread(code_table.astype(BF), jnp.concatenate(shards).astype(BF), 4)
+    enc_units, self_units, late_units = units[:12], units[12:16], units[16:]
     enc_weights = (enc_units[:3], enc_units[3], None, None, enc_units[4:8], enc_units[8:])
     dec_weights = (
         self_units[:3], self_units[3], late_units[:3], late_units[3], late_units[4:8], late_units[8:]
     )
 
-    base = me * text_table.shape[0]
-    owned = (all_ids[:, None] - base == jnp.arange(text_table.shape[0])[None, :]).astype(BF)
-    looked = matmul(owned, text_table.astype(BF)).astype(BF)
-    looked = looked.reshape(devices, TXT_LEN // rows, rows, D).transpose(1, 0, 2, 3)
-    text_in = sum_units(looked, 0).reshape(TXT_LEN, D) * scale_in + positions(TXT_LEN, D)
+    text_in = text_rows.astype(F32) * scale_in + positions(TXT_LEN, D)
     enc_gains = [gains[i] for i in range(3)]
     dec_gains = [gains[i] for i in range(3, 7)]
     memory, enc_stored = layer_forward(text_in, enc_weights, enc_gains, text_visible, None, None)
@@ -557,10 +943,10 @@
     ).astype(BF)
     grad_final = matmul(grad_logits, code_full)
 
-    grad_image, grad_memory, dec_gain_grads, dec_pairs = layer_backward(
+    grad_image, grad_memory, dec_gain_grads, dec_parts = layer_backward(
         grad_final, dec_weights, dec_gains, dec_stored, memory
     )
-    grad_text, _, enc_gain_grads, enc_pairs = layer_backward(
+    grad_text, _, enc_gain_grads, enc_parts = layer_backward(
         grad_memory, enc_weights, enc_gains, enc_stored, None
     )
     gain_part = jnp.stack(enc_gain_grads + dec_gain_grads)
@@ -570,39 +956,52 @@
 
     grad_looked = grad_image.reshape(image_count, IMG_LEN, D)[:, 1:] * scale_in
     grad_looked = jnp.pad(grad_looked, ((0, 0), (0, 1), (0, 0))).reshape(-1, D).astype(BF)
-    code_part = across(
-        jnp.concatenate([grad_logits, hit.astype(BF)]), jnp.concatenate([final_out, grad_looked])
-    ).astype(BF)
-    code_parts = 8
-    code_part = (
-        code_part.reshape(fsdp_size, code_parts, -1, dp_size, D // dp_size)
-        .transpose(1, 3, 0, 2, 4)
-        .reshape(code_parts, devices, -1, D // dp_size)
-    )
-    pairs = [pair for group in (*enc_pairs, *dec_pairs) for pair in group]
-    weight_part = jnp.stack([across(*pair).astype(BF) for pair in pairs])
-    weight_sum = sum_units(weight_part.reshape(len(pairs), devices, rows, D), 1)
-    code_grad = sum_units(code_part, 2).reshape(code_table.shape)
-
-    enc_sum, dec_sum = weight_sum[:12], weight_sum[12:]
-    small_sum = lax.psum(jnp.concatenate([gain_part.reshape(-1), loss_part[None]]), AXES)
-    loss_sum = small_sum[-1]
-    gains_grad = lax.dynamic_slice_in_dim(small_sum[:-1].reshape(7, D), me * rows, rows, 1)
+    code_x = jnp.concatenate([grad_logits, hit.astype(BF)])
+    code_g = jnp.concatenate([final_out, grad_looked]).T
+
+    def inputs(values):
+        return jnp.stack([value.T for value in values])
+
+    def gradients_of(values):
+        return jnp.stack(values)
+
+    enc_x, enc_g = enc_parts
+    dec_x, dec_g, memory_g = dec_parts
+    plain_sum, code_sum = sum_products(
+        inputs(dec_x),
+        gradients_of(dec_g),
+        inputs([memory] + enc_x),
+        gradients_of(memory_g + enc_g),
+        code_x,
+        code_g,
+        1,
+    )
+    code_grad = code_sum.T
+    dec_sum, enc_sum = plain_sum[:14], plain_sum[14:]
+
+    gain_blocks = gain_part.reshape(7, devices, rows).transpose(1, 0, 2).reshape(devices, 7 * rows)
+    gain_blocks = jnp.concatenate([gain_blocks, jnp.full((devices, 1), loss_part)], axis=1)
+    gain_blocks = jnp.pad(gain_blocks, ((0, 0), (0, 1024 - gain_blocks.shape[1])))
+    small_sum = jnp.sum(exchange(gain_blocks.reshape(devices, 8, 128), 5), axis=0).reshape(-1)
+    loss_sum = small_sum[7 * rows]
+    gains_grad = small_sum[: 7 * rows].reshape(7, rows)
     gradients = (
         jnp.stack(
-            [from_column_units(part) for part in (enc_sum[:3], dec_sum[:3], dec_sum[4:7])]
+            [
+                from_column_units(part)
+                for part in (enc_sum[2:5], dec_sum[:3], jnp.concatenate([dec_sum[4:5], enc_sum[:2]]))
+            ]
         ),
-        jnp.stack([enc_sum[3], dec_sum[3], dec_sum[7]]),
-        jnp.stack(
-            [from_hidden_units(part, devices) for part in (enc_sum[4:8], dec_sum[8:12])]
-        ),
-        jnp.stack([part.reshape(-1, D) for part in (enc_sum[8:], dec_sum[12:])]),
+        jnp.stack([enc_sum[5], dec_sum[3], dec_sum[5]]),
+        jnp.stack([from_hidden_units(part, devices) for part in (enc_sum[6:10], dec_sum[6:10])]),
+        jnp.stack([part.reshape(-1, D) for part in (enc_sum[10:], dec_sum[10:])]),
         gains_grad,
         text_grad,
         code_grad,
     )
     square_part = sum((jnp.sum(gradient * gradient) for gradient in gradients))
-    grad_norm = jnp.sqrt(lax.psum(square_part, AXES))
+    squares = exchange(tiles(square_part[None], devices), 6)[:, 0, 0]
+    grad_norm = jnp.sqrt(jnp.sum(squares))
     factor = CLIP_NORM / jnp.maximum(grad_norm, CLIP_NORM)
     params = (mix_in, mix_out, ffn_up, ffn_down, norm_gains, text_table, code_table)
     firsts = (

time: 1540 us -> 1340 us (0.87)
  Pallas kernels: 425 us -> 744 us
  waiting for transfers between devices: 316 us -> 0.04 us
  matrix products: 307 us -> 177 us
  blocking collectives: 119 us -> 0 us
  local copies, waits for them, and re-layouts: 246 us -> 282 us
  other arithmetic: 90.2 us -> 108 us
    pallas_call x3 -> x5, Pallas kernels: 425 us -> 744 us  [the longest x1 376 us: spread(): pl.pallas_call(partial(spread_kernel, tables, count, Z), out_shape=(jax.S...]
    all_gather x5 -> x0, waiting for transfers between devices: 316 us -> none  [the longest x3 220 us: gather(): return lax.all_gather(units.astype(BF), AXES, axis=1, tiled=True)]
    psum x2 -> x0, blocking collectives: 78.3 us -> none  [the longest x1 39.4 us: on_device(): lax.psum(jnp.concatenate([gain_part.reshape(-1), loss_part[None]]), AXES)]
    dot_general x30 -> x1, matrix products: 76.8 us -> 9.83 us  [across(): lax.dot_general(first_op, second_op, (((0,), (0,)), ((), ())), preferred_...]
    another operation x8 -> x22, local copies, waits for them, and re-layouts: 14.5 us -> 73.7 us  [the longest x12 33.5 us: gradients_of(): return jnp.stack(values)]
    reshape x6 -> x2, local copies, waits for them, and re-layouts: 52.6 us -> 0.86 us  [the longest x1 0.77 us: on_device(): norm_gains.reshape(-1)]
    dot_general x29, matrix products: 101 us -> 59.6 us  [against(): lax.dot_general(first_op, second_op, (((1,), (1,)), ((), ())), preferred_...]
    unnamed x1 -> x0, blocking collectives: 40.5 us -> none
  transfers between devices with their start and end apart: 6 -> 2, of which waited for: 4 -> 0; matrix products, arithmetic and copies ran while one was open for 22% -> 23% of each run, Pallas kernels for 28% -> 54%
where the time goes in v2:
time: 1340 us; the launch traced here: 1330 us
  Pallas kernels  744 us (56%)
  local copies, waits for them, and re-layouts  282 us (21%)
  matrix products  177 us (13%)
  other arithmetic  108 us (8%)
  between operations  24 us (2%)
    pallas_call x1, Pallas kernels, spread(): pl.pallas_call(partial(spread_kernel, tables, count, Z), out_shape=(jax.S...  376 us
    pallas_call x1, Pallas kernels, sum_products(): pl.pallas_call(partial(sum_kernel, Z), out_shape=jax.ShapeDtypeStruct((un...  335 us
    unnamed x566, local copies, waits for them, and re-layouts  89.5 us
    dot_general x30, matrix products, matmul(): return jnp.dot(first_op, second_op, preferred_element_type=jnp.float32)  71.5 us
    dot_general x29, matrix products, against(): lax.dot_general(first_op, second_op, (((1,), (1,)), ((), ())), preferred_...  59.6 us
    pallas_call x3, Pallas kernels, exchange(): pl.pallas_call(partial(exchange_kernel, size, inner), out_shape=jax.Shape...  33.8 us
    another operation x12, local copies, waits for them, and re-layouts, gradients_of(): return jnp.stack(values)  33.5 us
    another operation x1, local copies, waits for them, and re-layouts, layer_forward(): hidden_pre = [matmul(ffn_in, up) for up in ffn_up]  27 us
  transfers between devices with their start and end apart: 2, of which 0 were waited for; matrix products, arithmetic and copies ran while one was open for 23% of the time, Pallas kernels for 54%

profile of v2, /device:TPU:0, one launch (start us, length us, event | category | flops | bytes accessed | tf_op | source)
XLA Modules:
  0.0 1334.9 jit_solution(1119404722791274172)
XLA Ops:
  9.4 13.3 shard_map.416
  24.2 8.4 fusion.8
  53.7 375.7 %shard_map.417 = (bf16[4,2,1024,1024]{3,2,1,0:T(8,128)(2,1)}, bf16[28,4,4,2,32,1024]{5,4,3,2,1,0:T(8,128)(2,1)}) custom-call(bf16[1024,256]{1,0:T(8,128)(2,1)} %convert_element_type.331.table_ref, bf16[28,32,1024]{2,1,0:T(8,128)(2,1)} %copy-done.114), custom_call_target="tpu_custom_call" | custom-call | tf_op jit(solution)/shard_map/pallas_call | solution.py:584
  429.4 10.7 gather_fusion
  443.4 13.5 %fusion.287 = (bf16[1,4,4,2,32,1024]{5,4,3,2,1,0:T(8,128)(2,1)}, bf16[1,4,4,2,32,1024]{5,4,3,2,1,0:T(8,128)(2,1)}, bf16[1,4,4,2,32,1024]{5,4,3,2,1,0:T(8,128)(2,...) fusion(bf16[28,4,4,2,32,1024]{5,4,3,2,1,0:T(8,128)(2,1)} %get-t, ...), kind=kLoop, calls=%fused_computation.569 | loop fusion | bytes 37748736 | tf_op jit(solution)/shard_map/slice | solution.py:917
  463.1 4.1 convolution_convert_fusion.7
  469.9 3.2 convolution_convert_fusion.6
  474.4 10.3 reshape.804
  484.7 6.6 fusion.125
  491.3 9.3 fusion.295
  501.6 2.4 copy-done.8
  507.5 3.3 fusion.296
  518.4 27.0 %fusion.286 = (bf16[1,4,4,2,32,1024]{5,4,3,2,1,0:T(8,128)(2,1)}, bf16[1,4,4,2,32,1024]{5,4,3,2,1,0:T(8,128)(2,1)}, bf16[1,4,4,2,32,1024]{5,4,3,2,1,0:T(8,128)(2,...) fusion(bf16[28,4,4,2,32,1024]{5,4,3,2,1,0:T(8,128)(2,1)} %get-t, ...), kind=kLoop, calls=%fused_computation.568 | loop fusion | bytes 79691776 | tf_op jit(solution)/shard_map/unstack | solution.py:760
  545.4 6.6 fusion.3
  554.1 2.3 convolution_convert_fusion.16
  580.3 5.2 fusion.298
  585.5 2.9 divide_convert_fusion.1
  594.5 2.6 fusion.53
  597.1 2.6 fusion.61
  599.8 2.6 fusion.69
  602.4 2.6 fusion.77
  614.2 16.2 %fusion.301 = (f32[512]{0:T(512)S(1)}, f32[512,8192]{1,0:T(8,128)}) fusion(bf16[512,1024]{1,0:T(8,128)(2,1)S(1)} %multiply_convert_fusion.5, bf16[8192,1024]{1,0:T(8,128)(2,1)} %bitcast.526), kind=kOutput, calls=%fused_computation.583 | convolution fusion | flops 8594128896 | bytes 34605056 | tf_op jit(solution)/shard_map/dot_general | solution.py:687
  630.4 10.2 multiply_reduce_fusion
  641.3 5.2 multiply_convert_fusion
  646.5 16.8 %multiply_reduce_fusion.2 = (f32[1024]{0:T(1024)}, f32[512]{0:T(512)S(1)}, f32[512,1024]{1,0:T(8,128)S(1)}) fusion(f32[512,1024]{1,0:T(8,128)S(1)} %copy-done.12, f32[512]{0:T(512)S(1)} %fusion.223, f32[512]{0:T(512)S(1)} %broadcast_multiply_fusion, f32[1024]{0:T(1024)S(1)} %mul.1365, bf16[512,8192]{1,0:T(8,128)(2,1)S(1)} %multiply_convert_fusion, ...), kind=kOutput, calls=%fused_computation.122 | convolution fusion | flops 8593602560 | bytes 29374464 | tf_op jit(solution)/shard_map/dot_general | solution.py:677
  666.5 2.4 fusion.31
  668.9 2.4 fusion.24
  671.5 2.4 fusion.38
  674.1 2.4 fusion.45
  689.0 2.3 copy.122
  691.2 2.8 convolution_convert_fusion.12
  732.2 5.1 multiply_reduce_fusion.4
  741.5 2.3 convolution_convert_fusion.3
  743.7 2.3 copy.130
  748.1 4.3 fusion.4
  752.5 4.2 fusion.5
  756.8 2.4 fusion.88
  762.9 4.0 copy.187
  766.9 3.3 copy.138
  770.2 3.8 copy.188
  774.0 3.9 fusion.84
  780.9 3.9 copy.189
  798.8 3.9 copy.168
  820.0 4.1 reshape.851
  824.1 4.1 reshape.852
  828.2 3.4 reshape.853
  831.6 2.3 copy.155
  835.2 2.4 copy.144
  876.7 9.0 pad_maximum_fusion.code_x
  885.8 334.8 %shard_map.419 = f32[36,32,1024]{2,1,0:T(8,128)} custom-call(bf16[9,16,2,32,512]{4,3,2,1,0:T(8,128)(2,1)} %copy-done.38, bf16[11,512,1024]{2,1,0:T(8,128)(2,1)} %copy-done.37, bf16[8,16,2,32,128]{4,3,2,1,0:T(8,128)(2,1)} %constant_dynamic-update-slice_fusion.20.enc_x, bf16[11,128,1024]{2,1,0:T(8,128)(2,1)} %bitcast_dynamic-update-slice_fusion.7.enc_g, ...), custom_call_target="tpu_custom_call" | custom-call | tf_op jit(solution)/shard_map/pallas_call | solution.py:327
  1220.7 2.7 fusion.288
  1225.1 3.1 copy.172
  1228.2 4.4 stack_reshape.60
  1234.5 3.1 copy.173
  1237.6 4.4 stack_reshape.61
  1250.6 9.8 shard_map.418
  1275.2 9.8 multiply_reduce_fusion.13
  1287.0 10.7 shard_map.420
  1300.1 2.3 slice_multiply_fusion.1
  1302.4 2.5 copy.174
  1306.2 4.4 multiply_subtract_fusion.3
  1310.7 2.3 multiply_subtract_fusion.4
  1315.0 2.5 multiply_subtract_fusion.1
  1322.5 4.1 multiply_subtract_fusion
  (818 shorter events, 263.2 us)
Async XLA Ops:
  7.2 508.7 %copy-start = (s32[2]{0:T(128)S(1)}, s32[2]{0:T(128)}, u32[]{:S(2)}) copy-start(s32[2]{0:T(128)} %param.28) | copy-start | bytes 28
  7.2 544.8 %reduce-scatter.2.cloned.1.call-start = ((), (), s32[]{:S(2)}) async-start(), calls=%async_computation.1 | async-start | bytes 8650752 | tf_op jit(solution)/shard_map/reduce_scatter | solution.py:902
  32.7 1242.5 %all-gather.2.cloned.1.call-start = ((), (), s32[]{:S(2)}) async-start(), calls=%async_computation.2 | async-start | bytes 8650752 | tf_op jit(solution)/shard_map/all_gather | solution.py:954
  47.0 5.5 copy-start.153
  47.4 509.2 %copy-start.201 = (f32[1024]{0:T(1024)}, f32[1024]{0:T(1024)S(1)}, u32[]{:S(2)}) copy-start(f32[1024]{0:T(1024)S(1)} %mul.1286) | copy-start | bytes 12292
  47.5 516.0 %copy-start.205 = (f32[1024]{0:T(1024)}, f32[1024]{0:T(1024)S(1)}, u32[]{:S(2)}) copy-start(f32[1024]{0:T(1024)S(1)} %mul.1313) | copy-start | bytes 12292
  47.6 395.4 %copy-start.207 = (f32[1024]{0:T(1024)}, f32[1024]{0:T(1024)S(1)}, u32[]{:S(2)}) copy-start(f32[1024]{0:T(1024)S(1)} %mul.1299) | copy-start | bytes 12292
  442.7 64.8 %copy-start.4 = (f32[2,256,1024]{2,1,0:T(8,128)}, f32[2,256,1024]{2,1,0:T(8,128)S(1)}, u32[]{:S(2)}) copy-start(f32[2,256,1024]{2,1,0:T(8,128)S(1)} %get-tuple-element.88) | copy-start | bytes 6291460
  443.4 13.5 %copy-start.150 = (bf16[2,256,1024]{2,1,0:T(8,128)(2,1)}, bf16[2,256,1024]{2,1,0:T(8,128)(2,1)S(1)}, u32[]{:S(2)}) copy-start(bf16[2,256,1024]{2,1,0:T(8,128)(2,1)S(1)} %multiply_convert_fusion.12) | copy-start | bytes 3145732
  484.7 19.4 %copy-start.39 = (bf16[2,256,16,64]{1,0,3,2:T(2,128)(2,1)}, bf16[2,256,16,64]{1,0,3,2:T(2,128)(2,1)S(1)}, u32[]{:S(2)}) copy-start(bf16[2,256,16,64]{1,0,3,2:T(2,128)(2,1)S(1)} %reshape.804) | copy-start | bytes 3145732
  516.1 29.3 %copy-start.213 = (f32[1,2,2,128]{3,1,2,0:T(2,128)}, f32[1,2,2,128]{3,1,2,0:T(2,128)S(1)}, u32[]{:S(2)}) copy-start(f32[1,2,2,128]{3,1,2,0:T(2,128)S(1)} %copy.199) | copy-start | bytes 6148
  545.4 8.0 copy-start.20
  553.1 9.5 copy-start.6
  554.1 4.9 copy-start.174
  565.5 7.8 copy-start.195
  566.7 5.7 copy-start.189
  574.7 127.3 %copy-start.16 = (f32[128,1024]{1,0:T(8,128)}, f32[128,1024]{1,0:T(8,128)S(1)}, u32[]{:S(2)}) copy-start(f32[128,1024]{1,0:T(8,128)S(1)} %get-tuple-element.155) | copy-start | bytes 1572868
  580.3 5.2 copy-start.184
  597.1 7.9 copy-start.245
  599.7 6.7 copy-start.249
  602.4 6.4 copy-start.247
  605.0 5.4 copy-start.135
  614.2 16.2 %copy-start.88 = (bf16[512,1024]{1,0:T(8,128)(2,1)}, bf16[512,1024]{1,0:T(8,128)(2,1)S(1)}, u32[]{:S(2)}) copy-start(bf16[512,1024]{1,0:T(8,128)(2,1)S(1)} %multiply_convert_fusion.5) | copy-start | bytes 3145732
  630.4 10.9 copy-start.3
  641.3 5.2 copy-start.12
  646.5 16.8 %copy-start.13 = (bf16[512,8192]{1,0:T(8,128)(2,1)}, bf16[512,8192]{1,0:T(8,128)(2,1)S(1)}, u32[]{:S(2)}) copy-start(bf16[512,8192]{1,0:T(8,128)(2,1)S(1)} %multiply_convert_fusion) | copy-start | bytes 25165828
  664.0 20.4 %copy-start.9 = (f32[512,1024]{1,0:T(8,128)}, f32[512,1024]{1,0:T(8,128)S(1)}, u32[]{:S(2)}) copy-start(f32[512,1024]{1,0:T(8,128)S(1)} %get-tuple-element.86) | copy-start | bytes 6291460
  668.9 7.6 copy-start.155
  671.5 6.3 copy-start.159
  674.1 5.8 copy-start.157
  676.5 4.9 copy-start.79
  694.1 6.9 copy-start.109
  702.3 15.0 %copy-start.65 = (f32[128,1024]{1,0:T(8,128)}, f32[128,1024]{1,0:T(8,128)S(1)}, u32[]{:S(2)}) copy-start(f32[128,1024]{1,0:T(8,128)S(1)} %get-tuple-element.82) | copy-start | bytes 1572868
  705.4 9.3 copy-start.151
  707.2 5.9 copy-start.178
  732.1 5.2 copy-start.216
  732.2 5.2 copy-start.73
  812.9 6.3 copy-start.199
  844.2 6.5 copy-start.167
  844.2 7.2 copy-start.166
  844.2 8.0 copy-start.165
  845.6 7.4 copy-start.168
  845.6 8.1 copy-start.108
  845.6 8.8 copy-start.169
  847.3 7.8 copy-start.170
  849.0 6.8 copy-start.171
  850.7 5.8 copy-start.172
  851.5 5.8 copy-start.173
  852.2 5.8 copy-start.82
  860.8 7.0 copy-start.183
  860.8 7.7 copy-start.181
  861.1 10.6 copy-start.160
  862.1 14.4 %slice-start.2 = ((s8[8388608]{0:T(1024)(128)(4,1)}), s8[4194304]{0:T(1024)(128)(4,1)S(1)}, s32[]{:S(2)}) async-start(s8[8388608]{0:T(1024)(128)(4,1)} %bitcast.472), calls=%async_computation.5 | async-start | bytes 8388608
  864.0 12.5 slice-start
  867.0 7.4 copy-start.38
  867.0 9.4 slice-start.3
  871.5 5.2 slice-start.1
  876.7 9.2 copy-start.37
  1237.6 5.6 slice-start.4
  1248.4 15.3 %copy-start.141 = (f32[1,32,3072]{2,1,0:T(8,128)S(1)}, f32[1,32,3072]{2,1,0:T(8,128)}, u32[]{:S(2)}) copy-start(f32[1,32,3072]{2,1,0:T(8,128)} %stack_reshape.58) | copy-start | bytes 1179652
  1300.0 4.9 copy-start.227
  1300.0 4.9 copy-start.237
  1300.0 4.9 copy-start.238
  1315.0 5.7 copy-start.140
  (194 other events, 457.5 us)
Sparse Core Ops, SparseCore 0:
  32.8 157.4 reduce-scatter.1
  732.2 75.2 all-gather.1

commit v3 on v2

--- a/solution.py
+++ b/solution.py
@@ -39,17 +39,17 @@
 CODE_UNITS = 8
 
 
-def stepped(table, k):
-    rises = [i for i in range(1, len(table)) if table[i] > table[i - 1]]
-    return sum((k >= i).astype(jnp.int32) for i in rises)
-
-
-def sum_kernel(
-    Z, dec_x, dec_g, enc_x, enc_g, code_x, code_g, out_ref,
-    dec_xs, dec_gs, enc_xs, enc_gs, code_xs, code_gs, to_core,
-    own, from_core, held, from_x, from_y, all_x, all_y, kept, from_line,
-    load_sem, code_sem, core_send, core_recv, one_send, one_recv, two_send, two_recv, line_send, line_recv,
-):
+def sum_kernel(Z, *refs):
+    dec_x, refs = refs[:9], refs[9:]
+    dec_g, refs = refs[:11], refs[11:]
+    enc_x, refs = refs[:8], refs[8:]
+    enc_g, refs = refs[:11], refs[11:]
+    (
+        code_x, targets, code_g, look_g, out_ref,
+        dec_xs, dec_gs, dec_turned, enc_xs, enc_gs, enc_turned, code_xs, code_loaded, code_gs, to_core,
+        own, from_core, held, from_x, from_y, all_x, all_y, kept, from_line,
+        load_sem, code_sem, core_send, core_recv, one_send, one_recv, two_send, two_recv, line_send, line_recv,
+    ) = refs
     dec_units, enc_units = len(DEC_INPUTS), len(ENC_INPUTS)
     plain_units = dec_units + enc_units
     units = plain_units + CODE_UNITS
@@ -86,35 +86,32 @@
             src_ref=src, dst_ref=dst, send_sem=send, recv_sem=recv, device_id=device, device_id_type=MESH
         )
 
-    def loads(k):
-        slot, e = k % 2, k - dec_units
-        dec_place, enc_place = stepped(DEC_INPUTS, k), stepped(ENC_INPUTS, e)
-
-        def three(x, g, xs, gs, x_place, g_place):
-            return [
-                pltpu.make_async_copy(x.at[x_place, :, side], xs.at[slot, own_side], load_sem.at[own_side, slot])
-                for own_side, side in ((0, core), (1, 1 - core))
-            ] + [pltpu.make_async_copy(g.at[g_place], gs.at[slot], load_sem.at[2, slot])]
-
+    def pair(x, g, xs, gs, slot):
         return (
-            (k < dec_units, three(dec_x, dec_g, dec_xs, dec_gs, dec_place, jnp.minimum(k, 10))),
-            (
-                (k >= dec_units) & (k < plain_units),
-                three(enc_x, enc_g, enc_xs, enc_gs, enc_place, jnp.minimum(e, 10)),
-            ),
+            pltpu.make_async_copy(x, xs.at[slot], load_sem.at[0, slot]),
+            pltpu.make_async_copy(g, gs.at[slot], load_sem.at[1, slot]),
         )
 
     def start_loads(k):
-        for here, copies in loads(k):
-
-            @pl.when(here)
-            def _(copies=copies):
-                for copy in copies:
+        for i, place in enumerate(DEC_INPUTS):
+
+            @pl.when(k == i)
+            def _(i=i, place=place):
+                for copy in pair(dec_x[place], dec_g[min(i, 10)], dec_xs, dec_gs, i % 2):
                     copy.start()
 
+        for i, place in enumerate(ENC_INPUTS):
+
+            @pl.when(k == dec_units + i)
+            def _(i=i, place=place):
+                for copy in pair(enc_x[place], enc_g[min(i, 10)], enc_xs, enc_gs, (dec_units + i) % 2):
+                    copy.start()
+
+    code_rows = code_x.shape[0]
     code_loads = [
-        pltpu.make_async_copy(code_x, code_xs, code_sem.at[0]),
-        pltpu.make_async_copy(code_g, code_gs, code_sem.at[1]),
+        pltpu.make_async_copy(code_x, code_xs.at[pl.ds(0, code_rows)], code_sem.at[0]),
+        pltpu.make_async_copy(code_g, code_loaded.at[0], code_sem.at[1]),
+        pltpu.make_async_copy(look_g, code_loaded.at[1], code_sem.at[2]),
     ]
     for copy in code_loads:
         copy.start()
@@ -180,14 +177,52 @@
             down_copy(k, step).wait_recv()
             up_copy(k, step).wait_send()
 
-    def product(xs, gs, slot, side, into):
+    def turn(xs, slot, turned):
+        size = 256
+
+        def columns(i, carry):
+            part = xs[slot, :, pl.ds(pl.multiple_of(i * size, size), size)].T
+            count = size // (2 * turned.shape[2])
+            turned[pl.ds(i * count, count)] = part.reshape(count, *turned.shape[1:])
+            return carry
+
+        lax.fori_loop(0, xs.shape[2] // size, columns, 0)
+
+    def product(turned, gs, slot, side, into):
         def rows(block, carry):
-            value = xs[slot, side, pl.ds(block * Z, Z)].reshape(-1, xs.shape[-1])
+            value = turned[pl.ds(block * Z, Z), side].reshape(-1, turned.shape[-1])
             result = jnp.dot(value, gs[slot], preferred_element_type=F32).astype(BF)
             into[block] = result.reshape(into.shape[1:])
             return carry
 
         lax.fori_loop(0, 4, rows, 0)
+
+    def code_inputs():
+        for copy in code_loads:
+            copy.wait()
+        size = D // 4
+        for half_rows in range(2):
+
+            def turn_columns(i, carry, half_rows=half_rows):
+                part = code_loaded[half_rows, :, pl.ds(pl.multiple_of(i * size, size), size)].T
+                code_gs[i, :, :, pl.ds(half_rows * code_rows, code_rows)] = part.reshape(
+                    CODE_UNITS, size // CODE_UNITS, code_rows
+                )
+                return carry
+
+            lax.fori_loop(0, 4, turn_columns, 0)
+
+        width = 512
+
+        def hits(i, carry):
+            start = pl.multiple_of(i * width, width)
+            column = lax.broadcasted_iota(jnp.int32, (code_rows, width), 1) + i * width
+            code_xs[pl.ds(code_rows, code_rows), pl.ds(start, width)] = jnp.where(
+                targets[...] == column, 1.0, 0.0
+            ).astype(BF)
+            return carry
+
+        lax.fori_loop(0, VOCAB // width, hits, 0)
 
     def code_product(k, side, into):
         value = code_gs[:, k - plain_units].reshape(-1, code_gs.shape[-1])
@@ -203,21 +238,24 @@
 
     def begin(k):
         slot, o = k % 2, k % own_slots
-        for (here, copies), xs, gs in zip(loads(k), (dec_xs, enc_xs), (dec_gs, enc_gs)):
+        for here, x, g, xs, gs, turned in (
+            (k < dec_units, dec_x[0], dec_g[0], dec_xs, dec_gs, dec_turned),
+            ((k >= dec_units) & (k < plain_units), enc_x[0], enc_g[0], enc_xs, enc_gs, enc_turned),
+        ):
 
             @pl.when(here)
-            def _(copies=copies, xs=xs, gs=gs):
-                for copy in copies:
+            def _(x=x, g=g, xs=xs, gs=gs, turned=turned):
+                for copy in pair(x, g, xs, gs, slot):
                     copy.wait()
                 start_loads(k + 1)
-                product(xs, gs, slot, 1, to_core.at[o])
+                turn(xs, slot, turned)
+                product(turned, gs, slot, 1 - core, to_core.at[o])
                 core_copy(k).start()
-                product(xs, gs, slot, 0, own.at[o])
-
-        @pl.when(k == plain_units)
+                product(turned, gs, slot, core, own.at[o])
+
+        @pl.when(k == dec_units)
         def _():
-            for copy in code_loads:
-                copy.wait()
+            code_inputs()
 
         @pl.when(k >= plain_units)
         def _():
@@ -306,15 +344,17 @@
     lax.fori_loop(0, units + (len(stages) - 1) * LAG, loop_step, 0)
 
 
-def sum_products(dec_x, dec_g, enc_x, enc_g, code_x, code_g, call_id):
+def sum_products(dec_x, dec_g, enc_x, enc_g, code_x, targets, code_g, look_g, call_id):
     dp_size, fsdp_size = lax.axis_size("dp"), lax.axis_size("fsdp")
     devices, Z = dp_size * fsdp_size, fsdp_size // 2
     m = D // devices
     if dp_size != 4 or Z != 4 or m % 32:
-        products = [matmul(dec_x[i], dec_g[min(k, 10)]) for k, i in enumerate(DEC_INPUTS)]
-        products += [matmul(enc_x[i], enc_g[min(k, 10)]) for k, i in enumerate(ENC_INPUTS)]
+        products = [across(dec_x[i], dec_g[min(k, 10)]) for k, i in enumerate(DEC_INPUTS)]
+        products += [across(enc_x[i], enc_g[min(k, 10)]) for k, i in enumerate(ENC_INPUTS)]
         plain = jnp.stack(products).astype(BF).reshape(len(products), devices, m, D)
-        code = matmul(code_g, code_x).astype(BF).reshape(dp_size, D // dp_size, fsdp_size, VOCAB // fsdp_size)
+        hit = (targets[:, None] == jnp.arange(VOCAB)[None, :]).astype(BF)
+        code = across(jnp.concatenate([code_g, look_g]), jnp.concatenate([code_x, hit])).astype(BF)
+        code = code.reshape(dp_size, D // dp_size, fsdp_size, VOCAB // fsdp_size)
         code = code.transpose(0, 2, 1, 3).reshape(devices, D // dp_size, VOCAB // fsdp_size)
         plain = lax.psum_scatter(plain, AXES, scatter_dimension=1, tiled=True)
         code = lax.psum_scatter(code, AXES, scatter_dimension=0, tiled=True)
@@ -322,20 +362,24 @@
     n, units = D, len(DEC_INPUTS) + len(ENC_INPUTS) + CODE_UNITS
     depth, half = 2 * LAG, Z // 2
     own_slots, held_slots, kept_slots = LAG + 1, 2 * LAG + 1, Z * LAG + 1
-    dec_rows, enc_rows, code_rows = dec_x.shape[2], enc_x.shape[2], code_g.shape[1]
+    dec_rows, enc_rows, code_rows = dec_x[0].shape[0], enc_x[0].shape[0], code_x.shape[0]
     dma = pltpu.SemaphoreType.DMA
+    whole = pl.BlockSpec(memory_space=pl.ANY)
     out = pl.pallas_call(
         partial(sum_kernel, Z),
         out_shape=jax.ShapeDtypeStruct((units, m, n), F32),
-        in_specs=[pl.BlockSpec(memory_space=pl.ANY)] * 6,
+        in_specs=[whole] * 40 + [pl.BlockSpec(memory_space=pltpu.VMEM)] + [whole] * 2,
         out_specs=pl.BlockSpec(memory_space=pltpu.VMEM),
         scratch_shapes=[
-            pltpu.VMEM((2, 2, 4 * Z, m, dec_rows), BF),
             pltpu.VMEM((2, dec_rows, n), BF),
-            pltpu.VMEM((2, 2, 4 * Z, m, enc_rows), BF),
+            pltpu.VMEM((2, dec_rows, n), BF),
+            pltpu.VMEM((4 * Z, 2, m, dec_rows), BF),
             pltpu.VMEM((2, enc_rows, n), BF),
-            pltpu.VMEM(code_x.shape, BF),
-            pltpu.VMEM((4, CODE_UNITS, m, code_rows), BF),
+            pltpu.VMEM((2, enc_rows, n), BF),
+            pltpu.VMEM((4 * Z, 2, m, enc_rows), BF),
+            pltpu.VMEM((2 * code_rows, VOCAB), BF),
+            pltpu.VMEM((2, code_rows, n), BF),
+            pltpu.VMEM((4, CODE_UNITS, m, 2 * code_rows), BF),
             pltpu.VMEM((own_slots, 4, Z, m, n), BF),
             pltpu.VMEM((own_slots, 4, Z, m, n), BF),
             pltpu.VMEM((depth, 4, Z, m, n), BF),
@@ -346,8 +390,8 @@
             pltpu.VMEM((depth, Z, m, n), BF),
             pltpu.VMEM((kept_slots, Z, m, n), BF),
             pltpu.VMEM((2, Z - 1, depth, m, n), BF),
-            dma((3, 2)),
-            dma((2,)),
+            dma((2, 2)),
+            dma((3,)),
             dma((depth,)),
             dma((depth,)),
             dma((2, depth)),
@@ -360,14 +404,7 @@
         compiler_params=pltpu.CompilerParams(
             collective_id=call_id, has_side_effects=True, vmem_limit_bytes=60 << 20
         ),
-    )(
-        dec_x.reshape(-1, 4 * Z, 2, m, dec_rows),
-        dec_g,
-        enc_x.reshape(-1, 4 * Z, 2, m, enc_rows),
-        enc_g,
-        code_x,
-        code_g.reshape(4, CODE_UNITS, m, code_rows),
-    )
+    )(*dec_x, *dec_g, *enc_x, *enc_g, code_x, targets[:, None], code_g, look_g)
     return out[:-CODE_UNITS], out[-CODE_UNITS:].reshape(-1, n)
 
 
@@ -587,7 +624,7 @@
             jax.ShapeDtypeStruct((Z, 2, table.shape[0], 4 * table.shape[1]), BF),
             jax.ShapeDtypeStruct((count, 4, Z, 2, m, n), BF),
         ),
-        in_specs=[pl.BlockSpec(memory_space=pl.ANY)] * 2,
+        in_specs=[pl.BlockSpec(memory_space=pltpu.VMEM)] * 2,
         out_specs=[pl.BlockSpec(memory_space=pl.ANY)] * 2,
         scratch_shapes=[
             dma((2,)),
@@ -956,25 +993,10 @@
 
     grad_looked = grad_image.reshape(image_count, IMG_LEN, D)[:, 1:] * scale_in
     grad_looked = jnp.pad(grad_looked, ((0, 0), (0, 1), (0, 0))).reshape(-1, D).astype(BF)
-    code_x = jnp.concatenate([grad_logits, hit.astype(BF)])
-    code_g = jnp.concatenate([final_out, grad_looked]).T
-
-    def inputs(values):
-        return jnp.stack([value.T for value in values])
-
-    def gradients_of(values):
-        return jnp.stack(values)
-
     enc_x, enc_g = enc_parts
     dec_x, dec_g, memory_g = dec_parts
     plain_sum, code_sum = sum_products(
-        inputs(dec_x),
-        gradients_of(dec_g),
-        inputs([memory] + enc_x),
-        gradients_of(memory_g + enc_g),
-        code_x,
-        code_g,
-        1,
+        dec_x, dec_g, [memory] + enc_x, memory_g + enc_g, grad_logits, targets, final_out, grad_looked, 1
     )
     code_grad = code_sum.T
     dec_sum, enc_sum = plain_sum[:14], plain_sum[14:]

time: 1340 us -> 1220 us (0.910)
  local copies, waits for them, and re-layouts: 282 us -> 196 us
  Pallas kernels: 744 us -> 724 us
  other arithmetic: 108 us -> 91.4 us
    unnamed x566 -> x460, local copies, waits for them, and re-layouts: 89.5 us -> 54.2 us
    another operation x15 -> x1, local copies, waits for them, and re-layouts: 61.4 us -> 26.6 us  [layer_forward(): zip(hidden, ffn_down)]
    pallas_call x1, Pallas kernels: 376 us -> 351 us  [spread(): pl.pallas_call(partial(spread_kernel, tables, count, Z), out_shape=(jax.S...]
  transfers between devices with their start and end apart: 2 -> 2, of which waited for: 0 -> 0; matrix products, arithmetic and copies ran while one was open for 23% -> 18% of each run, Pallas kernels for 54% -> 58%
where the time goes in v3:
time: 1220 us; the launch traced here: 1210 us
  Pallas kernels  724 us (59%)
  local copies, waits for them, and re-layouts  196 us (16%)
  matrix products  171 us (14%)
  other arithmetic  91.4 us (7%)
  between operations  24 us (2%)
    pallas_call x1, Pallas kernels, spread(): pl.pallas_call(partial(spread_kernel, tables, count, Z), out_shape=(jax.S...  351 us
    pallas_call x1, Pallas kernels, sum_products(): pl.pallas_call(partial(sum_kernel, Z), out_shape=jax.ShapeDtypeStruct((un...  336 us
    dot_general x30, matrix products, matmul(): return jnp.dot(first_op, second_op, preferred_element_type=jnp.float32)  69.6 us
    dot_general x29, matrix products, against(): lax.dot_general(first_op, second_op, (((1,), (1,)), ((), ())), preferred_...  59.8 us
    unnamed x460, local copies, waits for them, and re-layouts  54.2 us
    pallas_call x3, Pallas kernels, exchange(): pl.pallas_call(partial(exchange_kernel, size, inner), out_shape=jax.Shape...  36.4 us
    another operation x1, local copies, waits for them, and re-layouts, layer_forward(): zip(hidden, ffn_down)  26.6 us
  transfers between devices with their start and end apart: 2, of which 0 were waited for; matrix products, arithmetic and copies ran while one was open for 18% of the time, Pallas kernels for 58%

profile of v3, /device:TPU:0, one launch (start us, length us, event | category | flops | bytes accessed | tf_op | source)
XLA Modules:
  0.0 1206.2 jit_solution(9835684225909548526)
XLA Ops:
  9.4 13.3 %shard_map.416 = f32[32,8,128]{2,1,0:T(8,128)} custom-call(f32[32,8,128]{2,1,0:T(8,128)} %broadcast_in_dim.91.in_ref), custom_call_target="tpu_custom_call" | custom-call | tf_op jit(solution)/shard_map/pallas_call | solution.py:680
  24.2 8.4 fusion.7
  38.4 1.9 reshape.755
  51.9 351.0 %shard_map.417 = (bf16[4,2,1024,1024]{3,2,1,0:T(8,128)(2,1)}, bf16[28,4,4,2,32,1024]{5,4,3,2,1,0:T(8,128)(2,1)}) custom-call(bf16[1024,256]{1,0:T(8,128)(2,1)} %convert_element_type.300.table_ref, bf16[28,32,1024]{2,1,0:T(8,128)(2,1)} %copy-done.105), custom_call_target="tpu_custom_call" | custom-call | tf_op jit(solution)/shard_map/pallas_call | solution.py:621
  402.9 10.7 gather_fusion
  413.5 1.9 fusion.106
  418.0 13.5 %fusion.154 = (bf16[1,4,4,2,32,1024]{5,4,3,2,1,0:T(8,128)(2,1)}, bf16[1,4,4,2,32,1024]{5,4,3,2,1,0:T(8,128)(2,1)}, bf16[1,4,4,2,32,1024]{5,4,3,2,1,0:T(8,128)(2,...) fusion(bf16[28,4,4,2,32,1024]{5,4,3,2,1,0:T(8,128)(2,1)} %get-t, ...), kind=kLoop, calls=%fused_computation.387 | loop fusion | bytes 37748736 | tf_op jit(solution)/shard_map/slice | solution.py:785
  432.8 2.2 convolution_convert_fusion.7
  437.7 4.1 convolution_convert_fusion.8
  444.4 3.2 convolution_convert_fusion.6
  448.9 10.4 reshape.765
  459.4 6.6 fusion.73
  466.0 9.3 fusion.162
  476.4 2.4 copy-done.8
  482.3 3.3 fusion.163
  491.9 26.6 %fusion.153 = (bf16[1,4,4,2,32,1024]{5,4,3,2,1,0:T(8,128)(2,1)}, bf16[1,4,4,2,32,1024]{5,4,3,2,1,0:T(8,128)(2,1)}, bf16[1,4,4,2,32,1024]{5,4,3,2,1,0:T(8,128)(2,...) fusion(bf16[28,4,4,2,32,1024]{5,4,3,2,1,0:T(8,128)(2,1)} %get-t, ...), kind=kLoop, calls=%fused_computation.386 | loop fusion | bytes 79691776 | tf_op jit(solution)/shard_map/unstack | solution.py:799
  521.8 2.2 convolution_convert_fusion.17
  525.6 2.6 fusion.160
  547.3 4.9 fusion.165
  552.2 3.0 divide_convert_fusion.1
  555.7 2.2 copy-done.27
  561.6 3.3 multiply_convert_fusion.6
  565.0 2.9 multiply_convert_fusion.7
  567.9 2.9 multiply_convert_fusion.8
  570.8 2.9 multiply_convert_fusion.9
  582.1 16.2 %fusion.168 = (f32[512]{0:T(512)S(1)}, f32[512,8192]{1,0:T(8,128)}) fusion(bf16[512,1024]{1,0:T(8,128)(2,1)} %multiply_convert_fusion.5.refs_41_, bf16[8192,1024]{1,0:T(8,128)(2,1)} %bitcast.440), kind=kOutput, calls=%fused_computation.401 | convolution fusion | flops 8594128896 | bytes 34605056 | tf_op jit(solution)/shard_map/dot_general | solution.py:724
  598.3 10.3 multiply_reduce_fusion
  609.3 5.2 multiply_convert_fusion.refs_39_
  614.5 16.1 %multiply_reduce_fusion.2 = (f32[1024]{0:T(1024)S(1)}, f32[512]{0:T(512)S(1)}, f32[512,1024]{1,0:T(8,128)S(1)}) fusion(f32[512,1024]{1,0:T(8,128)S(1)} %get-tuple-element.178, f32[512]{0:T(512)S(1)} %fusion.121, f32[512]{0:T(512)S(1)} %broadcast_multiply_fusion, f32[1024]{0:T(1024)S(1)} %mul.1269, bf16[512,8192]{1,0:T(8,128)(2,1)S(1)} %multiply_convert_fusion.refs_39_, ...), kind=kOutput, calls=%fused_computation.83 | convolution fusion | flops 8593602560 | bytes 29374464 | tf_op jit(solution)/shard_map/dot_general | solution.py:714
  633.5 2.4 fusion.44.refs_18_
  635.9 2.4 fusion.37.refs_17_
  640.9 2.4 fusion.23.refs_15_
  645.9 2.4 fusion.30.refs_16_
  651.0 2.0 multiply_reduce_fusion.3
  656.5 2.3 convolution_convert_fusion.4
  658.8 2.4 copy.110
  661.2 2.2 fusion.9
  705.9 2.3 multiply_convert_fusion.4
  709.5 3.5 multiply_reduce_fusion.4
  719.0 3.7 fusion.51
  726.4 4.3 fusion.4
  739.7 3.1 fusion.178
  745.7 3.2 multiply_reduce_fusion.1
  750.9 13.2 %shard_map.418 = f32[32,8,128]{2,1,0:T(8,128)} custom-call(f32[32,8,128]{2,1,0:T(8,128)} %bitcast.517), custom_call_target="tpu_custom_call" | custom-call | tf_op jit(solution)/shard_map/pallas_call | solution.py:680
  765.8 3.7 fusion.144
  771.2 336.5 %shard_map.419 = f32[36,32,1024]{2,1,0:T(8,128)} custom-call(bf16[512,1024]{1,0:T(8,128)(2,1)} %get-tuple-element.131.refs_0_, bf16[512,1024]{1,0:T(8,128)(2,1)} %copy.130.refs_1_, bf16[512,1024]{1,0:T(8,128)(2,1)} %copy-done.70, bf16[512,1024]{1,0:T(8,128)(2,1)} %copy.131.refs_3_, bf16[512,1024]{1,0:T(8,128)(2,1)} %copy-done.71, ...), custom_call_target="tpu_custom_call" | custom-call | tf_op jit(solution)/shard_map/pallas_call | solution.py:368
  1114.7 2.7 fusion.155
  1117.4 2.0 reshape.795
  1119.4 3.1 copy.146
  1122.5 4.4 stack_reshape.24
  1126.9 2.0 reshape.796
  1128.9 3.1 copy.147
  1132.0 4.5 stack_reshape.25
  1146.3 2.1 multiply_reduce_fusion.15
  1148.4 9.8 multiply_reduce_fusion.13
  1160.2 9.9 shard_map.420
  1172.4 2.4 slice_multiply_fusion.1
  1174.8 2.5 copy.148
  1177.4 4.4 multiply_subtract_fusion.1
  1183.8 2.3 multiply_subtract_fusion.4
  1187.1 2.3 multiply_subtract_fusion.3
  1189.4 1.9 multiply_subtract_fusion.6
  1191.4 4.1 multiply_subtract_fusion
  1195.5 2.2 multiply_subtract_fusion.2
  (684 shorter events, 181.3 us)
Async XLA Ops:
  7.2 38.4 %copy-start = (s32[2]{0:T(128)S(1)}, s32[2]{0:T(128)}, u32[]{:S(2)}) copy-start(s32[2]{0:T(128)} %param.28) | copy-start | bytes 28
  7.2 511.4 %reduce-scatter.2.cloned.1.call-start = ((), (), s32[]{:S(2)}) async-start(), calls=%async_computation.1 | async-start | bytes 8650752 | tf_op jit(solution)/shard_map/reduce_scatter | solution.py:939
  32.7 1115.7 %all-gather.2.cloned.1.call-start = ((), (), s32[]{:S(2)}) async-start(), calls=%async_computation.2 | async-start | bytes 8650752 | tf_op jit(solution)/shard_map/all_gather | solution.py:991
  33.9 486.8 %copy-start.172 = (f32[1024]{0:T(1024)}, f32[1024]{0:T(1024)S(1)}, u32[]{:S(2)}) copy-start(f32[1024]{0:T(1024)S(1)} %mul.1190) | copy-start | bytes 12292
  38.4 3.7 copy-start.164
  45.6 485.6 %copy-start.174 = (f32[1024]{0:T(1024)}, f32[1024]{0:T(1024)S(1)}, u32[]{:S(2)}) copy-start(f32[1024]{0:T(1024)S(1)} %mul.1217) | copy-start | bytes 12292
  45.8 371.9 %copy-start.170 = (f32[1024]{0:T(1024)}, f32[1024]{0:T(1024)S(1)}, u32[]{:S(2)}) copy-start(f32[1024]{0:T(1024)S(1)} %mul.1203) | copy-start | bytes 12292
  416.1 66.1 %copy-start.5 = (f32[2,256,1024]{2,1,0:T(8,128)}, f32[2,256,1024]{2,1,0:T(8,128)S(1)}, u32[]{:S(2)}) copy-start(f32[2,256,1024]{2,1,0:T(8,128)S(1)} %get-tuple-element.90) | copy-start | bytes 6291460
  418.0 13.6 %copy-start.155 = (bf16[2,256,1024]{2,1,0:T(8,128)(2,1)}, bf16[2,256,1024]{2,1,0:T(8,128)(2,1)S(1)}, u32[]{:S(2)}) copy-start(bf16[2,256,1024]{2,1,0:T(8,128)(2,1)S(1)} %multiply_convert_fusion.12) | copy-start | bytes 3145732
  459.4 19.3 %copy-start.35 = (bf16[2,256,16,64]{1,0,3,2:T(2,128)(2,1)}, bf16[2,256,16,64]{1,0,3,2:T(2,128)(2,1)S(1)}, u32[]{:S(2)}) copy-start(bf16[2,256,16,64]{1,0,3,2:T(2,128)(2,1)S(1)} %reshape.765) | copy-start | bytes 3145732
  482.3 3.7 copy-start.177
  519.9 10.5 copy-start.24
  520.8 4.1 copy-start.62
  521.8 3.8 copy-start.156
  525.6 4.3 copy-start.98
  525.6 4.8 copy-start.18
  531.3 5.0 copy-start.139
  533.2 4.4 copy-start.141
  534.5 4.2 copy-start.142
  542.2 4.2 copy-start.33
  542.4 4.0 copy-start.13
  542.6 4.3 copy-start.69
  547.0 8.2 copy-start.103
  555.2 4.1 copy-start.9
  560.0 10.8 copy-start.71
  565.0 13.6 %copy-start.72 = (bf16[512,1024]{1,0:T(8,128)(2,1)}, bf16[512,1024]{1,0:T(8,128)(2,1)S(1)}, u32[]{:S(2)}) copy-start(bf16[512,1024]{1,0:T(8,128)(2,1)S(1)} %get-tuple-element.175.refs_8_) | copy-start | bytes 3145732
  567.9 5.8 copy-start.149
  570.8 4.2 copy-start.150
  598.3 11.0 copy-start.4
  614.5 16.1 %copy-start.7 = (bf16[512,8192]{1,0:T(8,128)(2,1)}, bf16[512,8192]{1,0:T(8,128)(2,1)S(1)}, u32[]{:S(2)}) copy-start(bf16[512,8192]{1,0:T(8,128)(2,1)S(1)} %multiply_convert_fusion.refs_39_) | copy-start | bytes 25165828
  631.6 13.0 %copy-start.82 = (bf16[512,1024]{1,0:T(8,128)(2,1)}, bf16[512,1024]{1,0:T(8,128)(2,1)S(1)}, u32[]{:S(2)}) copy-start(bf16[512,1024]{1,0:T(8,128)(2,1)S(1)} %add_convert_fusion.refs_19_) | copy-start | bytes 3145732
  635.9 14.8 %copy-start.73 = (bf16[512,1024]{1,0:T(8,128)(2,1)}, bf16[512,1024]{1,0:T(8,128)(2,1)S(1)}, u32[]{:S(2)}) copy-start(bf16[512,1024]{1,0:T(8,128)(2,1)S(1)} %fusion.44.refs_18_) | copy-start | bytes 3145732
  656.5 4.7 copy-start.104
  664.3 4.6 copy-start.96
  670.3 7.4 copy-start.140
  684.5 4.0 copy-start.61
  684.6 4.0 copy-start.99
  698.2 3.9 copy-start.97
  719.0 5.0 copy-start.36
  726.4 4.3 copy-start.37
  765.1 379.9 %copy-start.176 = (f32[32,32]{1,0:T(8,128)}, f32[32,32]{1,0:T(8,128)S(1)}, u32[]{:S(2)}) copy-start(f32[32,32]{1,0:T(8,128)S(1)} %slice.321) | copy-start | bytes 12292
  765.7 3.7 copy-start.21
  765.7 3.7 copy-start.31
  1117.4 26.1 %copy-start.65 = (f32[4,32,1024]{2,1,0:T(8,128)}, f32[4,32,1024]{2,1,0:T(8,128)S(1)}, u32[]{:S(2)}) copy-start(f32[4,32,1024]{2,1,0:T(8,128)S(1)} %get-tuple-element.121) | copy-start | bytes 1572868
  1117.4 26.1 %copy-start.67 = (f32[4,32,1024]{2,1,0:T(8,128)}, f32[4,32,1024]{2,1,0:T(8,128)S(1)}, u32[]{:S(2)}) copy-start(f32[4,32,1024]{2,1,0:T(8,128)S(1)} %get-tuple-element.122) | copy-start | bytes 1572868
  1132.0 4.5 copy-start.129
  1132.0 4.5 copy-start.130
  1140.9 7.5 copy-start.191
  1172.4 4.9 copy-start.64
  1177.3 4.4 copy-start.132
  1177.3 4.4 copy-start.134
  1177.3 4.4 copy-start.136
  1177.3 4.4 copy-start.166
  1177.4 4.4 copy-start.167
  1177.4 5.7 copy-start.161
  1183.8 7.6 copy-start.128
  1187.1 4.3 copy-start.125
  1187.1 4.3 copy-start.126
  1187.1 4.3 copy-start.127
  1191.4 4.1 copy-start.77
  1191.4 4.1 copy-start.79
  1191.4 4.1 copy-start.147
  1191.4 4.1 copy-start.148
  1191.4 6.3 copy-start.1
  (156 other events, 338.2 us)
Sparse Core Ops, SparseCore 0:
  32.8 173.0 reduce-scatter.1
  697.0 78.4 all-gather.1

commit v4 on v3

--- a/solution.py
+++ b/solution.py
@@ -692,6 +692,152 @@
     return jnp.broadcast_to(padded, (count, 8, 128))
 
 
+def swap_groups(parts):
+    group = lax.broadcasted_iota(jnp.int32, parts[0].shape, 1) // 32
+    results = []
+    for i in range(4):
+        total = parts[i]
+        for j in range(4):
+            if j != i:
+                turned = pltpu.roll(parts[j], (32 * (j - i)) % 128, 1)
+                total = jnp.where(group == j, turned, total)
+        results.append(total)
+    return results
+
+
+def norm_kernel(size, inner, plain, code, text, gains, norm_out, squares, gathered, sum_scratch, send_sem, recv_sem):
+    rows = plain.shape[1]
+    text_rows = [(start, min(rows, text.shape[0] - start)) for start in range(0, text.shape[0], rows)]
+
+    sum_scratch[...] = jnp.zeros_like(sum_scratch)
+
+    def square(k, carry):
+        sum_scratch[...] += plain[k] * plain[k]
+        return carry
+
+    lax.fori_loop(0, plain.shape[0], square, 0)
+
+    def square_code(k, carry):
+        part = code[pl.ds(pl.multiple_of(k * rows, rows), rows), :]
+        sum_scratch[...] += part * part
+        return carry
+
+    lax.fori_loop(0, code.shape[0] // rows, square_code, 0)
+    for start, count in text_rows:
+        part = text[pl.ds(start, count), :]
+        sum_scratch[pl.ds(0, count), :] += part * part
+    own = jnp.sum(sum_scratch[...]) + jnp.sum(gains[...] * gains[...])
+    squares[...] = jnp.full(squares.shape, own)
+
+    me = lax.axis_index("dp") * inner + lax.axis_index("fsdp")
+
+    def peer(i):
+        other = lax.rem(me + i, size)
+        return (other // inner, lax.rem(other, inner))
+
+    def copy(i):
+        return pltpu.make_async_remote_copy(
+            src_ref=squares, dst_ref=gathered.at[me], send_sem=send_sem.at[i],
+            recv_sem=recv_sem.at[i], device_id=peer(i), device_id_type=MESH,
+        )
+
+    barrier = pltpu.get_barrier_semaphore()
+
+    def greet(i, carry):
+        pl.semaphore_signal(barrier, inc=1, device_id=peer(i), device_id_type=MESH)
+        return carry
+
+    def begin(i, carry):
+        copy(i).start()
+        return carry
+
+    def end(i, carry):
+        copy(i).wait()
+        return carry
+
+    lax.fori_loop(1, size, greet, 0)
+    gathered[me] = squares[...]
+    pl.semaphore_wait(barrier, size - 1)
+    lax.fori_loop(1, size, begin, 0)
+    lax.fori_loop(1, size, end, 0)
+    norm = jnp.sqrt(lax.fori_loop(0, size, lambda i, total: total + gathered[i], jnp.zeros_like(squares)))
+    norm_out[...] = norm
+
+
+def update_kernel(*refs):
+    norm, plain, code, text, gains, *refs = refs
+    weights, refs = refs[:7], refs[7:]
+    firsts, refs = refs[:7], refs[7:]
+    seconds, refs = refs[:7], refs[7:]
+    new_weights, refs = refs[:7], refs[7:]
+    new_firsts, new_seconds = refs[:7], refs[7:]
+    rows = plain.shape[1]
+    text_rows = [(start, min(rows, text.shape[0] - start)) for start in range(0, text.shape[0], rows)]
+    factor = (CLIP_NORM / jnp.maximum(norm[...], CLIP_NORM))[:1, :1]
+
+    def step(which, place, gradient):
+        updated = adam_step(
+            weights[which][place], firsts[which][place], seconds[which][place],
+            gradient * factor, STEP_RATES[which],
+        )
+        for out, value in zip((new_weights, new_firsts, new_seconds), updated):
+            out[which][place] = value
+
+    enc = len(DEC_INPUTS)
+    every = slice(None)
+    for layer, units in enumerate(((enc + 2, enc + 3, enc + 4), (0, 1, 2), (4, enc, enc + 1))):
+        for i, unit in enumerate(units):
+            step(0, (layer, every, pl.ds(i * D, D)), plain[unit])
+    for layer, unit in enumerate((enc + 5, 3, 5)):
+        step(1, (layer,), plain[unit])
+    for layer, first in enumerate((enc + 6, 6)):
+        for g in range(8):
+            parts = [plain[first + q, :, pl.ds(128 * g, 128)] for q in range(4)]
+            for j, part in enumerate(swap_groups(parts)):
+                step(2, (layer, every, pl.ds(128 * (4 * g + j), 128)), part)
+    for layer, first in enumerate((enc + 10, 10)):
+        for q in range(4):
+            step(3, (layer, pl.ds(q * rows, rows), every), plain[first + q])
+    step(4, (every, every), gains[...])
+    for start, count in text_rows:
+        step(5, (pl.ds(start, count), every), text[pl.ds(start, count), :])
+    columns = 256
+    for i in range(code.shape[1] // columns):
+        step(6, (pl.ds(i * columns, columns), every), code[:, pl.ds(i * columns, columns)].T)
+
+
+def update(plain, code, text, gains, weights, firsts, seconds, call_id):
+    inner = lax.axis_size("fsdp")
+    size = lax.axis_size("dp") * inner
+    shapes = [jax.ShapeDtypeStruct(weight.shape, F32) for weight in weights]
+    in_vmem = pl.BlockSpec(memory_space=pltpu.VMEM)
+    dma = pltpu.SemaphoreType.DMA
+    norm = pl.pallas_call(
+        partial(norm_kernel, size, inner),
+        out_shape=jax.ShapeDtypeStruct((8, 128), F32),
+        in_specs=[in_vmem] * 4,
+        out_specs=in_vmem,
+        scratch_shapes=[
+            pltpu.VMEM((8, 128), F32),
+            pltpu.VMEM((size, 8, 128), F32),
+            pltpu.VMEM(plain.shape[1:], F32),
+            dma((size,)),
+            dma((size,)),
+        ],
+        compiler_params=pltpu.CompilerParams(
+            collective_id=call_id, has_side_effects=True, vmem_limit_bytes=32 << 20
+        ),
+    )(plain, code, text, gains)
+    outs = pl.pallas_call(
+        update_kernel,
+        out_shape=shapes * 3,
+        in_specs=[in_vmem] * 26,
+        out_specs=[in_vmem] * 21,
+        compiler_params=pltpu.CompilerParams(vmem_limit_bytes=60 << 20),
+    )(norm, plain, code, text, gains, *weights, *firsts, *seconds)
+    return norm[0, 0], list(zip(outs[:7], outs[7:14], outs[14:]))
+
+
 def layer_norm(stream, gain):
     centred = stream - jnp.mean(stream, axis=-1, keepdims=True)
     return centred * lax.rsqrt(jnp.mean(centred * centred, axis=-1, keepdims=True) + 1e-05) * gain
@@ -998,33 +1144,12 @@
     plain_sum, code_sum = sum_products(
         dec_x, dec_g, [memory] + enc_x, memory_g + enc_g, grad_logits, targets, final_out, grad_looked, 1
     )
-    code_grad = code_sum.T
-    dec_sum, enc_sum = plain_sum[:14], plain_sum[14:]
-
     gain_blocks = gain_part.reshape(7, devices, rows).transpose(1, 0, 2).reshape(devices, 7 * rows)
     gain_blocks = jnp.concatenate([gain_blocks, jnp.full((devices, 1), loss_part)], axis=1)
     gain_blocks = jnp.pad(gain_blocks, ((0, 0), (0, 1024 - gain_blocks.shape[1])))
     small_sum = jnp.sum(exchange(gain_blocks.reshape(devices, 8, 128), 5), axis=0).reshape(-1)
     loss_sum = small_sum[7 * rows]
     gains_grad = small_sum[: 7 * rows].reshape(7, rows)
-    gradients = (
-        jnp.stack(
-            [
-                from_column_units(part)
-                for part in (enc_sum[2:5], dec_sum[:3], jnp.concatenate([dec_sum[4:5], enc_sum[:2]]))
-            ]
-        ),
-        jnp.stack([enc_sum[5], dec_sum[3], dec_sum[5]]),
-        jnp.stack([from_hidden_units(part, devices) for part in (enc_sum[6:10], dec_sum[6:10])]),
-        jnp.stack([part.reshape(-1, D) for part in (enc_sum[10:], dec_sum[10:])]),
-        gains_grad,
-        text_grad,
-        code_grad,
-    )
-    square_part = sum((jnp.sum(gradient * gradient) for gradient in gradients))
-    squares = exchange(tiles(square_part[None], devices), 6)[:, 0, 0]
-    grad_norm = jnp.sqrt(jnp.sum(squares))
-    factor = CLIP_NORM / jnp.maximum(grad_norm, CLIP_NORM)
     params = (mix_in, mix_out, ffn_up, ffn_down, norm_gains, text_table, code_table)
     firsts = (
         mix_in_first,
@@ -1044,16 +1169,40 @@
         text_second,
         code_second,
     )
-    updated = [
-        adam_step(
-            params[index],
-            firsts[index],
-            seconds[index],
-            gradients[index] * factor,
-            STEP_RATES[index],
-        )
-        for index in range(7)
-    ]
+    if rows == 32:
+        grad_norm, updated = update(
+            plain_sum, code_sum, text_grad, gains_grad, params, firsts, seconds, 6
+        )
+    else:
+        dec_sum, enc_sum = plain_sum[:14], plain_sum[14:]
+        gradients = (
+            jnp.stack(
+                [
+                    from_column_units(part)
+                    for part in (enc_sum[2:5], dec_sum[:3], jnp.concatenate([dec_sum[4:5], enc_sum[:2]]))
+                ]
+            ),
+            jnp.stack([enc_sum[5], dec_sum[3], dec_sum[5]]),
+            jnp.stack([from_hidden_units(part, devices) for part in (enc_sum[6:10], dec_sum[6:10])]),
+            jnp.stack([part.reshape(-1, D) for part in (enc_sum[10:], dec_sum[10:])]),
+            gains_grad,
+            text_grad,
+            code_sum.T,
+        )
+        square_part = sum((jnp.sum(gradient * gradient) for gradient in gradients))
+        squares = exchange(tiles(square_part[None], devices), 6)[:, 0, 0]
+        grad_norm = jnp.sqrt(jnp.sum(squares))
+        factor = CLIP_NORM / jnp.maximum(grad_norm, CLIP_NORM)
+        updated = [
+            adam_step(
+                params[index],
+                firsts[index],
+                seconds[index],
+                gradients[index] * factor,
+                STEP_RATES[index],
+            )
+            for index in range(7)
+        ]
     return (
         loss_sum,
         grad_norm,

time: 1220 us -> 1160 us (0.951)
  local copies, waits for them, and re-layouts: 196 us -> 161 us
  other arithmetic: 91.4 us -> 59.9 us
  Pallas kernels: 724 us -> 743 us
    pallas_call x0 -> x2, Pallas kernels: none -> 30.3 us  [the longest x1 19.9 us: update(): pl.pallas_call(update_kernel, out_shape=shapes * 3, in_specs=[in_vmem] *...]
    sub x7 -> x0, other arithmetic: 18.4 us -> none  [adam_step(): weight - rate * (first_hat / (jnp.sqrt(second_hat) + ADAM_EPS) + WEIGHT_D...]
    another operation x7 -> x0, local copies, waits for them, and re-layouts: 14.1 us -> none  [the longest x3 9.96 us: on_device(): jnp.stack([from_hidden_units(part, devices) for part in (enc_sum[6:10], d...]
    pallas_call x3 -> x2, Pallas kernels: 36.4 us -> 24.1 us  [exchange(): pl.pallas_call(partial(exchange_kernel, size, inner), out_shape=jax.Shape...]
    unnamed x460 -> x403, local copies, waits for them, and re-layouts: 54.2 us -> 52.7 us
  transfers between devices with their start and end apart: 2 -> 2, of which waited for: 0 -> 0; matrix products, arithmetic and copies ran while one was open for 18% -> 16% of each run, Pallas kernels for 58% -> 61%
where the time goes in v4:
time: 1160 us; the launch traced here: 1150 us
  Pallas kernels  743 us (64%)
  matrix products  168 us (14%)
  local copies, waits for them, and re-layouts  161 us (14%)
  other arithmetic  59.9 us (5%)
  between operations  17.1 us (1%)
    pallas_call x1, Pallas kernels, spread(): pl.pallas_call(partial(spread_kernel, tables, count, Z), out_shape=(jax.S...  352 us
    pallas_call x1, Pallas kernels, sum_products(): pl.pallas_call(partial(sum_kernel, Z), out_shape=jax.ShapeDtypeStruct((un...  336 us
    dot_general x30, matrix products, matmul(): return jnp.dot(first_op, second_op, preferred_element_type=jnp.float32)  69.6 us
    dot_general x29, matrix products, against(): lax.dot_general(first_op, second_op, (((1,), (1,)), ((), ())), preferred_...  59 us
    unnamed x403, local copies, waits for them, and re-layouts  52.7 us
    another operation x1, local copies, waits for them, and re-layouts, layer_forward(): zip(hidden, ffn_down)  26.7 us
    pallas_call x2, Pallas kernels, exchange(): pl.pallas_call(partial(exchange_kernel, size, inner), out_shape=jax.Shape...  24.1 us
  transfers between devices with their start and end apart: 2, of which 0 were waited for; matrix products, arithmetic and copies ran while one was open for 16% of the time, Pallas kernels for 61%

profile of v4, /device:TPU:0, one launch (start us, length us, event | category | flops | bytes accessed | tf_op | source)
XLA Modules:
  0.0 1149.7 jit_solution(4487696633453676454)
XLA Ops:
  9.4 13.3 %shard_map.416 = f32[32,8,128]{2,1,0:T(8,128)} custom-call(f32[32,8,128]{2,1,0:T(8,128)} %broadcast_in_dim.85.in_ref), custom_call_target="tpu_custom_call" | custom-call | tf_op jit(solution)/shard_map/pallas_call | solution.py:680
  24.2 8.4 fusion.7
  38.4 1.9 reshape.746
  50.2 352.3 %shard_map.417 = (bf16[4,2,1024,1024]{3,2,1,0:T(8,128)(2,1)}, bf16[28,4,4,2,32,1024]{5,4,3,2,1,0:T(8,128)(2,1)}) custom-call(bf16[1024,256]{1,0:T(8,128)(2,1)} %convert_element_type.298.table_ref, bf16[28,32,1024]{2,1,0:T(8,128)(2,1)} %copy-done.101), custom_call_target="tpu_custom_call" | custom-call | tf_op jit(solution)/shard_map/pallas_call | solution.py:621
  402.6 10.7 gather_fusion
  413.2 1.9 fusion.101
  417.7 13.5 %fusion.140 = (bf16[1,4,4,2,32,1024]{5,4,3,2,1,0:T(8,128)(2,1)}, bf16[1,4,4,2,32,1024]{5,4,3,2,1,0:T(8,128)(2,1)}, bf16[1,4,4,2,32,1024]{5,4,3,2,1,0:T(8,128)(2,...) fusion(bf16[28,4,4,2,32,1024]{5,4,3,2,1,0:T(8,128)(2,1)} %get-t, ...), kind=kLoop, calls=%fused_computation.338 | loop fusion | bytes 37748736 | tf_op jit(solution)/shard_map/slice | solution.py:931
  432.6 2.2 convolution_convert_fusion.7
  434.8 1.5 copy.94
  437.5 4.1 convolution_convert_fusion.8
  441.6 1.5 copy.93
  444.2 3.2 convolution_convert_fusion.6
  448.7 1.5 reshape.756
  450.3 6.6 fusion.68
  456.8 9.3 fusion.146
  467.1 2.3 copy-done.13
  473.0 3.3 fusion.147
  482.7 26.7 %fusion.139 = (bf16[1,4,4,2,32,1024]{5,4,3,2,1,0:T(8,128)(2,1)}, bf16[1,4,4,2,32,1024]{5,4,3,2,1,0:T(8,128)(2,1)}, bf16[1,4,4,2,32,1024]{5,4,3,2,1,0:T(8,128)(2,...) fusion(bf16[28,4,4,2,32,1024]{5,4,3,2,1,0:T(8,128)(2,1)} %get-t, ...), kind=kLoop, calls=%fused_computation.337 | loop fusion | bytes 79691776 | tf_op jit(solution)/shard_map/unstack | solution.py:945
  512.6 2.2 convolution_convert_fusion.17
  516.4 2.6 fusion.144
  535.3 1.8 copy.104
  538.1 4.8 fusion.149
  542.9 3.0 divide_convert_fusion.1
  546.4 2.2 copy-done.31
  550.7 1.6 copy-done.62
  552.3 3.4 multiply_convert_fusion.6
  555.7 2.9 multiply_convert_fusion.7
  558.6 2.9 multiply_convert_fusion.8
  561.5 2.9 multiply_convert_fusion.9
  569.6 1.5 fusion.151
  572.8 16.2 %fusion.152 = (f32[512]{0:T(512)S(1)}, f32[512,8192]{1,0:T(8,128)}) fusion(bf16[512,1024]{1,0:T(8,128)(2,1)} %multiply_convert_fusion.5.refs_41_, bf16[8192,1024]{1,0:T(8,128)(2,1)} %bitcast.419), kind=kOutput, calls=%fused_computation.350 | convolution fusion | flops 8594128896 | bytes 34605056 | tf_op jit(solution)/shard_map/dot_general | solution.py:870
  589.0 10.2 multiply_reduce_fusion
  599.8 5.2 multiply_convert_fusion.refs_39_
  605.0 16.1 %multiply_reduce_fusion.2 = (f32[1024]{0:T(1024)S(1)}, f32[512]{0:T(512)S(1)}, f32[512,1024]{1,0:T(8,128)S(1)}) fusion(f32[512,1024]{1,0:T(8,128)S(1)} %get-tuple-element.189, f32[512]{0:T(512)S(1)} %fusion.114, f32[512]{0:T(512)S(1)} %broadcast_multiply_fusion, f32[1024]{0:T(1024)S(1)} %mul.1023, bf16[512,8192]{1,0:T(8,128)(2,1)S(1)} %multiply_convert_fusion.refs_39_, ...), kind=kOutput, calls=%fused_computation.81 | convolution fusion | flops 8593602560 | bytes 29374464 | tf_op jit(solution)/shard_map/dot_general | solution.py:860
  624.0 2.4 fusion.44.refs_18_
  626.4 2.4 fusion.37.refs_17_
  631.4 2.4 fusion.23.refs_15_
  636.4 2.4 fusion.30.refs_16_
  641.5 2.0 multiply_reduce_fusion.3
  644.3 1.7 fusion.134
  647.1 2.3 convolution_convert_fusion.4
  649.3 2.4 copy.107
  651.8 2.2 fusion.9
  657.0 1.6 copy-done.27
  676.4 1.6 convolution_convert_fusion.11
  681.1 1.6 convolution_convert_fusion.10
  696.1 2.3 multiply_convert_fusion.4
  699.8 3.6 multiply_reduce_fusion.4
  709.5 1.7 reshape.778
  711.2 3.7 fusion.50
  717.2 1.5 fusion.3
  718.8 4.2 fusion.4
  726.1 1.5 fusion.54
  729.8 2.4 copy.129.refs_9_
  732.2 2.3 copy.130.refs_10_
  735.9 3.4 fusion.162
  741.6 2.0 multiply_reduce_fusion.1
  743.6 1.7 fusion.130
  747.1 336.2 %shard_map.419 = f32[36,32,1024]{2,1,0:T(8,128)} custom-call(bf16[512,1024]{1,0:T(8,128)(2,1)} %get-tuple-element.142.refs_0_, bf16[512,1024]{1,0:T(8,128)(2,1)} %copy.127.refs_1_, bf16[512,1024]{1,0:T(8,128)(2,1)} %copy-done.71, bf16[512,1024]{1,0:T(8,128)(2,1)} %copy.128.refs_3_, bf16[512,1024]{1,0:T(8,128)(2,1)} %copy-done.72, ...), custom_call_target="tpu_custom_call" | custom-call | tf_op jit(solution)/shard_map/pallas_call | solution.py:368
  1083.3 4.3 slice.264.plain.refs_1_
  1091.1 10.8 shard_map.418
  1103.6 8.1 fusion.5.text.refs_3_
  1111.7 10.4 shard_map.420.refs_0_
  1122.7 19.9 %shard_map.421 = (f32[3,32,3072]{2,1,0:T(8,128)}, f32[3,32,1024]{2,1,0:T(8,128)}, f32[2,32,4096]{2,1,0:T(8,128)}, f32[2,128,1024]{2,1,0:T(8,128)}, f32[7,32]{1,0...) custom-call(f32[8,128]{1,0:T(8,128)} %copy-done.6, ...), custom_call_target="tpu_custom_call" | custom-call | tf_op jit(solution)/shard_map/pallas_call | solution.py:831
  (595 shorter events, 144.3 us)
Async XLA Ops:
  7.2 36.8 %copy-start = (s32[2]{0:T(128)S(1)}, s32[2]{0:T(128)}, u32[]{:S(2)}) copy-start(s32[2]{0:T(128)} %param.28) | copy-start | bytes 28
  7.2 502.2 %reduce-scatter.2.cloned.1.call-start = ((), (), s32[]{:S(2)}) async-start(), calls=%async_computation.1 | async-start | bytes 8650752 | tf_op jit(solution)/shard_map/reduce_scatter | solution.py:1085
  32.7 1070.9 %all-gather.2.cloned.1.call-start = ((), (), s32[]{:S(2)}) async-start(), calls=%async_computation.2 | async-start | bytes 8650752 | tf_op jit(solution)/shard_map/all_gather | solution.py:1137
  33.9 477.5 %copy-start.149 = (f32[1024]{0:T(1024)}, f32[1024]{0:T(1024)S(1)}, u32[]{:S(2)}) copy-start(f32[1024]{0:T(1024)S(1)} %mul.944) | copy-start | bytes 12292
  43.9 478.0 %copy-start.151 = (f32[1024]{0:T(1024)}, f32[1024]{0:T(1024)S(1)}, u32[]{:S(2)}) copy-start(f32[1024]{0:T(1024)S(1)} %mul.971) | copy-start | bytes 12292
  44.1 373.3 %copy-start.147 = (f32[1024]{0:T(1024)}, f32[1024]{0:T(1024)S(1)}, u32[]{:S(2)}) copy-start(f32[1024]{0:T(1024)S(1)} %mul.957) | copy-start | bytes 12292
  415.8 57.2 %copy-start.10 = (f32[2,256,1024]{2,1,0:T(8,128)}, f32[2,256,1024]{2,1,0:T(8,128)S(1)}, u32[]{:S(2)}) copy-start(f32[2,256,1024]{2,1,0:T(8,128)S(1)} %get-tuple-element.111) | copy-start | bytes 6291460
  417.7 13.5 %copy-start.137 = (bf16[2,256,1024]{2,1,0:T(8,128)(2,1)}, bf16[2,256,1024]{2,1,0:T(8,128)(2,1)S(1)}, u32[]{:S(2)}) copy-start(bf16[2,256,1024]{2,1,0:T(8,128)(2,1)S(1)} %multiply_convert_fusion.12) | copy-start | bytes 3145732
  450.2 19.3 %copy-start.40 = (bf16[2,256,16,64]{1,0,3,2:T(2,128)(2,1)}, bf16[2,256,16,64]{1,0,3,2:T(2,128)(2,1)S(1)}, u32[]{:S(2)}) copy-start(bf16[2,256,16,64]{1,0,3,2:T(2,128)(2,1)S(1)} %reshape.756) | copy-start | bytes 3145732
  472.9 3.4 copy-start.81
  473.0 3.7 copy-start.153
  510.7 10.4 copy-start.28
  511.6 4.1 copy-start.68
  512.6 3.8 copy-start.139
  516.3 4.3 copy-start.94
  516.4 4.7 copy-start.23
  521.9 3.4 copy-start.180
  522.1 5.0 copy-start.123
  524.0 4.4 copy-start.125
  525.3 4.2 copy-start.126
  527.1 3.6 copy-start.127
  532.9 4.2 copy-start.38
  533.1 4.0 copy-start.18
  533.3 4.3 copy-start.70
  537.8 8.1 copy-start.99
  542.9 3.4 copy-start.106
  545.9 4.1 copy-start.14
  546.3 3.7 copy-start.84
  550.7 10.8 copy-start.72
  555.7 13.6 %copy-start.73 = (bf16[512,1024]{1,0:T(8,128)(2,1)}, bf16[512,1024]{1,0:T(8,128)(2,1)S(1)}, u32[]{:S(2)}) copy-start(bf16[512,1024]{1,0:T(8,128)(2,1)S(1)} %get-tuple-element.186.refs_8_) | copy-start | bytes 3145732
  558.6 5.8 copy-start.131
  561.5 4.2 copy-start.132
  589.0 10.8 copy-start.9
  605.0 16.1 %copy-start.12 = (bf16[512,8192]{1,0:T(8,128)(2,1)}, bf16[512,8192]{1,0:T(8,128)(2,1)S(1)}, u32[]{:S(2)}) copy-start(bf16[512,8192]{1,0:T(8,128)(2,1)S(1)} %multiply_convert_fusion.refs_39_) | copy-start | bytes 25165828
  622.1 13.0 %copy-start.83 = (bf16[512,1024]{1,0:T(8,128)(2,1)}, bf16[512,1024]{1,0:T(8,128)(2,1)S(1)}, u32[]{:S(2)}) copy-start(bf16[512,1024]{1,0:T(8,128)(2,1)S(1)} %add_convert_fusion.refs_19_) | copy-start | bytes 3145732
  626.4 14.8 %copy-start.74 = (bf16[512,1024]{1,0:T(8,128)(2,1)}, bf16[512,1024]{1,0:T(8,128)(2,1)S(1)}, u32[]{:S(2)}) copy-start(bf16[512,1024]{1,0:T(8,128)(2,1)S(1)} %fusion.44.refs_18_) | copy-start | bytes 3145732
  636.4 3.5 copy-start.109
  647.1 4.7 copy-start.100
  654.8 4.6 copy-start.92
  657.0 3.5 copy-start.97
  660.9 7.4 copy-start.124
  675.1 4.0 copy-start.67
  675.1 4.0 copy-start.95
  676.4 3.4 copy-start.86
  676.4 3.4 copy-start.156
  687.4 3.6 copy-start.91
  688.7 3.9 copy-start.93
  696.1 3.6 copy-start.32
  696.1 3.6 copy-start.154
  696.1 3.6 copy-start.158
  696.1 3.6 copy-start.160
  699.7 3.7 copy-start.164
  699.8 3.7 copy-start.33
  711.2 6.0 copy-start.41
  718.7 4.3 copy-start.43
  729.8 4.6 copy-start.42
  735.9 3.4 copy-start.88
  735.9 3.4 copy-start.103
  1087.7 15.9 %copy-start.166 = (s32[4096]{0:T(1024)S(1)}, s32[4096]{0:T(1024)}, u32[]{:S(2)}) copy-start(s32[4096]{0:T(1024)} %copy-done.165) | copy-start | bytes 49156
  1089.0 22.7 %copy-start.3 = (f32[8,32,1024]{2,1,0:T(8,128)}, f32[8,32,1024]{2,1,0:T(8,128)S(1)}, u32[]{:S(2)}) copy-start(f32[8,32,1024]{2,1,0:T(8,128)S(1)} %slice.265) | copy-start | bytes 3145732
  1103.6 8.1 copy-start.5
  1103.6 8.1 copy-start.2
  1111.7 10.5 copy-start.4
  1122.7 19.9 %copy-start.1 = (s32[2]{0:T(128)S(1)}, s32[2]{0:T(128)}, u32[]{:S(2)}) copy-start(s32[2]{0:T(128)} %param.28) | copy-start | bytes 28
  (128 other events, 250.8 us)
Sparse Core Ops, SparseCore 0:
  32.8 173.1 reduce-scatter.1
  687.5 78.4 all-gather.1

commit v5 on v4

--- a/solution.py
+++ b/solution.py
@@ -39,16 +39,198 @@
 CODE_UNITS = 8
 
 
-def sum_kernel(Z, *refs):
-    dec_x, refs = refs[:9], refs[9:]
-    dec_g, refs = refs[:11], refs[11:]
-    enc_x, refs = refs[:8], refs[8:]
-    enc_g, refs = refs[:11], refs[11:]
+def place_of(Z):
+    dp, fs = lax.axis_index("dp"), lax.axis_index("fsdp")
+    z, core = fs // 2, fs % 2
+    x_mate, y_mate = dp + 1 - 2 * (dp % 2), (dp + 2) % 4
+    devices = ((dp, fs + 1 - 2 * core), (x_mate, fs), (y_mate, fs), (dp, fs + 2), (dp, fs - 2))
+    return dp, z, core, x_mate, y_mate, (x_mate + 2) % 4, devices, z < Z - 1, z > 0
+
+
+def add(a, b):
+    return (a.astype(F32) + b.astype(F32)).astype(BF)
+
+
+def remote(src, dst, send, recv, device):
+    return pltpu.make_async_remote_copy(
+        src_ref=src, dst_ref=dst, send_sem=send, recv_sem=recv, device_id=device, device_id_type=MESH
+    )
+
+
+def sum_scratch(Z, m, n):
+    depth, half = 2 * LAG, Z // 2
+    own_slots, held_slots, kept_slots = LAG + 1, 2 * LAG + 1, Z * LAG + 1
+    return [
+        pltpu.VMEM((own_slots, 4, Z, m, n), BF),
+        pltpu.VMEM((depth, 4, Z, m, n), BF),
+        pltpu.VMEM((held_slots, 4, Z, m, n), BF),
+        pltpu.VMEM((depth, half, m, n), BF),
+        pltpu.VMEM((depth, Z - half, m, n), BF),
+        pltpu.VMEM((depth, Z, m, n), BF),
+        pltpu.VMEM((depth, Z, m, n), BF),
+        pltpu.VMEM((kept_slots, Z, m, n), BF),
+        pltpu.VMEM((2, Z - 1, depth, m, n), BF),
+    ]
+
+
+def sum_semaphores(Z):
+    depth, dma = 2 * LAG, pltpu.SemaphoreType.DMA
+    return [
+        dma((depth,)),
+        dma((depth,)),
+        dma((2, depth)),
+        dma((2, depth)),
+        dma((2, depth)),
+        dma((2, depth)),
+        dma((2, Z - 1, depth)),
+        dma((2, Z - 1, depth)),
+    ]
+
+
+def sum_stages(Z, scratch, semaphores, arrive, out_ref):
+    own, from_core, held, from_x, from_y, all_x, all_y, kept, from_line = scratch
+    _, _, one_send, one_recv, two_send, two_recv, line_send, line_recv = semaphores
+    dp, z, core, x_mate, y_mate, across_dp, devices, has_up, has_down = place_of(Z)
+    _, x_dev, y_dev, up_dev, down_dev = devices
+    depth, half = 2 * LAG, Z // 2
+    own_slots, held_slots, kept_slots = own.shape[0], held.shape[0], kept.shape[0]
+
+    def one_copies(k):
+        s, block = k % depth, held.at[k % held_slots, across_dp]
+        return (
+            remote(block.at[pl.ds(0, half)], from_x.at[s], one_send.at[0, s], one_recv.at[0, s], x_dev),
+            remote(block.at[pl.ds(half, Z - half)], from_y.at[s], one_send.at[1, s], one_recv.at[1, s], y_dev),
+        )
+
+    def two_copies(k):
+        s, h = k % depth, k % held_slots
+        return (
+            remote(held.at[h, x_mate], all_x.at[s], two_send.at[0, s], two_recv.at[0, s], x_dev),
+            remote(held.at[h, y_mate], all_y.at[s], two_send.at[1, s], two_recv.at[1, s], y_dev),
+        )
+
+    def up_block(step):
+        return jnp.minimum(z + Z - step, Z - 1)
+
+    def down_block(step):
+        return jnp.maximum(z - Z + step, 0)
+
+    def up_copy(k, step):
+        s = k % depth
+        return remote(
+            kept.at[k % kept_slots, up_block(step)], from_line.at[0, step - 1, s],
+            line_send.at[0, step - 1, s], line_recv.at[0, step - 1, s], up_dev,
+        )
+
+    def down_copy(k, step):
+        s = k % depth
+        return remote(
+            kept.at[k % kept_slots, down_block(step)], from_line.at[1, step - 1, s],
+            line_send.at[1, step - 1, s], line_recv.at[1, step - 1, s], down_dev,
+        )
+
+    def line_start(k, step):
+        @pl.when(has_up)
+        def _():
+            up_copy(k, step).start()
+
+        @pl.when(has_down)
+        def _():
+            down_copy(k, step).start()
+
+    def line_wait(k, step):
+        @pl.when(has_down)
+        def _():
+            up_copy(k, step).wait_recv()
+            down_copy(k, step).wait_send()
+
+        @pl.when(has_up)
+        def _():
+            down_copy(k, step).wait_recv()
+            up_copy(k, step).wait_send()
+
+    def after_core(k):
+        arrive(k)
+
+        def one(block, carry):
+            for q in range(Z):
+                held[k % held_slots, block, q] = add(
+                    own[k % own_slots, block, q], from_core[k % depth, block, q]
+                )
+            return carry
+
+        lax.fori_loop(0, 4, one, 0)
+        for copy in one_copies(k):
+            copy.start()
+
+    def after_one(k):
+        s, h = k % depth, k % held_slots
+        for copy in one_copies(k):
+            copy.wait()
+        for q in range(half):
+            held[h, y_mate, q] = add(held[h, y_mate, q], from_x[s, q])
+        for q in range(Z - half):
+            held[h, x_mate, half + q] = add(held[h, x_mate, half + q], from_y[s, q])
+        for copy in two_copies(k):
+            copy.start()
+
+    def after_two(k):
+        s, h = k % depth, k % held_slots
+        for copy in two_copies(k):
+            copy.wait()
+        for q in range(Z):
+            kept[k % kept_slots, q] = (
+                held[h, dp, q].astype(F32) + all_x[s, q].astype(F32) + all_y[s, q].astype(F32)
+            ).astype(BF)
+        line_start(k, 1)
+
+    def along_line(step):
+        def run(k):
+            s, h = k % depth, k % kept_slots
+            line_wait(k, step - 1)
+
+            @pl.when(has_down & (z + Z - step <= Z - 1))
+            def _():
+                kept[h, up_block(step)] = add(kept[h, up_block(step)], from_line[0, step - 2, s])
+
+            @pl.when(has_up & (z - Z + step >= 0))
+            def _():
+                kept[h, down_block(step)] = add(kept[h, down_block(step)], from_line[1, step - 2, s])
+
+            line_start(k, step)
+
+        return run
+
+    def finish(k):
+        s = k % depth
+        line_wait(k, Z - 1)
+        out_ref[k] = kept[k % kept_slots, z].astype(F32)
+
+        @pl.when(has_down)
+        def _():
+            out_ref[k] = out_ref[k] + from_line[0, Z - 2, s].astype(F32)
+
+        @pl.when(has_up)
+        def _():
+            out_ref[k] = out_ref[k] + from_line[1, Z - 2, s].astype(F32)
+
+    stages = [after_core, after_one, after_two]
+    return stages + [along_line(step) for step in range(2, Z)] + [finish], up_block, down_block
+
+
+def sum_kernel(Z, counts, *refs):
+    groups = []
+    for count in counts:
+        groups.append([ref.at[i] for ref in refs[:count] for i in range(ref.shape[0])])
+        refs = refs[count:]
+    dec_x, dec_g, enc_x, enc_g = groups
     (
         code_x, targets, code_g, look_g, out_ref,
         dec_xs, dec_gs, dec_turned, enc_xs, enc_gs, enc_turned, code_xs, code_loaded, code_gs, to_core,
         own, from_core, held, from_x, from_y, all_x, all_y, kept, from_line,
+        rare_held, rare_line, rare_kept, rare_x, rare_y, rare_all_x, rare_all_y,
         load_sem, code_sem, core_send, core_recv, one_send, one_recv, two_send, two_recv, line_send, line_recv,
+        rare_line_send, rare_line_recv, rare_send, rare_recv,
     ) = refs
     dec_units, enc_units = len(DEC_INPUTS), len(ENC_INPUTS)
     plain_units = dec_units + enc_units
@@ -75,16 +257,11 @@
         pl.semaphore_signal(barrier, inc=1, device_id=down_dev, device_id_type=MESH)
 
     pl.semaphore_wait(barrier, 3 + has_up.astype(jnp.int32) + has_down.astype(jnp.int32))
-    half = Z // 2
-    own_slots, held_slots, kept_slots = own.shape[0], held.shape[0], kept.shape[0]
-
-    def add(a, b):
-        return (a.astype(F32) + b.astype(F32)).astype(BF)
-
-    def remote(src, dst, send, recv, device):
-        return pltpu.make_async_remote_copy(
-            src_ref=src, dst_ref=dst, send_sem=send, recv_sem=recv, device_id=device, device_id_type=MESH
-        )
+    scratch = (own, from_core, held, from_x, from_y, all_x, all_y, kept, from_line)
+    semaphores = (
+        core_send, core_recv, one_send, one_recv, two_send, two_recv, line_send, line_recv
+    )
+    own_slots = own.shape[0]
 
     def pair(x, g, xs, gs, slot):
         return (
@@ -123,60 +300,6 @@
             to_core.at[k % own_slots], from_core.at[s], core_send.at[s], core_recv.at[s], core_dev
         )
 
-    def one_copies(k):
-        s, block = k % depth, held.at[k % held_slots, across_dp]
-        return (
-            remote(block.at[pl.ds(0, half)], from_x.at[s], one_send.at[0, s], one_recv.at[0, s], x_dev),
-            remote(block.at[pl.ds(half, Z - half)], from_y.at[s], one_send.at[1, s], one_recv.at[1, s], y_dev),
-        )
-
-    def two_copies(k):
-        s, h = k % depth, k % held_slots
-        return (
-            remote(held.at[h, x_mate], all_x.at[s], two_send.at[0, s], two_recv.at[0, s], x_dev),
-            remote(held.at[h, y_mate], all_y.at[s], two_send.at[1, s], two_recv.at[1, s], y_dev),
-        )
-
-    def up_block(step):
-        return jnp.minimum(z + Z - step, Z - 1)
-
-    def down_block(step):
-        return jnp.maximum(z - Z + step, 0)
-
-    def up_copy(k, step):
-        s = k % depth
-        return remote(
-            kept.at[k % kept_slots, up_block(step)], from_line.at[0, step - 1, s],
-            line_send.at[0, step - 1, s], line_recv.at[0, step - 1, s], up_dev,
-        )
-
-    def down_copy(k, step):
-        s = k % depth
-        return remote(
-            kept.at[k % kept_slots, down_block(step)], from_line.at[1, step - 1, s],
-            line_send.at[1, step - 1, s], line_recv.at[1, step - 1, s], down_dev,
-        )
-
-    def line_start(k, step):
-        @pl.when(has_up)
-        def _():
-            up_copy(k, step).start()
-
-        @pl.when(has_down)
-        def _():
-            down_copy(k, step).start()
-
-    def line_wait(k, step):
-        @pl.when(has_down)
-        def _():
-            up_copy(k, step).wait_recv()
-            down_copy(k, step).wait_send()
-
-        @pl.when(has_up)
-        def _():
-            down_copy(k, step).wait_recv()
-            up_copy(k, step).wait_send()
-
     def turn(xs, slot, turned):
         size = 256
 
@@ -263,82 +386,127 @@
             core_copy(k).start()
             code_product(k, core, own.at[o])
 
-    def after_core(k):
+    def arrive(k):
+        core_copy(k).wait()
+
+    later, up_block, down_block = sum_stages(Z, scratch, semaphores, arrive, out_ref)
+
+    def turn_of(k):
+        return (k // 9) * 2 + (k % 9 >= 7).astype(jnp.int32)
+
+    def rare_slot(k):
+        return turn_of(k) % rare_held.shape[0]
+
+    def rare_line_copies(k, step):
+        t, s = turn_of(k), rare_slot(k)
+        return [
+            remote(
+                rare_held.at[s, :, block], rare_line.at[s, way, step - 1],
+                rare_line_send.at[way, step - 1, t], rare_line_recv.at[way, step - 1, t], device,
+            )
+            for way, block, device in ((0, up_block(step), up_dev), (1, down_block(step), down_dev))
+        ]
+
+    def rare_valid(step):
+        return (has_up & (z + Z - step <= Z - 1), has_down & (z - Z + step >= 0)), (
+            has_down & (z - 1 + Z - step <= Z - 1),
+            has_up & (z + 1 - Z + step >= 0),
+        )
+
+    def rare_line_start(k, step):
+        for copy, sends in zip(rare_line_copies(k, step), rare_valid(step)[0]):
+            pl.when(sends)(copy.start)
+
+    def rare_line_wait(k, step):
+        for copy, sends, receives in zip(rare_line_copies(k, step), *rare_valid(step)):
+            pl.when(sends)(copy.wait_send)
+            pl.when(receives)(copy.wait_recv)
+
+    def rare_add(into, k, step):
+        for way, receives in enumerate(rare_valid(step)[1]):
+
+            @pl.when(receives)
+            def _(way=way):
+                for block in range(4):
+                    ref = into(way, block)
+                    ref[...] = add(ref[...], rare_line[rare_slot(k), way, step - 1, block])
+
+    def rare_square(k, slot):
+        t, s = turn_of(k), rare_slot(k)
+        small = rare_kept.shape[2] // 2
+        source, target, device = (
+            (rare_kept.at[s, across_dp, pl.ds(0, small)], rare_x.at[s], x_dev),
+            (rare_kept.at[s, across_dp, pl.ds(small, small)], rare_y.at[s], y_dev),
+            (rare_kept.at[s, x_mate], rare_all_x.at[s], x_dev),
+            (rare_kept.at[s, y_mate], rare_all_y.at[s], y_dev),
+        )[slot]
+        return remote(source, target, rare_send.at[slot, t], rare_recv.at[slot, t], device)
+
+    def rare_after_core(k):
         core_copy(k).wait()
 
         def one(block, carry):
             for q in range(Z):
-                held[k % held_slots, block, q] = add(
+                rare_held[rare_slot(k), block, q] = add(
                     own[k % own_slots, block, q], from_core[k % depth, block, q]
                 )
             return carry
 
         lax.fori_loop(0, 4, one, 0)
-        for copy in one_copies(k):
-            copy.start()
-
-    def after_one(k):
-        s, h = k % depth, k % held_slots
-        for copy in one_copies(k):
-            copy.wait()
-        for q in range(half):
-            held[h, y_mate, q] = add(held[h, y_mate, q], from_x[s, q])
-        for q in range(Z - half):
-            held[h, x_mate, half + q] = add(held[h, x_mate, half + q], from_y[s, q])
-        for copy in two_copies(k):
-            copy.start()
-
-    def after_two(k):
-        s, h = k % depth, k % held_slots
-        for copy in two_copies(k):
-            copy.wait()
-        for q in range(Z):
-            kept[k % kept_slots, q] = (
-                held[h, dp, q].astype(F32) + all_x[s, q].astype(F32) + all_y[s, q].astype(F32)
-            ).astype(BF)
-        line_start(k, 1)
-
-    def along_line(step):
+        rare_line_start(k, 1)
+
+    def rare_along(step):
         def run(k):
-            s, h = k % depth, k % kept_slots
-            line_wait(k, step - 1)
-
-            @pl.when(has_down & (z + Z - step <= Z - 1))
-            def _():
-                kept[h, up_block(step)] = add(kept[h, up_block(step)], from_line[0, step - 2, s])
-
-            @pl.when(has_up & (z - Z + step >= 0))
-            def _():
-                kept[h, down_block(step)] = add(kept[h, down_block(step)], from_line[1, step - 2, s])
-
-            line_start(k, step)
+            rare_line_wait(k, step - 1)
+            s = rare_slot(k)
+            rare_add(
+                lambda way, block: rare_held.at[s, block, (up_block, down_block)[way](step)], k, step - 1
+            )
+            rare_line_start(k, step)
 
         return run
 
-    def finish(k):
-        s = k % depth
-        line_wait(k, Z - 1)
-        out_ref[k] = kept[k % kept_slots, z].astype(F32)
-
-        @pl.when(has_down)
-        def _():
-            out_ref[k] = out_ref[k] + from_line[0, Z - 2, s].astype(F32)
-
-        @pl.when(has_up)
-        def _():
-            out_ref[k] = out_ref[k] + from_line[1, Z - 2, s].astype(F32)
-
-    stages = [begin, after_core, after_one, after_two]
-    stages += [along_line(step) for step in range(2, Z)] + [finish]
+    def rare_after_line(k):
+        rare_line_wait(k, Z - 1)
+        s = rare_slot(k)
+        for block in range(4):
+            rare_kept[s, block] = rare_held[s, block, z]
+        rare_add(lambda way, block: rare_kept.at[s, block], k, Z - 1)
+        for slot in range(2):
+            rare_square(k, slot).start()
+
+    def rare_after_one(k):
+        s, small = rare_slot(k), rare_kept.shape[2] // 2
+        for slot in range(2):
+            rare_square(k, slot).wait()
+        first, second = pl.ds(0, small), pl.ds(small, small)
+        rare_kept[s, y_mate, first] = add(rare_kept[s, y_mate, first], rare_x[s])
+        rare_kept[s, x_mate, second] = add(rare_kept[s, x_mate, second], rare_y[s])
+        for slot in range(2, 4):
+            rare_square(k, slot).start()
+
+    def rare_finish(k):
+        s = rare_slot(k)
+        for slot in range(2, 4):
+            rare_square(k, slot).wait()
+        out_ref[k] = (
+            rare_kept[s, dp].astype(F32) + rare_all_x[s].astype(F32) + rare_all_y[s].astype(F32)
+        )
+
+    stages = [begin] + later
+    rare_stages = [begin, rare_after_core] + [rare_along(step) for step in range(2, Z)]
+    rare_stages += [rare_after_line, rare_after_one, rare_finish]
 
     def loop_step(j, carry):
         for place in reversed(range(len(stages))):
             k = j - place * LAG
-
-            @pl.when((k >= 0) & (k < units))
-            def _(k=k, run=stages[place]):
-                run(k)
-
+            here = (k >= 0) & (k < units)
+            rare = (k % 9 == 3) | (k % 9 == 7)
+            if place == 0:
+                pl.when(here)(partial(begin, k))
+            else:
+                pl.when(here & jnp.logical_not(rare))(partial(stages[place], k))
+                pl.when(here & rare)(partial(rare_stages[place], k))
         return carry
 
     lax.fori_loop(0, units + (len(stages) - 1) * LAG, loop_step, 0)
@@ -348,7 +516,9 @@
     dp_size, fsdp_size = lax.axis_size("dp"), lax.axis_size("fsdp")
     devices, Z = dp_size * fsdp_size, fsdp_size // 2
     m = D // devices
+    stacks = (dec_x, dec_g, enc_x, enc_g)
     if dp_size != 4 or Z != 4 or m % 32:
+        dec_x, dec_g, enc_x, enc_g = [[row for stack in group for row in stack] for group in stacks]
         products = [across(dec_x[i], dec_g[min(k, 10)]) for k, i in enumerate(DEC_INPUTS)]
         products += [across(enc_x[i], enc_g[min(k, 10)]) for k, i in enumerate(ENC_INPUTS)]
         plain = jnp.stack(products).astype(BF).reshape(len(products), devices, m, D)
@@ -358,17 +528,18 @@
         code = code.transpose(0, 2, 1, 3).reshape(devices, D // dp_size, VOCAB // fsdp_size)
         plain = lax.psum_scatter(plain, AXES, scatter_dimension=1, tiled=True)
         code = lax.psum_scatter(code, AXES, scatter_dimension=0, tiled=True)
-        return plain.reshape(-1, m, D).astype(F32), code.reshape(D // dp_size, -1).astype(F32)
+        return jnp.concatenate([plain.reshape(-1, m, D), code.reshape(-1, m, D)]).astype(F32)
     n, units = D, len(DEC_INPUTS) + len(ENC_INPUTS) + CODE_UNITS
     depth, half = 2 * LAG, Z // 2
     own_slots, held_slots, kept_slots = LAG + 1, 2 * LAG + 1, Z * LAG + 1
-    dec_rows, enc_rows, code_rows = dec_x[0].shape[0], enc_x[0].shape[0], code_x.shape[0]
+    dec_rows, enc_rows, code_rows = dec_x[0].shape[1], enc_x[0].shape[1], code_x.shape[0]
+    counts = [len(group) for group in stacks]
     dma = pltpu.SemaphoreType.DMA
     whole = pl.BlockSpec(memory_space=pl.ANY)
     out = pl.pallas_call(
-        partial(sum_kernel, Z),
+        partial(sum_kernel, Z, counts),
         out_shape=jax.ShapeDtypeStruct((units, m, n), F32),
-        in_specs=[whole] * 40 + [pl.BlockSpec(memory_space=pltpu.VMEM)] + [whole] * 2,
+        in_specs=[whole] * (sum(counts) + 1) + [pl.BlockSpec(memory_space=pltpu.VMEM)] + [whole] * 2,
         out_specs=pl.BlockSpec(memory_space=pltpu.VMEM),
         scratch_shapes=[
             pltpu.VMEM((2, dec_rows, n), BF),
@@ -390,6 +561,13 @@
             pltpu.VMEM((depth, Z, m, n), BF),
             pltpu.VMEM((kept_slots, Z, m, n), BF),
             pltpu.VMEM((2, Z - 1, depth, m, n), BF),
+            pltpu.VMEM((3, 4, Z, m, n), BF),
+            pltpu.VMEM((3, 2, Z - 1, 4, m, n), BF),
+            pltpu.VMEM((3, 4, m, n), BF),
+            pltpu.VMEM((3, m // 2, n), BF),
+            pltpu.VMEM((3, m // 2, n), BF),
+            pltpu.VMEM((3, m, n), BF),
+            pltpu.VMEM((3, m, n), BF),
             dma((2, 2)),
             dma((3,)),
             dma((depth,)),
@@ -400,17 +578,23 @@
             dma((2, depth)),
             dma((2, Z - 1, depth)),
             dma((2, Z - 1, depth)),
+            dma((2, Z - 1, 2 * (units // 9 + 1))),
+            dma((2, Z - 1, 2 * (units // 9 + 1))),
+            dma((4, 2 * (units // 9 + 1))),
+            dma((4, 2 * (units // 9 + 1))),
         ],
         compiler_params=pltpu.CompilerParams(
-            collective_id=call_id, has_side_effects=True, vmem_limit_bytes=60 << 20
+            collective_id=call_id, has_side_effects=True, vmem_limit_bytes=62 << 20
         ),
     )(*dec_x, *dec_g, *enc_x, *enc_g, code_x, targets[:, None], code_g, look_g)
-    return out[:-CODE_UNITS], out[-CODE_UNITS:].reshape(-1, n)
+    return out
 
 
 def spread_kernel(
-    tables, units, Z, table_ref, unit_ref, table_out, unit_out,
-    own_sem, line_send, line_recv, square_send, square_recv, core_send, core_recv,
+    tables, units, Z, token_count, table_f32, mix_in, mix_out, ffn_up, ffn_down, text_table, small,
+    table_out, unit_out, text_out, small_all,
+    table_ref, unit_ref, looked, own_sem, line_send, line_recv, square_send, square_recv, core_send, core_recv,
+    small_send, small_recv, text_sem, *sum_refs,
 ):
     dp, fs = lax.axis_index("dp"), lax.axis_index("fsdp")
     z, core = fs // 2, fs % 2
@@ -434,10 +618,54 @@
         size = unit_out.shape[4] // 2
         return unit_out.at[k - tables, dp_at, z_at, core_at, pl.ds(part * size, size)]
 
-    def remote(ref, send, recv, device):
-        return pltpu.make_async_remote_copy(
-            src_ref=ref, dst_ref=ref, send_sem=send, recv_sem=recv, device_id=device, device_id_type=MESH
-        )
+    def passed(ref, send, recv, device):
+        return remote(ref, ref, send, recv, device)
+
+    size, inner = 8 * Z, 2 * Z
+    me = dp * inner + fs
+
+    def peer(i):
+        other = lax.rem(me + i, size)
+        return (other // inner, lax.rem(other, inner))
+
+    def each(run):
+        def one(i, carry):
+            run(i)
+            return carry
+
+        lax.fori_loop(1, size, one, 0)
+
+    def small_copy(i):
+        return remote(small, small_all.at[me], small_send.at[i], small_recv.at[i], peer(i))
+
+    barrier = pltpu.get_barrier_semaphore()
+    each(lambda i: pl.semaphore_signal(barrier, inc=1, device_id=peer(i), device_id_type=MESH))
+    small_all[me] = small[...]
+
+    rows = unit_ref.shape[1]
+    place = 0
+
+    def put(value):
+        nonlocal place
+        unit_ref[place] = value.astype(BF)
+        place += 1
+
+    def put_ffn(layer, with_down):
+        turned = [
+            swap_groups([ffn_up[layer, :, pl.ds(128 * (4 * g + j), 128)] for j in range(4)]) for g in range(8)
+        ]
+        for q in range(4):
+            put(jnp.concatenate([parts[q] for parts in turned], axis=1))
+        for q in range(4 if with_down else 0):
+            put(ffn_down[layer, pl.ds(q * rows, rows), :])
+
+    for layer in range(3):
+        for i in range(3):
+            put(mix_in[layer, :, pl.ds(i * D, D)])
+        put(mix_out[layer])
+        if layer != 1:
+            put_ffn(min(layer, 1), layer == 0)
+    table_ref[...] = table_f32[...].astype(BF)
 
     own = (
         pltpu.make_async_copy(
@@ -448,28 +676,17 @@
     for copy in own:
         copy.start()
 
-    barrier = pltpu.get_barrier_semaphore()
-    for device in (core_dev, x_dev, y_dev):
-        pl.semaphore_signal(barrier, inc=1, device_id=device, device_id_type=MESH)
-
-    @pl.when(has_up)
-    def _():
-        pl.semaphore_signal(barrier, inc=1, device_id=up_dev, device_id_type=MESH)
-
-    @pl.when(has_down)
-    def _():
-        pl.semaphore_signal(barrier, inc=1, device_id=down_dev, device_id_type=MESH)
-
     for copy in own:
         copy.wait()
-    pl.semaphore_wait(barrier, 3 + has_up.astype(jnp.int32) + has_down.astype(jnp.int32))
+    pl.semaphore_wait(barrier, size - 1)
+    each(lambda i: small_copy(i).start())
 
     def line_copies(view, k, step):
         s = step - 1
         return (
-            (remote(view(jnp.maximum(z - s, 0)), line_send.at[0, s, k], line_recv.at[0, s, k], up_dev),
+            (passed(view(jnp.maximum(z - s, 0)), line_send.at[0, s, k], line_recv.at[0, s, k], up_dev),
              has_up & (z >= s), has_down & (z >= s + 1)),
-            (remote(view(jnp.minimum(z + s, Z - 1)), line_send.at[1, s, k], line_recv.at[1, s, k], down_dev),
+            (passed(view(jnp.minimum(z + s, Z - 1)), line_send.at[1, s, k], line_recv.at[1, s, k], down_dev),
              has_down & (z + s <= Z - 1), has_up & (z + s + 1 <= Z - 1)),
         )
 
@@ -483,10 +700,10 @@
             pl.when(receives)(copy.wait_recv)
 
     def to_core(ref, k, slot):
-        return remote(ref, core_send.at[slot, k], core_recv.at[slot, k], core_dev)
+        return passed(ref, core_send.at[slot, k], core_recv.at[slot, k], core_dev)
 
     def square_copy(ref, k, slot):
-        return remote(
+        return passed(
             ref, square_send.at[slot, k], square_recv.at[slot, k], x_dev if slot % 2 == 0 else y_dev
         )
 
@@ -592,9 +809,55 @@
              for is_table in (True, False) for first, form in ((True, line_first), (False, square_first))]
     n_stages = Z + 3
 
+    scratch, semaphores = sum_refs[:9], sum_refs[9:]
+    own_slots, depth = scratch[0].shape[0], scratch[1].shape[0]
+
+    def look_up():
+        each(lambda i: small_copy(i).wait())
+        owned_rows = text_table.shape[0]
+        base = me * token_count
+
+        def of_device(device, carry):
+            ids = small_all[device][:1]
+            row = lax.broadcasted_iota(jnp.int32, (owned_rows, ids.shape[1]), 0)
+            hit = (row + base == ids.astype(jnp.int32)) & (row < token_count)
+            found = across(jnp.where(hit, 1.0, 0.0).astype(BF), text_table[...]).astype(BF)
+            dp_at, line_at, core_at = device // inner, lax.rem(device, inner) // 2, lax.rem(device, 2)
+            for u in range(looked.shape[0]):
+                looked[u, dp_at, line_at, core_at] = found[u * rows : (u + 1) * rows]
+            return carry
+
+        lax.fori_loop(0, size, of_device, 0)
+
+    def text_own(k):
+        return pltpu.make_async_copy(
+            looked.at[k, :, :, core], scratch[0].at[k % own_slots], text_sem.at[k % own_slots]
+        )
+
+    def text_core(k):
+        s = k % depth
+        return remote(
+            looked.at[k, :, :, 1 - core], scratch[1].at[s], semaphores[0].at[s], semaphores[1].at[s], core_dev
+        )
+
+    def text_begin(k):
+        text_own(k).start()
+        text_core(k).start()
+
+    def text_arrive(k):
+        text_own(k).wait()
+        text_core(k).wait()
+
+    text_stages = [text_begin] + sum_stages(Z, scratch, semaphores, text_arrive, text_out)[0]
+
+    text_first = 3
+
     def loop_step(j, carry):
+        pl.when(j == text_first)(look_up)
         for place in reversed(range(n_stages)):
             k = j - place * LAG
+            turn = k - text_first
+            pl.when((turn >= 0) & (turn < looked.shape[0]))(partial(text_stages[place], turn))
             turn = k % 9
             by_line = (turn != 3) & (turn != 7)
             for is_table, first, stages in forms:
@@ -610,23 +873,48 @@
     lax.fori_loop(0, total + (n_stages - 1) * LAG, loop_step, 0)
 
 
-def spread(table, units, call_id):
-    count, m, n = units.shape
-    Z = lax.axis_size("fsdp") // 2
-    if lax.axis_size("dp") != 4 or Z != 4 or m % 32:
-        whole = lax.all_gather(lax.all_gather(table, "dp", axis=1, tiled=True), "fsdp", axis=0, tiled=True)
-        return whole, lax.all_gather(units, AXES, axis=1, tiled=True)
-    tables, dma = 8, pltpu.SemaphoreType.DMA
+def spread(table, weights, text_table, small, call_id):
+    mix_in, mix_out, ffn_up, ffn_down = weights
+    dp_size, fsdp_size = lax.axis_size("dp"), lax.axis_size("fsdp")
+    m, Z = mix_in.shape[1], fsdp_size // 2
+    if dp_size != 4 or Z != 4 or m != 32:
+        shards = []
+        for layer in range(3):
+            shards += [column_units(mix_in[layer]), mix_out[layer][None]]
+            if layer != 1:
+                which = min(layer, 1)
+                shards += [hidden_units(ffn_up[which], dp_size * fsdp_size)]
+            if layer == 0:
+                shards += [ffn_down[0].reshape(4, m, D)]
+        table = lax.all_gather(table.astype(BF), "dp", axis=1, tiled=True)
+        whole = lax.all_gather(table, "fsdp", axis=0, tiled=True)
+        units = lax.all_gather(jnp.concatenate(shards).astype(BF), AXES, axis=1, tiled=True)
+        devices, count = dp_size * fsdp_size, text_table.shape[0]
+        small_all = exchange(jnp.broadcast_to(small[None], (devices, 8, 128)), 3)
+        ids = small_all[:, 0].astype(jnp.int32).reshape(-1)
+        base = (lax.axis_index("dp") * fsdp_size + lax.axis_index("fsdp")) * count
+        owned = (ids[:, None] - base == jnp.arange(count)[None, :]).astype(BF)
+        looked = matmul(owned, text_table.astype(BF)).astype(BF)
+        text = lax.psum_scatter(looked, AXES, scatter_dimension=0, tiled=True).astype(F32)
+        return whole, units, text, small_all
+    text_units, token_count = TXT_LEN // m, text_table.shape[0]
+    text_table = jnp.pad(text_table.astype(BF), ((0, -token_count % 128), (0, 0)))
+    tables, count, dma = 8, 24, pltpu.SemaphoreType.DMA
     total = tables + count
-    whole, units = pl.pallas_call(
-        partial(spread_kernel, tables, count, Z),
+    whole, units, text, small_all = pl.pallas_call(
+        partial(spread_kernel, tables, count, Z, token_count),
         out_shape=(
             jax.ShapeDtypeStruct((Z, 2, table.shape[0], 4 * table.shape[1]), BF),
-            jax.ShapeDtypeStruct((count, 4, Z, 2, m, n), BF),
+            jax.ShapeDtypeStruct((count, 4, Z, 2, m, D), BF),
+            jax.ShapeDtypeStruct((text_units, m, D), F32),
+            jax.ShapeDtypeStruct((8 * Z, *small.shape), F32),
         ),
-        in_specs=[pl.BlockSpec(memory_space=pltpu.VMEM)] * 2,
-        out_specs=[pl.BlockSpec(memory_space=pl.ANY)] * 2,
+        in_specs=[pl.BlockSpec(memory_space=pltpu.VMEM)] * 7,
+        out_specs=[pl.BlockSpec(memory_space=pl.ANY)] * 2 + [pl.BlockSpec(memory_space=pltpu.VMEM)] * 2,
         scratch_shapes=[
+            pltpu.VMEM(table.shape, BF),
+            pltpu.VMEM((count, m, D), BF),
+            pltpu.VMEM((text_units, 4, Z, 2, m, D), BF),
             dma((2,)),
             dma((2, Z - 1, total)),
             dma((2, Z - 1, total)),
@@ -634,10 +922,17 @@
             dma((4, total)),
             dma((4, total)),
             dma((4, total)),
+            dma((8 * Z,)),
+            dma((8 * Z,)),
+            dma((LAG + 1,)),
+            *sum_scratch(Z, m, D),
+            *sum_semaphores(Z),
         ],
-        compiler_params=pltpu.CompilerParams(collective_id=call_id, has_side_effects=True),
-    )(table, units)
-    return whole.reshape(-1, 4 * table.shape[1]), units.reshape(count, -1, n)
+        compiler_params=pltpu.CompilerParams(
+            collective_id=call_id, has_side_effects=True, vmem_limit_bytes=48 << 20
+        ),
+    )(table, *weights, text_table, small)
+    return whole.reshape(-1, 4 * table.shape[1]), units.reshape(count, -1, D), text.reshape(-1, D), small_all
 
 
 def exchange_kernel(size, inner, in_ref, out_ref, send_sem, recv_sem):
@@ -705,67 +1000,66 @@
     return results
 
 
-def norm_kernel(size, inner, plain, code, text, gains, norm_out, squares, gathered, sum_scratch, send_sem, recv_sem):
-    rows = plain.shape[1]
+def norm_kernel(
+    size, inner, count, sums, text, small, small_out, norm_out,
+    squares, small_all, squares_all, sum_scratch, small_send, small_recv, square_send, square_recv,
+):
+    rows = sums.shape[1]
     text_rows = [(start, min(rows, text.shape[0] - start)) for start in range(0, text.shape[0], rows)]
-
-    sum_scratch[...] = jnp.zeros_like(sum_scratch)
-
-    def square(k, carry):
-        sum_scratch[...] += plain[k] * plain[k]
-        return carry
-
-    lax.fori_loop(0, plain.shape[0], square, 0)
-
-    def square_code(k, carry):
-        part = code[pl.ds(pl.multiple_of(k * rows, rows), rows), :]
-        sum_scratch[...] += part * part
-        return carry
-
-    lax.fori_loop(0, code.shape[0] // rows, square_code, 0)
-    for start, count in text_rows:
-        part = text[pl.ds(start, count), :]
-        sum_scratch[pl.ds(0, count), :] += part * part
-    own = jnp.sum(sum_scratch[...]) + jnp.sum(gains[...] * gains[...])
-    squares[...] = jnp.full(squares.shape, own)
-
     me = lax.axis_index("dp") * inner + lax.axis_index("fsdp")
 
     def peer(i):
         other = lax.rem(me + i, size)
-        return (other // inner, lax.rem(other, inner))
-
-    def copy(i):
-        return pltpu.make_async_remote_copy(
-            src_ref=squares, dst_ref=gathered.at[me], send_sem=send_sem.at[i],
-            recv_sem=recv_sem.at[i], device_id=peer(i), device_id_type=MESH,
-        )
+        return other, (other // inner, lax.rem(other, inner))
+
+    def small_copy(i):
+        other, device = peer(i)
+        return remote(small.at[other], small_all.at[me], small_send.at[i], small_recv.at[i], device)
+
+    def square_copy(i):
+        return remote(squares, squares_all.at[me], square_send.at[i], square_recv.at[i], peer(i)[1])
+
+    def each(run):
+        def one(i, carry):
+            run(i)
+            return carry
+
+        lax.fori_loop(1, size, one, 0)
 
     barrier = pltpu.get_barrier_semaphore()
-
-    def greet(i, carry):
-        pl.semaphore_signal(barrier, inc=1, device_id=peer(i), device_id_type=MESH)
+    each(lambda i: pl.semaphore_signal(barrier, inc=1, device_id=peer(i)[1], device_id_type=MESH))
+    small_all[me] = small[me]
+    pl.semaphore_wait(barrier, size - 1)
+    each(lambda i: small_copy(i).start())
+
+    sum_scratch[...] = jnp.zeros_like(sum_scratch)
+
+    def square(k, carry):
+        sum_scratch[...] += sums[k] * sums[k]
         return carry
 
-    def begin(i, carry):
-        copy(i).start()
-        return carry
-
-    def end(i, carry):
-        copy(i).wait()
-        return carry
-
-    lax.fori_loop(1, size, greet, 0)
-    gathered[me] = squares[...]
-    pl.semaphore_wait(barrier, size - 1)
-    lax.fori_loop(1, size, begin, 0)
-    lax.fori_loop(1, size, end, 0)
-    norm = jnp.sqrt(lax.fori_loop(0, size, lambda i, total: total + gathered[i], jnp.zeros_like(squares)))
-    norm_out[...] = norm
+    lax.fori_loop(0, sums.shape[0], square, 0)
+    for start, length in text_rows:
+        part = text[pl.ds(start, length), :]
+        sum_scratch[pl.ds(0, length), :] += part * part
+
+    each(lambda i: small_copy(i).wait())
+    total = lax.fori_loop(0, size, lambda i, total: total + small_all[i], jnp.zeros_like(squares))
+    small_out[...] = total
+    place = lax.broadcasted_iota(jnp.int32, total.shape, 0) * 128 + lax.broadcasted_iota(jnp.int32, total.shape, 1)
+    gains = jnp.where(place < count, total, 0.0)
+    squares[...] = jnp.full(squares.shape, jnp.sum(sum_scratch[...]) + jnp.sum(gains * gains))
+
+    squares_all[me] = squares[...]
+    each(lambda i: square_copy(i).start())
+    each(lambda i: square_copy(i).wait())
+    norm_out[...] = jnp.sqrt(
+        lax.fori_loop(0, size, lambda i, total: total + squares_all[i], jnp.zeros_like(squares))
+    )
 
 
 def update_kernel(*refs):
-    norm, plain, code, text, gains, *refs = refs
+    norm, plain, text, gains, *refs = refs
     weights, refs = refs[:7], refs[7:]
     firsts, refs = refs[:7], refs[7:]
     seconds, refs = refs[:7], refs[7:]
@@ -801,41 +1095,48 @@
     step(4, (every, every), gains[...])
     for start, count in text_rows:
         step(5, (pl.ds(start, count), every), text[pl.ds(start, count), :])
-    columns = 256
-    for i in range(code.shape[1] // columns):
-        step(6, (pl.ds(i * columns, columns), every), code[:, pl.ds(i * columns, columns)].T)
-
-
-def update(plain, code, text, gains, weights, firsts, seconds, call_id):
+    columns, first = 256, len(DEC_INPUTS) + len(ENC_INPUTS)
+    for i in range(D // columns):
+        part = plain[pl.ds(first, CODE_UNITS), :, pl.ds(i * columns, columns)]
+        step(6, (pl.ds(i * columns, columns), every), part.reshape(-1, columns).T)
+
+
+def update(sums, text, small, weights, firsts, seconds, call_id):
     inner = lax.axis_size("fsdp")
     size = lax.axis_size("dp") * inner
     shapes = [jax.ShapeDtypeStruct(weight.shape, F32) for weight in weights]
+    gains_shape = weights[4].shape
+    count = gains_shape[0] * gains_shape[1]
     in_vmem = pl.BlockSpec(memory_space=pltpu.VMEM)
-    dma = pltpu.SemaphoreType.DMA
-    norm = pl.pallas_call(
-        partial(norm_kernel, size, inner),
-        out_shape=jax.ShapeDtypeStruct((8, 128), F32),
-        in_specs=[in_vmem] * 4,
-        out_specs=in_vmem,
+    dma, tile = pltpu.SemaphoreType.DMA, jax.ShapeDtypeStruct((8, 128), F32)
+    small, norm = pl.pallas_call(
+        partial(norm_kernel, size, inner, count),
+        out_shape=[tile, tile],
+        in_specs=[in_vmem] * 3,
+        out_specs=[in_vmem] * 2,
         scratch_shapes=[
             pltpu.VMEM((8, 128), F32),
             pltpu.VMEM((size, 8, 128), F32),
-            pltpu.VMEM(plain.shape[1:], F32),
+            pltpu.VMEM((size, 8, 128), F32),
+            pltpu.VMEM(sums.shape[1:], F32),
+            dma((size,)),
+            dma((size,)),
             dma((size,)),
             dma((size,)),
         ],
         compiler_params=pltpu.CompilerParams(
             collective_id=call_id, has_side_effects=True, vmem_limit_bytes=32 << 20
         ),
-    )(plain, code, text, gains)
+    )(sums, text, small)
+    small = small.reshape(-1)
     outs = pl.pallas_call(
         update_kernel,
         out_shape=shapes * 3,
-        in_specs=[in_vmem] * 26,
+        in_specs=[in_vmem] * 25,
         out_specs=[in_vmem] * 21,
         compiler_params=pltpu.CompilerParams(vmem_limit_bytes=60 << 20),
-    )(norm, plain, code, text, gains, *weights, *firsts, *seconds)
-    return norm[0, 0], list(zip(outs[:7], outs[7:14], outs[14:]))
+    )(norm, sums, text, small[:count].reshape(gains_shape), *weights, *firsts, *seconds)
+    return small[count], norm[0, 0], list(zip(outs[:7], outs[7:14], outs[14:]))
 
 
 def layer_norm(stream, gain):
@@ -844,8 +1145,13 @@
 
 
 def norm_back(stream, gain, grad_out):
-    _, pullback = jax.vjp(layer_norm, stream, gain)
-    return pullback(grad_out)
+    centred = stream - jnp.mean(stream, axis=-1, keepdims=True)
+    inverse = lax.rsqrt(jnp.mean(centred * centred, axis=-1, keepdims=True) + 1e-05)
+    plain = centred * inverse
+    scaled = grad_out * gain
+    inner = jnp.mean(scaled * plain, axis=-1, keepdims=True)
+    grad = inverse * (scaled - jnp.mean(scaled, axis=-1, keepdims=True) - plain * inner)
+    return grad, jnp.sum(grad_out * plain, axis=0, keepdims=True)
 
 
 def positions(length, width):
@@ -872,126 +1178,379 @@
     )
 
 
-def heads_first(matrix, blocks):
-    return matrix.reshape(blocks, -1, HEADS, HEAD).transpose(0, 2, 1, 3)
-
-
-def heads_last(array):
-    return array.transpose(0, 2, 1, 3).reshape(-1, HEADS * HEAD)
-
-
-def attention(queries, keys_in, values, visible):
-    scores = jnp.einsum(
-        "bhqd,bhkd->bhqk", queries, keys_in, preferred_element_type=F32
-    ) * HEAD ** (-0.5)
-    scores = jnp.where(visible[:, None], scores, MASKED)
+LOCAL = 56 << 20
+
+
+def gain_at(i):
+    return pl.BlockSpec((1, 1, D), lambda *_: (i, 0, 0))
+
+
+def fixed(shape):
+    return pl.BlockSpec(shape, lambda *_: (0,) * len(shape))
+
+
+def turns(shape):
+    return pl.BlockSpec((1, *shape[1:]), lambda i: (i,) + (0,) * (len(shape) - 1))
+
+
+def unit_from(first):
+    return pl.BlockSpec((1, D, D), lambda i: (first + i, 0, 0))
+
+
+def cost(rows, count):
+    return pl.CostEstimate(flops=2 * rows * D * D * count, bytes_accessed=2 * D * D * count + 8 * rows * D, transcendentals=0)
+
+
+def steps(kernel, count, rows, in_specs, out_specs, out_shape, scratch, *args):
+    return pl.pallas_call(
+        kernel,
+        grid=(count,),
+        in_specs=in_specs,
+        out_specs=out_specs,
+        out_shape=out_shape,
+        scratch_shapes=scratch,
+        cost_estimate=cost(rows, count),
+        compiler_params=pltpu.CompilerParams(vmem_limit_bytes=LOCAL),
+    )(*args)
+
+
+def shaped(shape, kind):
+    return jax.ShapeDtypeStruct(shape, kind)
+
+
+def project(stream, gain, units, first, count):
+    rows = stream.shape[0]
+
+    def kernel(x, g, w, normed, out):
+        @pl.when(pl.program_id(0) == 0)
+        def _():
+            normed[...] = layer_norm(x[...], g[0]).astype(BF)
+
+        out[0] = matmul(normed[...], w[0]).astype(BF)
+
+    whole = (count, rows, D)
+    return steps(
+        kernel, count, rows,
+        [fixed((rows, D)), gain_at(gain[1]), unit_from(first)],
+        [fixed((rows, D)), turns(whole)],
+        [shaped((rows, D), BF), shaped(whole, BF)], [],
+        stream, gain[0], units,
+    )
+
+
+def products(value, units, first, count):
+    rows = value.shape[0]
+
+    def kernel(x, w, out):
+        out[0] = matmul(x[...], w[0]).astype(BF)
+
+    whole = (count, rows, D)
+    return steps(
+        kernel, count, rows, [fixed((rows, D)), unit_from(first)], turns(whole), shaped(whole, BF), [],
+        value, units,
+    )
+
+
+def add_products(stream, parts, units, first):
+    count, rows, _ = parts.shape
+
+    def kernel(x, a, w, out):
+        @pl.when(pl.program_id(0) == 0)
+        def _():
+            out[...] = x[...]
+
+        out[...] += matmul(a[0], w[0])
+
+    return steps(
+        kernel, count, rows,
+        [fixed((rows, D)), turns(parts.shape), unit_from(first)], fixed((rows, D)), shaped((rows, D), F32), [],
+        stream, parts, units,
+    )
+
+
+def hidden_layer(stream, gain, units, first):
+    rows = stream.shape[0]
+    bend, rate = 0.044715, math.sqrt(2.0 / math.pi)
+
+    def kernel(x, g, w, normed, out, slope):
+        @pl.when(pl.program_id(0) == 0)
+        def _():
+            normed[...] = layer_norm(x[...], g[0]).astype(BF)
+
+        for start in range(0, rows, 128):
+            at = pl.ds(start, 128)
+            z = matmul(normed[at], w[0])
+            square = z * z
+            flat = jnp.tanh(rate * z * (1.0 + bend * square))
+            out[0, at] = (0.5 * z * (1.0 + flat)).astype(BF)
+            slope[0, at] = (
+                0.5 * (1.0 + flat) + 0.5 * z * (1.0 - flat * flat) * rate * (1.0 + 3.0 * bend * square)
+            ).astype(BF)
+
+    whole = (4, rows, D)
+    return steps(
+        kernel, 4, rows,
+        [fixed((rows, D)), gain_at(gain[1]), unit_from(first)],
+        [fixed((rows, D)), turns(whole), turns(whole)],
+        [shaped((rows, D), BF), shaped(whole, BF), shaped(whole, BF)], [],
+        stream, gain[0], units,
+    )
+
+
+def norm_only(stream, gain):
+    def kernel(x, g, out):
+        out[...] = layer_norm(x[...], g[0]).astype(BF)
+
+    return steps(
+        kernel, 1, 8, [fixed(stream.shape), gain_at(gain[1])], fixed(stream.shape), shaped(stream.shape, BF), [],
+        stream, gain[0],
+    )
+
+
+def norm_only_back(grad, stream, gain):
+    shape = stream.shape
+
+    def kernel(d, x, g, out, low, gain_out):
+        out[...], gain_out[...] = norm_back(x[...], g[0], d[...])
+        low[...] = out[...].astype(BF)
+
+    return steps(
+        kernel, 1, 8, [fixed(shape), fixed(shape), gain_at(gain[1])],
+        [fixed(shape), fixed(shape), fixed((1, D))],
+        [shaped(shape, F32), shaped(shape, BF), shaped((1, D), F32)], [],
+        grad, stream, gain[0],
+    )
+
+
+def project_back(parts, units, first, stream, gain, grad):
+    count, rows, _ = parts.shape
+    shape = (rows, D)
+
+    def kernel(d, w, x, g, above, out, low, gain_out, total):
+        @pl.when(pl.program_id(0) == 0)
+        def _():
+            total[...] = jnp.zeros_like(total)
+
+        total[...] += against(d[0], w[0])
+
+        @pl.when(pl.program_id(0) == count - 1)
+        def _():
+            part, gain_out[...] = norm_back(x[...], g[0], total[...])
+            out[...] = above[...] + part
+            low[...] = out[...].astype(BF)
+
+    return steps(
+        kernel, count, rows,
+        [turns(parts.shape), unit_from(first), fixed(shape), gain_at(gain[1]), fixed(shape)],
+        [fixed(shape), fixed(shape), fixed((1, D))],
+        [shaped(shape, F32), shaped(shape, BF), shaped((1, D), F32)], [pltpu.VMEM(shape, F32)],
+        parts, units, stream, gain[0], grad,
+    )
+
+
+def products_back(parts, units, first):
+    count, rows, _ = parts.shape
+    shape = (rows, D)
+
+    def kernel(d, w, out):
+        @pl.when(pl.program_id(0) == 0)
+        def _():
+            out[...] = jnp.zeros_like(out)
+
+        out[...] += against(d[0], w[0])
+
+    return steps(
+        kernel, count, rows, [turns(parts.shape), unit_from(first)], fixed(shape), shaped(shape, F32), [],
+        parts, units,
+    )
+
+
+def mix_back(low, units, first):
+    rows = low.shape[0]
+
+    def kernel(d, w, out):
+        out[...] = against(d[...], w[0]).astype(BF)
+
+    return steps(
+        kernel, 1, rows, [fixed((rows, D)), unit_from(first)], fixed((rows, D)), shaped((rows, D), BF), [],
+        low, units,
+    )
+
+
+def hidden_back(low, slope, units, up_first, down_units, down_first, stream, gain, grad):
+    rows = low.shape[0]
+    shape = (rows, D)
+
+    def kernel(d, s, up, down, x, g, above, hidden, out, out_low, gain_out, total):
+        @pl.when(pl.program_id(0) == 0)
+        def _():
+            total[...] = jnp.zeros_like(total)
+
+        for start in range(0, rows, 128):
+            at = pl.ds(start, 128)
+            hidden[0, at] = (against(d[at], down[0]) * s[0, at].astype(F32)).astype(BF)
+            total[at] += against(hidden[0, at], up[0])
+
+        @pl.when(pl.program_id(0) == 3)
+        def _():
+            part, gain_out[...] = norm_back(x[...], g[0], total[...])
+            out[...] = above[...] + part
+            out_low[...] = out[...].astype(BF)
+
+    return steps(
+        kernel, 4, 2 * rows,
+        [fixed(shape), turns(slope.shape), unit_from(up_first), unit_from(down_first),
+         fixed(shape), gain_at(gain[1]), fixed(shape)],
+        [turns(slope.shape), fixed(shape), fixed(shape), fixed((1, D))],
+        [shaped(slope.shape, BF), shaped(shape, F32), shaped(shape, BF), shaped((1, D), F32)],
+        [pltpu.VMEM(shape, F32)],
+        low, slope, units, down_units, stream, gain[0], grad,
+    )
+
+
+PAIR = 2 * HEAD
+PAIRS = 4
+
+
+def head_lanes(value, head):
+    lane = lax.broadcasted_iota(jnp.int32, value.shape, 1)
+    return jnp.where(lane // HEAD == head, value, jnp.zeros_like(value))
+
+
+def head_shares(query, key, labels, head):
+    scores = against(head_lanes(query, head), key) * HEAD ** (-0.5)
+    if labels is None:
+        row = lax.broadcasted_iota(jnp.int32, scores.shape, 0)
+        visible = lax.broadcasted_iota(jnp.int32, scores.shape, 1) <= row
+    else:
+        visible = labels[0][...] == labels[1][...]
+    scores = jnp.where(visible, scores, MASKED)
     weights = jnp.exp(scores - jnp.max(scores, axis=-1, keepdims=True))
-    shares = weights / jnp.sum(weights, axis=-1, keepdims=True)
-    low = shares.astype(BF)
-    attended = jnp.einsum("bhqk,bhkd->bhqd", low, values, preferred_element_type=F32)
-    return heads_last(attended.astype(BF)), low
-
-
-def attention_back(queries, keys_in, values, shares, grad_mixed):
-    grad_heads = heads_first(grad_mixed, queries.shape[0])
-    grad_shares = jnp.einsum(
-        "bhqd,bhkd->bhqk", grad_heads, values, preferred_element_type=F32
-    )
-    wide = shares.astype(F32)
-    grad_scores = (
-        wide * (grad_shares - jnp.sum(wide * grad_shares, axis=-1, keepdims=True))
-    ).astype(BF)
-    grad_query = jnp.einsum(
-        "bhqk,bhkd->bhqd", grad_scores, keys_in, preferred_element_type=F32
-    ) * HEAD ** (-0.5)
-    grad_keys = jnp.einsum(
-        "bhqk,bhqd->bhkd", grad_scores, queries, preferred_element_type=F32
-    ) * HEAD ** (-0.5)
-    grad_values = jnp.einsum(
-        "bhqk,bhqd->bhkd", shares, grad_heads, preferred_element_type=F32
-    )
-    return grad_query, grad_keys, grad_values
-
-
-def layer_forward(stream, weights, gains, self_visible, memory, cross_visible):
-    project, mix_out, cross, cross_out, ffn_up, ffn_down = weights
-    blocks = self_visible.shape[0]
+    return weights / jnp.sum(weights, axis=-1, keepdims=True)
+
+
+def attention_specs(blocks, parts, labels):
+    def one(array, place):
+        return pl.BlockSpec((1, array.shape[1] // blocks, PAIRS * PAIR), lambda b, h: (place, b, h))
+
+    marks = [] if labels is None else [fixed(label.shape) for label in labels]
+    return (blocks, D // (PAIRS * PAIR)), [one(*part) for part in parts], marks
+
+
+def pair_columns(count, rows, blocks):
+    return pl.BlockSpec((count, rows // blocks, PAIRS * PAIR), lambda b, h: (0, b, h))
+
+
+def attention(parts, blocks, labels):
+    grid, specs, marks = attention_specs(blocks, parts, labels)
+    rows = parts[0][0].shape[1]
+
+    def kernel(q, k, v, *rest):
+        seen, out = (rest[:-1] or None), rest[-1]
+        for pair in range(PAIRS):
+            at = pl.ds(pair * PAIR, PAIR)
+            query, key, value = q[0, :, at], k[0, :, at], v[0, :, at]
+            total = 0.0
+            for head in range(2):
+                shares = head_shares(query, key, seen, head).astype(BF)
+                total = total + matmul(shares, head_lanes(value, head))
+            out[0, :, at] = total.astype(BF)
+
+    return pl.pallas_call(
+        kernel,
+        grid=grid,
+        in_specs=[*specs, *marks],
+        out_specs=pair_columns(1, rows, blocks),
+        out_shape=shaped((1, rows, D), BF),
+        compiler_params=pltpu.CompilerParams(vmem_limit_bytes=LOCAL),
+    )(*[array for array, _ in parts], *(labels or ()))
+
+
+def attention_back(parts, grad, blocks, labels):
+    grid, specs, marks = attention_specs(blocks, parts, labels)
+    rows, keys = parts[0][0].shape[1], parts[1][0].shape[1]
+    counts = [(3, rows)] if rows == keys else [(1, rows), (2, keys)]
+
+    def kernel(q, k, v, d, *rest):
+        seen, outs = (rest[: -len(counts)] or None), rest[-len(counts) :]
+        places = [(out, i) for out in outs for i in range(out.shape[0])]
+        for pair in range(PAIRS):
+            at = pl.ds(pair * PAIR, PAIR)
+            query, key, value, grads = q[0, :, at], k[0, :, at], v[0, :, at], d[:, at]
+            grad_query = grad_key = grad_value = 0.0
+            for head in range(2):
+                shares = head_shares(query, key, seen, head)
+                above = head_lanes(grads, head)
+                grad_shares = against(above, value)
+                inner = jnp.sum(shares * grad_shares, axis=-1, keepdims=True)
+                grad_scores = (shares * (grad_shares - inner)).astype(BF)
+                grad_query = grad_query + matmul(grad_scores, head_lanes(key, head))
+                grad_key = grad_key + across(grad_scores, head_lanes(query, head))
+                grad_value = grad_value + across(shares.astype(BF), above)
+            results = (grad_query * HEAD ** (-0.5), grad_key * HEAD ** (-0.5), grad_value)
+            for (out, i), result in zip(places, results):
+                out[i, :, at] = result.astype(BF)
+
+    return pl.pallas_call(
+        kernel,
+        grid=grid,
+        in_specs=[*specs, pl.BlockSpec((rows // blocks, PAIRS * PAIR), lambda b, h: (b, h)), *marks],
+        out_specs=[pair_columns(count, length, blocks) for count, length in counts],
+        out_shape=[shaped((count, length, D), BF) for count, length in counts],
+        compiler_params=pltpu.CompilerParams(vmem_limit_bytes=LOCAL),
+    )(*[array for array, _ in parts], grad, *(labels or ()))
+
+
+def layer_forward(stream, units, first, down_units, down, gains, blocks, labels, memory, cross_labels):
     stored = {"stream": stream}
-    normed = layer_norm(stream, gains[0]).astype(BF)
-    queries, keys_in, values = [
-        heads_first(matmul(normed, project[i]).astype(BF), blocks) for i in range(3)
-    ]
-    attended, shares = attention(queries, keys_in, values, self_visible)
-    stream = stream + matmul(attended, mix_out)
-    stored.update(
-        normed=normed, self_attention=(queries, keys_in, values, shares), attended=attended, after_self=stream
-    )
+    stored["normed"], qkv = project(stream, gains[0], units, first, 3)
+    stored["self"] = [(qkv, i) for i in range(3)]
+    stored["attended"] = attention(stored["self"], blocks, labels)
+    stream = add_products(stream, stored["attended"], units, first + 3)
+    last = first + 4
     if memory is not None:
-        cross_in = layer_norm(stream, gains[1]).astype(BF)
-        cross_query = heads_first(matmul(cross_in, cross[0]).astype(BF), 1)
-        memory_keys = heads_first(matmul(memory, cross[1]).astype(BF), 1)
-        memory_values = heads_first(matmul(memory, cross[2]).astype(BF), 1)
-        cross_mixed, cross_shares = attention(cross_query, memory_keys, memory_values, cross_visible)
-        stream = stream + matmul(cross_mixed, cross_out)
-        stored.update(
-            cross_in=cross_in,
-            cross_attention=(cross_query, memory_keys, memory_values, cross_shares),
-            cross_mixed=cross_mixed,
-        )
+        stored["after_self"] = stream
+        stored["cross_in"], cross_query = project(stream, gains[1], units, first + 4, 1)
+        memory_kv = products(memory, units, first + 5, 2)
+        stored["cross"] = [(cross_query, 0), (memory_kv, 0), (memory_kv, 1)]
+        stored["cross_mixed"] = attention(stored["cross"], 1, cross_labels)
+        stream = add_products(stream, stored["cross_mixed"], units, first + 7)
+        last = first + 8
     stored["before_ffn"] = stream
-    ffn_in = layer_norm(stream, gains[-2]).astype(BF)
-    hidden_pre = [matmul(ffn_in, up) for up in ffn_up]
-    hidden = [jax.nn.gelu(pre, approximate=True).astype(BF) for pre in hidden_pre]
-    for low, down in zip(hidden, ffn_down):
-        stream = stream + matmul(low, down)
-    stored.update(ffn_in=ffn_in, hidden_pre=hidden_pre, hidden=hidden, before_final=stream)
-    return layer_norm(stream, gains[-1]).astype(BF), stored
-
-
-def layer_backward(grad_final, weights, gains, stored, memory):
-    project, mix_out, cross, cross_out, ffn_up, ffn_down = weights
+    stored["ffn_in"], stored["hidden"], stored["slope"] = hidden_layer(stream, gains[-2], units, last)
+    stream = add_products(stream, stored["hidden"], down_units, down)
+    stored["before_final"] = stream
+    return norm_only(stream, gains[-1]), stored
+
+
+def layer_backward(
+    grad_final, units, first, down_units, down, gains, blocks, labels, stored, memory, cross_labels
+):
     gain_grads = [None] * len(gains)
-    grad_stream, gain_grads[-1] = norm_back(stored["before_final"], gains[-1], grad_final)
-    ffn_low = grad_stream.astype(BF)
-    grad_pres = []
-    grad_ffn = 0.0
-    for pre, up, down in zip(stored["hidden_pre"], ffn_up, ffn_down):
-        _, gelu_pull = jax.vjp(partial(jax.nn.gelu, approximate=True), pre)
-        grad_pres.append(gelu_pull(against(ffn_low, down))[0].astype(BF))
-        grad_ffn = grad_ffn + against(grad_pres[-1], up)
-    grad_normed, gain_grads[-2] = norm_back(stored["before_ffn"], gains[-2], grad_ffn)
-    grad_stream = grad_stream + grad_normed
+    last = first + (4 if memory is None else 8)
+    grad, ffn_low, gain_grads[-1] = norm_only_back(grad_final, stored["before_final"], gains[-1])
+    hidden_grads, grad, low, gain_grads[-2] = hidden_back(
+        ffn_low, stored["slope"], units, last, down_units, down, stored["before_ffn"], gains[-2], grad
+    )
     cross_inputs, cross_grads, memory_grads = [], [], []
     grad_memory = None
     if memory is not None:
-        cross_low = grad_stream.astype(BF)
-        grad_mixed = against(cross_low, cross_out).astype(BF)
-        grads = [
-            heads_last(grad.astype(BF)) for grad in attention_back(*stored["cross_attention"], grad_mixed)
-        ]
-        cross_inputs = [stored["cross_in"], stored["cross_mixed"]]
-        cross_grads = [grads[0], cross_low]
-        memory_grads = grads[1:]
-        grad_memory = against(grads[1], cross[1]) + against(grads[2], cross[2])
-        grad_normed, gain_grads[1] = norm_back(
-            stored["after_self"], gains[1], against(grads[0], cross[0])
+        grad_query, grad_memory_kv = attention_back(
+            stored["cross"], mix_back(low, units, first + 7), 1, cross_labels
         )
-        grad_stream = grad_stream + grad_normed
-    self_low = grad_stream.astype(BF)
-    grad_mixed = against(self_low, mix_out).astype(BF)
-    grads = [
-        heads_last(grad.astype(BF)) for grad in attention_back(*stored["self_attention"], grad_mixed)
-    ]
-    grad_normed, gain_grads[0] = norm_back(
-        stored["stream"],
-        gains[0],
-        sum(against(grads[i], project[i]) for i in range(3)),
-    )
-    grad_stream = grad_stream + grad_normed
-    inputs = [stored["normed"], stored["attended"], *cross_inputs, stored["ffn_in"], *stored["hidden"]]
-    outputs = [*grads, self_low, *cross_grads, *grad_pres, ffn_low]
+        cross_inputs = [stored["cross_in"][None], stored["cross_mixed"]]
+        cross_grads = [grad_query, low[None]]
+        memory_grads = [grad_memory_kv]
+        grad_memory = products_back(grad_memory_kv, units, first + 5)
+        grad, low, gain_grads[1] = project_back(
+            grad_query, units, first + 4, stored["after_self"], gains[1], grad
+        )
+    (grads,) = attention_back(stored["self"], mix_back(low, units, first + 3), blocks, labels)
+    inputs = [stored["normed"][None], stored["attended"], *cross_inputs, stored["ffn_in"][None], stored["hidden"]]
+    outputs = [grads, low[None], *cross_grads, hidden_grads, ffn_low[None]]
+    grad, _, gain_grads[0] = project_back(grads, units, first, stored["stream"], gains[0], grad)
     parts = (inputs, outputs) if memory is None else (inputs, outputs, memory_grads)
-    return grad_stream, grad_memory, gain_grads, parts
+    return grad, grad_memory, gain_grads, parts
 
 
 def adam_step(weight, moment_one, second, gradient, rate):
@@ -1065,51 +1624,32 @@
     scale_in = math.sqrt(D)
     rows = mix_in.shape[1]
     segments = text_segments[0]
-    text_visible = (segments[:, None] == segments[None, :])[None]
-    place = jnp.arange(IMG_LEN)
-    self_visible = jnp.broadcast_to(
-        place[None, :] <= place[:, None], (image_count, IMG_LEN, IMG_LEN)
-    )
-    wanted = jnp.repeat(caption_of, IMG_LEN)
-    cross_visible = (segments[None, :] == wanted[:, None])[None]
-
-    small = tiles(jnp.concatenate([text_ids[0].astype(F32), norm_gains.reshape(-1)]), devices)
-    small = exchange(small, 3).reshape(devices, 1024)[:, : TXT_LEN + 7 * norm_gains.shape[1]]
+    text_labels = (segments[:, None], segments[None, :])
+    cross_labels = (jnp.repeat(caption_of, IMG_LEN)[:, None], segments[None, :])
+
+    small = tiles(jnp.concatenate([text_ids[0].astype(F32), norm_gains.reshape(-1)]), 1)[0]
+    code_full, units, text_rows, small = spread(
+        code_table, (mix_in, mix_out, ffn_up, ffn_down), text_table, small, 4
+    )
+    small = small.reshape(devices, 1024)[:, : TXT_LEN + 7 * norm_gains.shape[1]]
     all_ids = small[:, :TXT_LEN].astype(jnp.int32).reshape(-1)
-    gains = small[:, TXT_LEN:].reshape(devices, 7, -1).transpose(1, 0, 2).reshape(7, D)
+    gains = small[:, TXT_LEN:].reshape(devices, 7, -1).transpose(1, 0, 2).reshape(7, 1, D)
     gains = gains.astype(BF).astype(F32)
-
     base = me * text_table.shape[0]
     owned = (all_ids[:, None] - base == jnp.arange(text_table.shape[0])[None, :]).astype(BF)
-    looked = matmul(owned, text_table.astype(BF)).astype(BF)
-    text_rows = lax.psum_scatter(looked, AXES, scatter_dimension=0, tiled=True)
-
-    def layer_units(which):
-        return [
-            column_units(mix_in[which]),
-            mix_out[which][None],
-            hidden_units(ffn_up[min(which, 1)], devices),
-            ffn_down[min(which, 1)].reshape(4, rows, D),
-        ]
-
-    shards = layer_units(0) + layer_units(1)[:2] + layer_units(2)
-    code_full, units = spread(code_table.astype(BF), jnp.concatenate(shards).astype(BF), 4)
-    enc_units, self_units, late_units = units[:12], units[12:16], units[16:]
-    enc_weights = (enc_units[:3], enc_units[3], None, None, enc_units[4:8], enc_units[8:])
-    dec_weights = (
-        self_units[:3], self_units[3], late_units[:3], late_units[3], late_units[4:8], late_units[8:]
-    )
-
-    text_in = text_rows.astype(F32) * scale_in + positions(TXT_LEN, D)
-    enc_gains = [gains[i] for i in range(3)]
-    dec_gains = [gains[i] for i in range(3, 7)]
-    memory, enc_stored = layer_forward(text_in, enc_weights, enc_gains, text_visible, None, None)
+    last = ffn_down[1].reshape(4, rows, D).astype(BF)
+    last = lax.optimization_barrier((last, text_rows))[0]
+    down_units = lax.all_gather(last, AXES, axis=1, tiled=True)
+    text_in = text_rows * scale_in + positions(TXT_LEN, D)
+    enc_gains = [(gains, i) for i in range(3)]
+    dec_gains = [(gains, i) for i in range(3, 7)]
+    memory, enc_stored = layer_forward(text_in, units, 0, units, 8, enc_gains, 1, text_labels, None, None)
 
     image_rows = code_full[codes].astype(F32) * scale_in
     shifted = jnp.concatenate([jnp.zeros_like(image_rows[:, :1]), image_rows[:, :-1]], axis=1)
     image_in = (shifted + positions(IMG_LEN, D)[None]).reshape(-1, D)
     final_out, dec_stored = layer_forward(
-        image_in, dec_weights, dec_gains, self_visible, memory, cross_visible
+        image_in, units, 12, down_units, 0, dec_gains, image_count, None, memory, cross_labels
     )
 
     targets = codes.reshape(-1)
@@ -1127,12 +1667,12 @@
     grad_final = matmul(grad_logits, code_full)
 
     grad_image, grad_memory, dec_gain_grads, dec_parts = layer_backward(
-        grad_final, dec_weights, dec_gains, dec_stored, memory
+        grad_final, units, 12, down_units, 0, dec_gains, image_count, None, dec_stored, memory, cross_labels
     )
     grad_text, _, enc_gain_grads, enc_parts = layer_backward(
-        grad_memory, enc_weights, enc_gains, enc_stored, None
-    )
-    gain_part = jnp.stack(enc_gain_grads + dec_gain_grads)
+        grad_memory, units, 0, units, 8, enc_gains, 1, text_labels, enc_stored, None, None
+    )
+    gain_part = jnp.concatenate(enc_gain_grads + dec_gain_grads)
 
     grad_rows = lax.all_gather((grad_text * scale_in).astype(BF), AXES, axis=0, tiled=True)
     text_grad = across(owned, grad_rows)
@@ -1141,15 +1681,13 @@
     grad_looked = jnp.pad(grad_looked, ((0, 0), (0, 1), (0, 0))).reshape(-1, D).astype(BF)
     enc_x, enc_g = enc_parts
     dec_x, dec_g, memory_g = dec_parts
-    plain_sum, code_sum = sum_products(
-        dec_x, dec_g, [memory] + enc_x, memory_g + enc_g, grad_logits, targets, final_out, grad_looked, 1
+    sums = sum_products(
+        dec_x, dec_g, [memory[None]] + enc_x, memory_g + enc_g, grad_logits, targets, final_out, grad_looked, 1
     )
     gain_blocks = gain_part.reshape(7, devices, rows).transpose(1, 0, 2).reshape(devices, 7 * rows)
     gain_blocks = jnp.concatenate([gain_blocks, jnp.full((devices, 1), loss_part)], axis=1)
     gain_blocks = jnp.pad(gain_blocks, ((0, 0), (0, 1024 - gain_blocks.shape[1])))
-    small_sum = jnp.sum(exchange(gain_blocks.reshape(devices, 8, 128), 5), axis=0).reshape(-1)
-    loss_sum = small_sum[7 * rows]
-    gains_grad = small_sum[: 7 * rows].reshape(7, rows)
+    gain_blocks = gain_blocks.reshape(devices, 8, 128)
     params = (mix_in, mix_out, ffn_up, ffn_down, norm_gains, text_table, code_table)
     firsts = (
         mix_in_first,
@@ -1170,11 +1708,12 @@
         code_second,
     )
     if rows == 32:
-        grad_norm, updated = update(
-            plain_sum, code_sum, text_grad, gains_grad, params, firsts, seconds, 6
-        )
+        loss_sum, grad_norm, updated = update(sums, text_grad, gain_blocks, params, firsts, seconds, 6)
     else:
-        dec_sum, enc_sum = plain_sum[:14], plain_sum[14:]
+        small_sum = jnp.sum(exchange(gain_blocks, 5), axis=0).reshape(-1)
+        loss_sum = small_sum[7 * rows]
+        gains_grad = small_sum[: 7 * rows].reshape(7, rows)
+        dec_sum, enc_sum = sums[:14], sums[14:28]
         gradients = (
             jnp.stack(
                 [
@@ -1187,7 +1726,7 @@
             jnp.stack([part.reshape(-1, D) for part in (enc_sum[10:], dec_sum[10:])]),
             gains_grad,
             text_grad,
-            code_sum.T,
+            sums[28:].reshape(D // dp_size, -1).T,
         )
         square_part = sum((jnp.sum(gradient * gradient) for gradient in gradients))
         squares = exchange(tiles(square_part[None], devices), 6)[:, 0, 0]

time: 1160 us -> 998 us (0.86)
  Pallas kernels: 743 us -> 877 us
  local copies, waits for them, and re-layouts: 161 us -> 29.7 us
  matrix products: 168 us -> 37.8 us
  other arithmetic: 59.9 us -> 29.8 us
    pallas_call x5 -> x33, Pallas kernels: 723 us -> 857 us  [the longest x1 322 us: spread(): pl.pallas_call(partial(spread_kernel, tables, count, Z, token_count), out...]
    dot_general x30 -> x1, matrix products: 69.6 us -> 13.6 us  [matmul(): return jnp.dot(first_op, second_op, preferred_element_type=jnp.float32)]
    dot_general x29 -> x1, matrix products: 59 us -> 16.1 us  [against(): lax.dot_general(first_op, second_op, (((1,), (1,)), ((), ())), preferred_...]
    unnamed x403 -> x53, local copies, waits for them, and re-layouts: 52.7 us -> 11.1 us
    another operation x16 -> x1, local copies, waits for them, and re-layouts: 30.9 us -> 0.73 us  [on_device(): text_labels = (segments[:, None], segments[None, :])]
    dot_general x16 -> x0, matrix products: 24.3 us -> none  [the longest x1 6.55 us: attention(): jnp.einsum('bhqd,bhkd->bhqk', queries, keys_in, preferred_element_type=F32)]
    reshape x18 -> x0, local copies, waits for them, and re-layouts: 23.6 us -> none  [the longest x12 15.1 us: heads_last(): return array.transpose(0, 2, 1, 3).reshape(-1, HEADS * HEAD)]
    slice x11 -> x5, local copies, waits for them, and re-layouts: 22.2 us -> 3.54 us  [the longest x1 1.78 us: on_device(): last = ffn_down[1].reshape(4, rows, D).astype(BF)]
  transfers between devices with their start and end apart: 2 -> 2, of which waited for: 0 -> 0; matrix products, arithmetic and copies ran while one was open for 16% -> 3% of each run, Pallas kernels for 61% -> 75%
where the time goes in v5:
time: 998 us; the launch traced here: 989 us
  Pallas kernels  877 us (88%)
  matrix products  37.8 us (4%)
  other arithmetic  29.8 us (3%)
  local copies, waits for them, and re-layouts  29.7 us (3%)
  between operations  14.7 us (1%)
    pallas_call x1, Pallas kernels, spread(): pl.pallas_call(partial(spread_kernel, tables, count, Z, token_count), out...  322 us
    pallas_call x1, Pallas kernels, sum_products(): pl.pallas_call(partial(sum_kernel, Z, counts), out_shape=jax.ShapeDtypeSt...  301 us
    pallas_call x24, Pallas kernels, steps(): pl.pallas_call(kernel, grid=(count,), in_specs=in_specs, out_specs=out_sp...  168 us
    pallas_call x3, Pallas kernels, attention_back(): pl.pallas_call(kernel, grid=grid, in_specs=[*specs, pl.BlockSpec((rows //...  31 us
    pallas_call x3, Pallas kernels, attention(): pl.pallas_call(kernel, grid=grid, in_specs=[*specs, *marks], out_specs=pa...  20.1 us
  transfers between devices with their start and end apart: 2, of which 0 were waited for; matrix products, arithmetic and copies ran while one was open for 3% of the time, Pallas kernels for 75%

profile of v5, /device:TPU:0, one launch (start us, length us, event | category | flops | bytes accessed | tf_op | source)
XLA Modules:
  0.0 988.8 jit_solution(6587381827288293544)
XLA Ops:
  7.3 1.8 slice.61
  9.1 1.7 convert_element_type.58
  10.8 0.8 reshape.142
  11.6 0.7 fusion.11
  12.4 0.7 convert_bitcast_fusion
  13.1 1.2 copy-done.4
  14.3 1.2 copy-done.5
  15.5 1.2 copy-done.6
  16.7 1.0 copy-done.7
  17.7 321.9 %shard_map.416 = (bf16[4,2,1024,1024]{3,2,1,0:T(8,128)(2,1)}, bf16[24,4,4,2,32,1024]{5,4,3,2,1,0:T(8,128)(2,1)}, f32[4,32,1024]{2,1,0:T(8,128)S(1)}, f32[32,8,128]{2,1,0:T(8,128)S(1)}) custom-call(f32[1024,256]{1,0:T(8,128)S(1)} %copy-done.5, f32[3,32,3072]{2,1,0:T(8,128)} %refs_4_.1, f32[3,32,1024]{2,1,0:T(8,128)S(1)} %copy-done.7, ...), custom_call_target="tpu_custom_call" | custom-call | tf_op jit(solution)/shard_map/pallas_call | solution.py:904
  340.4 0.7 reshape.153.g
  341.1 10.7 %gather_fusion = bf16[512,1024]{1,0:T(8,128)(2,1)S(1)} fusion(bf16[8192,1024]{1,0:T(8,128)(2,1)} %bitcast.92, s32[1024]{0:T(1024)S(1)} %pad_clamp_fusion), kind=kCustom, calls=%fused_computation | custom fusion | bytes 2099200 | tf_op jit(solution)/shard_map/gather | solution.py:1648
  351.8 1.9 fusion.4
  354.0 1.6 pad_add_fusion
  355.6 8.5 shard_map.417
  364.1 8.7 shard_map.418.a.refs_1_
  372.8 0.7 copy.52.rest_0_
  373.6 0.9 copy.61
  375.1 0.9 fusion.6
  376.0 0.9 maximum_add_fusion.x
  376.9 5.3 shard_map.421
  382.2 5.0 shard_map.422.a.refs_14_
  387.2 3.1 shard_map.423.x
  390.3 6.8 shard_map.424
  397.1 6.1 shard_map.425.x
  403.3 2.0 shard_map.426.x
  405.2 3.5 shard_map.427.k.v
  408.7 5.1 shard_map.419.x
  413.8 4.8 shard_map.420
  418.7 6.4 shard_map.428.a.refs_3_
  425.1 5.1 shard_map.429.x
  430.2 13.5 %shard_map.430 = (bf16[512,1024]{1,0:T(8,128)(2,1)}, bf16[4,512,1024]{2,1,0:T(8,128)(2,1)}, bf16[4,512,1024]{2,1,0:T(8,128)(2,1)}) custom-call(f32[512,1024]{1,0:T(8,128)} %shard_map.429.x, f32[7,1,1024]{2,1,0:T(1,128)} %reshape.153.g, bf16[24,1024,1024]{2,1,0:T(8,128)(2,1)} %bitcast.73), custom_call_target="tpu_custom_call" | custom-call | flops 4294967296 | bytes 12582912 | tf_op jit(solution)/shard_map/pallas_call | solution.py:1205
  443.7 9.9 shard_map.431.x
  453.6 3.1 shard_map.432.refs_24_
  456.7 16.1 %fusion.12 = (f32[512]{0:T(512)S(1)}, f32[512,8192]{1,0:T(8,128)}) fusion(bf16[512,1024]{1,0:T(8,128)(2,1)} %shard_map.432.refs_24_, bf16[8192,1024]{1,0:T(8,128)(2,1)} %bitcast.93), kind=kOutput, calls=%fused_computation.42 | convolution fusion | flops 8594128896 | bytes 34605056 | tf_op jit(solution)/shard_map/dot_general | solution.py:1176
  472.8 10.2 %multiply_reduce_fusion = (f32[512]{0:T(512)S(1)}, f32[512]{0:T(512)S(1)}) fusion(f32[512,8192]{1,0:T(8,128)} %get-tuple-element.158, s32[512]{0:T(512)S(1)} %bitcast.114, f32[512]{0:T(512)S(1)} %get-tuple-element.157), kind=kLoop, calls=%fused_computation.1 | loop fusion | flops 25164800 | bytes 16785408 | tf_op jit(solution)/shard_map/reduce_sum | solution.py:1660
  483.6 5.2 multiply_convert_fusion.refs_22_
  488.8 3.2 copy-done.10
  492.1 13.6 %fusion.13.d = f32[512,1024]{1,0:T(8,128)} fusion(bf16[512,8192]{1,0:T(8,128)(2,1)S(1)} %multiply_convert_fusion.refs_22_, bf16[8192,1024]{1,0:T(8,128)(2,1)} %bitcast.94), kind=kOutput, calls=%fused_computation.43 | convolution fusion | flops 8589934592 | bytes 27262976 | tf_op jit(solution)/shard_map/dot_general | solution.py:1166
  505.7 5.2 shard_map.433
  511.0 30.9 %shard_map.434 = (bf16[4,512,1024]{2,1,0:T(8,128)(2,1)}, f32[512,1024]{1,0:T(8,128)}, bf16[512,1024]{1,0:T(8,128)(2,1)}, f32[1,1024]{1,0:T(1,128)}) custom-call(bf16[512,1024]{1,0:T(8,128)(2,1)} %get-tuple-element.99.d, bf16[4,512,1024]{2,1,0:T(8,128)(2,1)} %get-tuple-element.100.s, bf16[24,1024,1024]{2,1,0:T(8,128)(2,1)} %bitcast.74, ...), custom_call_target="tpu_custom_call" | custom-call | flops 8589934592 | bytes 16777216 | tf_op jit(solution)/shard_map/pallas_call | solution.py:1205
  541.9 4.2 shard_map.435.d
  546.0 9.3 shard_map.436
  555.4 4.2 shard_map.440.d
  559.6 2.6 shard_map.441
  562.1 11.8 %shard_map.442 = (bf16[4,128,1024]{2,1,0:T(8,128)(2,1)}, f32[128,1024]{1,0:T(8,128)}, bf16[128,1024]{1,0:T(8,128)(2,1)}, f32[1,1024]{1,0:T(1,128)}) custom-call(bf16[128,1024]{1,0:T(8,128)(2,1)} %get-tuple-element.110.d, bf16[4,128,1024]{2,1,0:T(8,128)(2,1)} %get-tuple-element.111.s, bf16[24,1024,1024]{2,1,0:T(8,128)(2,1)} %bitcast.77, ...), custom_call_target="tpu_custom_call" | custom-call | flops 2147483648 | bytes 10485760 | tf_op jit(solution)/shard_map/pallas_call | solution.py:1205
  573.9 3.2 shard_map.443.d
  577.2 6.4 shard_map.444.refs_18_.d
  583.6 6.6 shard_map.447
  590.2 1.8 multiply_convert_fusion.1
  592.0 0.9 copy.64
  592.9 0.7 fusion.9
  593.6 6.9 shard_map.437
  600.6 4.3 shard_map.438.d
  604.8 15.2 %shard_map.439.d.refs_6_ = bf16[3,512,1024]{2,1,0:T(8,128)(2,1)} custom-call(bf16[3,512,1024]{2,1,0:T(8,128)(2,1)} %get-tuple-element.90.q.k.v, bf16[3,512,1024]{2,1,0:T(8,128)(2,1)} %get-tuple-element.90.q.k.v, bf16[3,512,1024]{2,1,0:T(8,128)(2,1)} %get-tuple-element.90.q.k.v, bf16[512,1024]{1,0:T(8,128)(2,1)} %shard_map.438.d), custom_call_target="tpu_custom_call" | custom-call | tf_op jit(solution)/shard_map/pallas_call | solution.py:1494
  620.1 11.0 %shard_map.445 = (f32[512,1024]{1,0:T(8,128)}, bf16[512,1024]{1,0:T(8,128)(2,1)}, f32[1,1024]{1,0:T(1,128)}) custom-call(bf16[3,512,1024]{2,1,0:T(8,128)(2,1)} %shard_map.439.d.refs_6_, bf16[24,1024,1024]{2,1,0:T(8,128)(2,1)} %bitcast.83, f32[512,1024]{1,0:T(8,128)} %bitcast.86, f32[7,1,1024]{2,1,0:T(1,128)} %reshape.153.g, f32[512,1024]{1,0:T(8,128)} %get-tuple-element.115.above), custom_call_target="tpu_custom_call" | custom-call | flops 3221225472 | bytes 10485760 | tf_op jit(solution)/shard_map/pallas_call | solution.py:1205
  631.1 1.9 fusion.2
  633.0 1.1 pad.21
  634.1 0.7 concatenate.22
  635.1 0.7 select_bitcast_fusion
  635.8 300.6 %shard_map.446.sums.refs_1_ = f32[36,32,1024]{2,1,0:T(8,128)} custom-call(bf16[1,512,1024]{2,1,0:T(8,128)(2,1)} %bitcast.102, bf16[1,512,1024]{2,1,0:T(8,128)(2,1)} %shard_map.418.a.refs_1_, bf16[1,512,1024]{2,1,0:T(8,128)(2,1)} %bitcast.103, bf16[1,512,1024]{2,1,0:T(8,128)(2,1)} %shard_map.428.a.refs_3_, bf16[1,512,1024]{2,1,0:T(8,128)(2,1)} %bitcast.104, ...), custom_call_target="tpu_custom_call" | custom-call | tf_op jit(solution)/shard_map/pallas_call | solution.py:539
  936.4 8.1 fusion.text.refs_2_
  944.5 15.5 %shard_map.448 = (f32[8,128]{1,0:T(8,128)S(1)}, f32[8,128]{1,0:T(8,128)S(1)}) custom-call(f32[36,32,1024]{2,1,0:T(8,128)S(1)} %copy-done.2, f32[500,1024]{1,0:T(8,128)S(1)} %fusion.text.refs_2_, f32[32,8,128]{2,1,0:T(8,128)S(1)} %bitcast.61), custom_call_target="tpu_custom_call" | custom-call | tf_op jit(solution)/shard_map/pallas_call | solution.py:1112
  961.8 19.9 %shard_map.449 = (f32[3,32,3072]{2,1,0:T(8,128)}, f32[3,32,1024]{2,1,0:T(8,128)}, f32[2,32,4096]{2,1,0:T(8,128)}, f32[2,128,1024]{2,1,0:T(8,128)}, f32[7,32]{1,0...) custom-call(f32[8,128]{1,0:T(8,128)} %copy-done.8, ...), custom_call_target="tpu_custom_call" | custom-call | tf_op jit(solution)/shard_map/pallas_call | solution.py:1132
  (69 shorter events, 4.7 us)
Async XLA Ops:
  7.2 366.4 %copy-start = (s32[2]{0:T(128)S(1)}, s32[2]{0:T(128)}, u32[]{:S(2)}) copy-start(s32[2]{0:T(128)} %param.28) | copy-start | bytes 28
  7.2 436.5 %all-gather.3.cloned.1.call-start = ((), (), s32[]{:S(2)}) async-start(), calls=%async_computation | async-start | bytes 8650752 | tf_op jit(solution)/shard_map/all_gather | solution.py:1642
  9.1 927.3 %all-gather.5.cloned.1.call-start = ((), (), s32[]{:S(2)}) async-start(), calls=%async_computation.1 | async-start | bytes 8650752 | tf_op jit(solution)/shard_map/all_gather | solution.py:1677
  13.1 1.2 copy-start.4
  14.3 1.2 copy-start.5
  15.5 1.2 copy-start.6
  16.7 1.0 copy-start.7
  339.6 0.6 copy-start.11
  364.1 8.7 copy-start.15
  364.1 10.4 %copy-start.12 = (s32[2,256]{1,0:T(2,128)S(1)}, s32[2,256]{1,0:T(2,128)}, u32[]{:S(2)}) copy-start(s32[2,256]{1,0:T(2,128)} %param.27) | copy-start | bytes 6148
  456.7 16.1 %copy-start.14 = (s32[1,2,2,128]{3,1,2,0:T(2,128)S(1)}, s32[1,2,2,128]{3,1,2,0:T(2,128)}, u32[]{:S(2)}) copy-start(s32[1,2,2,128]{3,1,2,0:T(2,128)} %copy.62) | copy-start | bytes 6148
  472.8 10.8 %copy-start.9 = (f32[512,8192]{1,0:T(8,128)S(1)}, f32[512,8192]{1,0:T(8,128)}, u32[]{:S(2)}) copy-start(f32[512,8192]{1,0:T(8,128)} %get-tuple-element.158) | copy-start | bytes 50331652
  488.8 3.3 copy-start.10
  583.6 8.4 copy-start.13
  620.0 14.0 %copy-start.16 = (f32[1,1024]{1,0:T(1,128)S(1)}, f32[1,1024]{1,0:T(1,128)}, u32[]{:S(2)}) copy-start(f32[1,1024]{1,0:T(1,128)} %get-tuple-element.125) | copy-start | bytes 12292
  620.0 14.0 %copy-start.17 = (f32[1,1024]{1,0:T(1,128)S(1)}, f32[1,1024]{1,0:T(1,128)}, u32[]{:S(2)}) copy-start(f32[1,1024]{1,0:T(1,128)} %get-tuple-element.124) | copy-start | bytes 12292
  620.0 14.0 %copy-start.18 = (f32[1,1024]{1,0:T(1,128)S(1)}, f32[1,1024]{1,0:T(1,128)}, u32[]{:S(2)}) copy-start(f32[1,1024]{1,0:T(1,128)} %get-tuple-element.121) | copy-start | bytes 12292
  620.0 14.0 %copy-start.19 = (f32[1,1024]{1,0:T(1,128)S(1)}, f32[1,1024]{1,0:T(1,128)}, u32[]{:S(2)}) copy-start(f32[1,1024]{1,0:T(1,128)} %get-tuple-element.120) | copy-start | bytes 12292
  620.1 14.0 %copy-start.20 = (f32[1,1024]{1,0:T(1,128)S(1)}, f32[1,1024]{1,0:T(1,128)}, u32[]{:S(2)}) copy-start(f32[1,1024]{1,0:T(1,128)} %get-tuple-element.119) | copy-start | bytes 12292
  620.1 14.0 %copy-start.21 = (f32[1,1024]{1,0:T(1,128)S(1)}, f32[1,1024]{1,0:T(1,128)}, u32[]{:S(2)}) copy-start(f32[1,1024]{1,0:T(1,128)} %get-tuple-element.123) | copy-start | bytes 12292
  936.4 8.1 copy-start.2
  944.5 15.5 %copy-start.3 = (f32[500,1024]{1,0:T(8,128)}, f32[500,1024]{1,0:T(8,128)S(1)}, u32[]{:S(2)}) copy-start(f32[500,1024]{1,0:T(8,128)S(1)} %fusion.text.refs_2_) | copy-start | bytes 6144004
  960.0 1.8 copy-start.8
  961.2 20.5 %copy-start.1 = (s32[2]{0:T(128)S(1)}, s32[2]{0:T(128)}, u32[]{:S(2)}) copy-start(s32[2]{0:T(128)} %param.28) | copy-start | bytes 28
Sparse Core Ops, SparseCore 0:
  11.7 104.5 all-gather.2
  592.1 84.7 all-gather.4

commit v6 on v5

--- a/solution.py
+++ b/solution.py
@@ -591,9 +591,9 @@
 
 
 def spread_kernel(
-    tables, units, Z, token_count, table_f32, mix_in, mix_out, ffn_up, ffn_down, text_table, small,
-    table_out, unit_out, text_out, small_all,
-    table_ref, unit_ref, looked, own_sem, line_send, line_recv, square_send, square_recv, core_send, core_recv,
+    tables, units, Z, token_count, table_f32, mix_in, mix_out, ffn_up, ffn_down, text_table, small, codes,
+    table_out, unit_out, text_out, small_all, code_rows,
+    table_ref, unit_ref, looked, chunk, chunk_sem, own_sem, line_send, line_recv, square_send, square_recv, core_send, core_recv,
     small_send, small_recv, text_sem, *sum_refs,
 ):
     dp, fs = lax.axis_index("dp"), lax.axis_index("fsdp")
@@ -812,22 +812,24 @@
     scratch, semaphores = sum_refs[:9], sum_refs[9:]
     own_slots, depth = scratch[0].shape[0], scratch[1].shape[0]
 
-    def look_up():
-        each(lambda i: small_copy(i).wait())
+    look_ups, text_first = 8, 9
+
+    def look_up(part):
         owned_rows = text_table.shape[0]
         base = me * token_count
 
-        def of_device(device, carry):
-            ids = small_all[device][:1]
-            row = lax.broadcasted_iota(jnp.int32, (owned_rows, ids.shape[1]), 0)
+        def of_device(i, carry):
+            device = part * (size // look_ups) + i
+            ids = small_all[device].T[:, :1]
+            row = lax.broadcasted_iota(jnp.int32, (ids.shape[0], owned_rows), 1)
             hit = (row + base == ids.astype(jnp.int32)) & (row < token_count)
-            found = across(jnp.where(hit, 1.0, 0.0).astype(BF), text_table[...]).astype(BF)
+            found = matmul(jnp.where(hit, 1.0, 0.0).astype(BF), text_table[...]).astype(BF)
             dp_at, line_at, core_at = device // inner, lax.rem(device, inner) // 2, lax.rem(device, 2)
             for u in range(looked.shape[0]):
                 looked[u, dp_at, line_at, core_at] = found[u * rows : (u + 1) * rows]
             return carry
 
-        lax.fori_loop(0, size, of_device, 0)
+        lax.fori_loop(0, size // look_ups, of_device, 0)
 
     def text_own(k):
         return pltpu.make_async_copy(
@@ -850,10 +852,28 @@
 
     text_stages = [text_begin] + sum_stages(Z, scratch, semaphores, text_arrive, text_out)[0]
 
-    text_first = 3
+    code_first = (n_stages - 1) * LAG + 1
+
+    def chunk_copy(k):
+        source = table_out.at[:, :, pl.ds(k * table_rows, table_rows), :]
+        return pltpu.make_async_copy(source, chunk.at[k % 2], chunk_sem.at[k % 2])
+
+    def find_codes(k):
+        chunk_copy(k).wait()
+        pl.when(k + 1 < tables)(lambda: chunk_copy(k + 1).start())
+        place = lax.broadcasted_iota(jnp.int32, (codes.shape[0], inner * table_rows), 1)
+        code = (place // table_rows) * table_out.shape[2] + k * table_rows + place % table_rows
+        hit = jnp.where(codes[...] == code, 1.0, 0.0).astype(BF)
+        code_rows[...] += matmul(hit, chunk[k % 2].reshape(-1, chunk.shape[-1]))
+
+    code_rows[...] = jnp.zeros_like(code_rows)
 
     def loop_step(j, carry):
-        pl.when(j == text_first)(look_up)
+        @pl.when(j == 1)
+        def _():
+            each(lambda i: small_copy(i).wait())
+
+        pl.when((j >= 1) & (j < 1 + look_ups))(lambda: look_up(j - 1))
         for place in reversed(range(n_stages)):
             k = j - place * LAG
             turn = k - text_first
@@ -868,12 +888,19 @@
                 def _(k=k, run=stages[place]):
                     run(k)
 
+        found = j - code_first
+
+        @pl.when(found == -1)
+        def _():
+            chunk_copy(0).start()
+
+        pl.when((found >= 0) & (found < tables))(lambda: find_codes(found))
         return carry
 
     lax.fori_loop(0, total + (n_stages - 1) * LAG, loop_step, 0)
 
 
-def spread(table, weights, text_table, small, call_id):
+def spread(table, weights, text_table, small, codes, call_id):
     mix_in, mix_out, ffn_up, ffn_down = weights
     dp_size, fsdp_size = lax.axis_size("dp"), lax.axis_size("fsdp")
     m, Z = mix_in.shape[1], fsdp_size // 2
@@ -896,25 +923,29 @@
         owned = (ids[:, None] - base == jnp.arange(count)[None, :]).astype(BF)
         looked = matmul(owned, text_table.astype(BF)).astype(BF)
         text = lax.psum_scatter(looked, AXES, scatter_dimension=0, tiled=True).astype(F32)
-        return whole, units, text, small_all
+        found = jnp.where(codes[:, None] >= 0, whole[jnp.maximum(codes, 0)].astype(F32), 0.0)
+        return whole, units, text, small_all, found
     text_units, token_count = TXT_LEN // m, text_table.shape[0]
     text_table = jnp.pad(text_table.astype(BF), ((0, -token_count % 128), (0, 0)))
     tables, count, dma = 8, 24, pltpu.SemaphoreType.DMA
     total = tables + count
-    whole, units, text, small_all = pl.pallas_call(
+    whole, units, text, small_all, found = pl.pallas_call(
         partial(spread_kernel, tables, count, Z, token_count),
         out_shape=(
             jax.ShapeDtypeStruct((Z, 2, table.shape[0], 4 * table.shape[1]), BF),
             jax.ShapeDtypeStruct((count, 4, Z, 2, m, D), BF),
             jax.ShapeDtypeStruct((text_units, m, D), F32),
             jax.ShapeDtypeStruct((8 * Z, *small.shape), F32),
+            jax.ShapeDtypeStruct((codes.shape[0], D), F32),
         ),
-        in_specs=[pl.BlockSpec(memory_space=pltpu.VMEM)] * 7,
-        out_specs=[pl.BlockSpec(memory_space=pl.ANY)] * 2 + [pl.BlockSpec(memory_space=pltpu.VMEM)] * 2,
+        in_specs=[pl.BlockSpec(memory_space=pltpu.VMEM)] * 8,
+        out_specs=[pl.BlockSpec(memory_space=pl.ANY)] * 2 + [pl.BlockSpec(memory_space=pltpu.VMEM)] * 3,
         scratch_shapes=[
             pltpu.VMEM(table.shape, BF),
             pltpu.VMEM((count, m, D), BF),
             pltpu.VMEM((text_units, 4, Z, 2, m, D), BF),
+            pltpu.VMEM((2, Z, 2, table.shape[0] // tables, D), BF),
+            dma((2,)),
             dma((2,)),
             dma((2, Z - 1, total)),
             dma((2, Z - 1, total)),
@@ -931,8 +962,9 @@
         compiler_params=pltpu.CompilerParams(
             collective_id=call_id, has_side_effects=True, vmem_limit_bytes=48 << 20
         ),
-    )(table, *weights, text_table, small)
-    return whole.reshape(-1, 4 * table.shape[1]), units.reshape(count, -1, D), text.reshape(-1, D), small_all
+    )(table, *weights, text_table, small, codes[:, None])
+    whole, units = whole.reshape(-1, 4 * table.shape[1]), units.reshape(count, -1, D)
+    return whole, units, text.reshape(-1, D), small_all, found
 
 
 def exchange_kernel(size, inner, in_ref, out_ref, send_sem, recv_sem):
@@ -1386,10 +1418,8 @@
         def _():
             total[...] = jnp.zeros_like(total)
 
-        for start in range(0, rows, 128):
-            at = pl.ds(start, 128)
-            hidden[0, at] = (against(d[at], down[0]) * s[0, at].astype(F32)).astype(BF)
-            total[at] += against(hidden[0, at], up[0])
+        hidden[0] = (against(d[...], down[0]) * s[0].astype(F32)).astype(BF)
+        total[...] += against(hidden[0], up[0])
 
         @pl.when(pl.program_id(0) == 3)
         def _():
@@ -1628,8 +1658,9 @@
     cross_labels = (jnp.repeat(caption_of, IMG_LEN)[:, None], segments[None, :])
 
     small = tiles(jnp.concatenate([text_ids[0].astype(F32), norm_gains.reshape(-1)]), 1)[0]
-    code_full, units, text_rows, small = spread(
-        code_table, (mix_in, mix_out, ffn_up, ffn_down), text_table, small, 4
+    before = jnp.pad(codes[:, :-1], ((0, 0), (1, 0)), constant_values=-1).reshape(-1)
+    code_full, units, text_rows, small, image_rows = spread(
+        code_table, (mix_in, mix_out, ffn_up, ffn_down), text_table, small, before, 4
     )
     small = small.reshape(devices, 1024)[:, : TXT_LEN + 7 * norm_gains.shape[1]]
     all_ids = small[:, :TXT_LEN].astype(jnp.int32).reshape(-1)
@@ -1645,9 +1676,8 @@
     dec_gains = [(gains, i) for i in range(3, 7)]
     memory, enc_stored = layer_forward(text_in, units, 0, units, 8, enc_gains, 1, text_labels, None, None)
 
-    image_rows = code_full[codes].astype(F32) * scale_in
-    shifted = jnp.concatenate([jnp.zeros_like(image_rows[:, :1]), image_rows[:, :-1]], axis=1)
-    image_in = (shifted + positions(IMG_LEN, D)[None]).reshape(-1, D)
+    image_in = image_rows.reshape(image_count, IMG_LEN, D) * scale_in + positions(IMG_LEN, D)[None]
+    image_in = image_in.reshape(-1, D)
     final_out, dec_stored = layer_forward(
         image_in, units, 12, down_units, 0, dec_gains, image_count, None, memory, cross_labels
     )

time: 998 us -> 978 us (0.980)
  Pallas kernels: 877 us -> 865 us
    pallas_call x24, Pallas kernels: 168 us -> 155 us  [steps(): pl.pallas_call(kernel, grid=(count,), in_specs=in_specs, out_specs=out_sp...]
    gather x1 -> x0, local copies, waits for them, and re-layouts: 10.7 us -> none  [on_device(): image_rows = code_full[codes].astype(F32) * scale_in]
  transfers between devices with their start and end apart: 2 -> 2, of which waited for: 0 -> 0; matrix products, arithmetic and copies ran while one was open for 3% -> 2% of each run, Pallas kernels for 75% -> 77%
where the time goes in v6:
time: 978 us; the launch traced here: 968 us
  Pallas kernels  865 us (88%)
  matrix products  37.9 us (4%)
  other arithmetic  30.5 us (3%)
  local copies, waits for them, and re-layouts  19.9 us (2%)
  between operations  14.9 us (2%)
    pallas_call x1, Pallas kernels, spread(): pl.pallas_call(partial(spread_kernel, tables, count, Z, token_count), out...  323 us
    pallas_call x1, Pallas kernels, sum_products(): pl.pallas_call(partial(sum_kernel, Z, counts), out_shape=jax.ShapeDtypeSt...  300 us
    pallas_call x24, Pallas kernels, steps(): pl.pallas_call(kernel, grid=(count,), in_specs=in_specs, out_specs=out_sp...  155 us
    pallas_call x3, Pallas kernels, attention_back(): pl.pallas_call(kernel, grid=grid, in_specs=[*specs, pl.BlockSpec((rows //...  30.7 us
    pallas_call x3, Pallas kernels, attention(): pl.pallas_call(kernel, grid=grid, in_specs=[*specs, *marks], out_specs=pa...  19.9 us
    pallas_call x1, Pallas kernels, update(): pl.pallas_call(update_kernel, out_shape=shapes * 3, in_specs=[in_vmem] *...  19.9 us
  transfers between devices with their start and end apart: 2, of which 0 were waited for; matrix products, arithmetic and copies ran while one was open for 2% of the time, Pallas kernels for 77%

profile of v6, /device:TPU:0, one launch (start us, length us, event | category | flops | bytes accessed | tf_op | source)
XLA Modules:
  0.0 968.2 jit_solution(5624989455804663363)
XLA Ops:
  7.3 1.8 slice.58
  9.1 1.7 convert_element_type.55
  10.8 0.8 reshape.142
  11.6 0.8 pad_bitcast_fusion
  12.6 0.7 convert_bitcast_fusion
  13.3 1.2 copy-done.4
  14.5 1.2 copy-done.5
  15.7 1.2 copy-done.6
  17.0 1.0 copy-done.7
  18.0 322.9 %shard_map.416 = (bf16[4,2,1024,1024]{3,2,1,0:T(8,128)(2,1)}, bf16[24,4,4,2,32,1024]{5,4,3,2,1,0:T(8,128)(2,1)}, f32[4,32,1024]{2,1,0:T(8,128)S(1)}, f32[32,8,128]{2,1,0:T(8,128)S(1)}, f32[512,1024]{1,0:T(8,128)}) custom-call(f32[1024,256]{1,0:T(8,128)S(1)} %copy-done.5, f32[3,32,3072]{2,1,0:T(8,128)} %refs_4_.1, f32[3,32,1024]{2,1,0:T(8,128)S(1)} %copy-done.7, ...), custom_call_target="tpu_custom_call" | custom-call | tf_op jit(solution)/shard_map/pallas_call | solution.py:932
  340.9 0.6 copy-done.11
  341.7 0.7 reshape.152.g
  342.4 1.9 fusion.4
  344.3 3.3 bitcast_add_fusion.x
  347.6 8.3 shard_map.417
  355.9 8.9 shard_map.418.a.refs_1_
  364.8 0.7 copy.53.rest_0_
  365.6 0.9 copy.63
  367.0 0.9 fusion.6
  368.0 0.9 maximum_add_fusion.x
  368.8 5.3 shard_map.421
  374.1 5.0 shard_map.422.a.refs_14_
  379.2 3.1 shard_map.423.x
  382.3 6.8 shard_map.424
  389.1 6.1 shard_map.425.x
  395.2 2.0 shard_map.426.x
  397.2 3.5 shard_map.427.k.v
  400.6 5.1 shard_map.419.x
  405.8 4.8 shard_map.420
  410.6 6.0 shard_map.428.a.refs_3_
  416.6 5.1 shard_map.429.x
  421.8 13.7 %shard_map.430 = (bf16[512,1024]{1,0:T(8,128)(2,1)}, bf16[4,512,1024]{2,1,0:T(8,128)(2,1)}, bf16[4,512,1024]{2,1,0:T(8,128)(2,1)}) custom-call(f32[512,1024]{1,0:T(8,128)} %shard_map.429.x, f32[7,1,1024]{2,1,0:T(1,128)} %reshape.152.g, bf16[24,1024,1024]{2,1,0:T(8,128)(2,1)} %bitcast.76), custom_call_target="tpu_custom_call" | custom-call | flops 4294967296 | bytes 12582912 | tf_op jit(solution)/shard_map/pallas_call | solution.py:1237
  435.5 9.9 %shard_map.431.x = f32[512,1024]{1,0:T(8,128)} custom-call(f32[512,1024]{1,0:T(8,128)} %shard_map.429.x, bf16[4,512,1024]{2,1,0:T(8,128)(2,1)} %get-tuple-element.98.a.refs_5_, bf16[4,1024,1024]{2,1,0:T(8,128)(2,1)} %all-gather.3.cloned.1.call-done.w.down), custom_call_target="tpu_custom_call" | custom-call | flops 4294967296 | bytes 12582912 | tf_op jit(solution)/shard_map/pallas_call | solution.py:1237
  445.4 3.1 shard_map.432.refs_24_
  448.5 16.1 %fusion.11 = (f32[512]{0:T(512)S(1)}, f32[512,8192]{1,0:T(8,128)}) fusion(bf16[512,1024]{1,0:T(8,128)(2,1)} %shard_map.432.refs_24_, bf16[8192,1024]{1,0:T(8,128)(2,1)} %bitcast.117), kind=kOutput, calls=%fused_computation.38 | convolution fusion | flops 8594128896 | bytes 34605056 | tf_op jit(solution)/shard_map/dot_general | solution.py:1208
  464.5 10.2 %multiply_reduce_fusion = (f32[512]{0:T(512)S(1)}, f32[512]{0:T(512)S(1)}) fusion(f32[512,8192]{1,0:T(8,128)} %get-tuple-element.160, s32[512]{0:T(512)S(1)} %bitcast.111, f32[512]{0:T(512)S(1)} %get-tuple-element.159), kind=kLoop, calls=%fused_computation | loop fusion | flops 25164800 | bytes 16785408 | tf_op jit(solution)/shard_map/reduce_sum | solution.py:1690
  475.4 5.2 multiply_convert_fusion.refs_22_
  480.6 3.2 copy-done.10
  483.8 13.7 %fusion.12.d = f32[512,1024]{1,0:T(8,128)} fusion(bf16[512,8192]{1,0:T(8,128)(2,1)S(1)} %multiply_convert_fusion.refs_22_, bf16[8192,1024]{1,0:T(8,128)(2,1)} %bitcast.118), kind=kOutput, calls=%fused_computation.39 | convolution fusion | flops 8589934592 | bytes 27262976 | tf_op jit(solution)/shard_map/dot_general | solution.py:1198
  497.6 5.2 shard_map.433
  502.8 18.5 %shard_map.434 = (bf16[4,512,1024]{2,1,0:T(8,128)(2,1)}, f32[512,1024]{1,0:T(8,128)}, bf16[512,1024]{1,0:T(8,128)(2,1)}, f32[1,1024]{1,0:T(1,128)}) custom-call(bf16[512,1024]{1,0:T(8,128)(2,1)} %get-tuple-element.101.d, bf16[4,512,1024]{2,1,0:T(8,128)(2,1)} %get-tuple-element.102.s, bf16[24,1024,1024]{2,1,0:T(8,128)(2,1)} %bitcast.77, ...), custom_call_target="tpu_custom_call" | custom-call | flops 8589934592 | bytes 16777216 | tf_op jit(solution)/shard_map/pallas_call | solution.py:1237
  521.4 4.2 shard_map.435.d
  525.5 9.3 shard_map.436
  534.8 4.2 shard_map.440.d
  539.0 2.6 shard_map.441
  541.6 11.8 %shard_map.442 = (bf16[4,128,1024]{2,1,0:T(8,128)(2,1)}, f32[128,1024]{1,0:T(8,128)}, bf16[128,1024]{1,0:T(8,128)(2,1)}, f32[1,1024]{1,0:T(1,128)}) custom-call(bf16[128,1024]{1,0:T(8,128)(2,1)} %get-tuple-element.112.d, bf16[4,128,1024]{2,1,0:T(8,128)(2,1)} %get-tuple-element.113.s, bf16[24,1024,1024]{2,1,0:T(8,128)(2,1)} %bitcast.80, ...), custom_call_target="tpu_custom_call" | custom-call | flops 2147483648 | bytes 10485760 | tf_op jit(solution)/shard_map/pallas_call | solution.py:1237
  553.4 3.2 shard_map.443.d
  556.6 6.4 shard_map.444.refs_18_.d
  563.0 6.6 shard_map.447
  569.6 1.8 multiply_convert_fusion.1
  571.5 0.9 copy.66
  572.3 0.7 fusion.9
  573.1 6.9 shard_map.437
  580.0 4.3 shard_map.438.d
  584.3 15.0 %shard_map.439.d.refs_6_ = bf16[3,512,1024]{2,1,0:T(8,128)(2,1)} custom-call(bf16[3,512,1024]{2,1,0:T(8,128)(2,1)} %get-tuple-element.91.q.k.v, bf16[3,512,1024]{2,1,0:T(8,128)(2,1)} %get-tuple-element.91.q.k.v, bf16[3,512,1024]{2,1,0:T(8,128)(2,1)} %get-tuple-element.91.q.k.v, bf16[512,1024]{1,0:T(8,128)(2,1)} %shard_map.438.d), custom_call_target="tpu_custom_call" | custom-call | tf_op jit(solution)/shard_map/pallas_call | solution.py:1524
  599.3 11.0 %shard_map.445 = (f32[512,1024]{1,0:T(8,128)}, bf16[512,1024]{1,0:T(8,128)(2,1)}, f32[1,1024]{1,0:T(1,128)}) custom-call(bf16[3,512,1024]{2,1,0:T(8,128)(2,1)} %shard_map.439.d.refs_6_, bf16[24,1024,1024]{2,1,0:T(8,128)(2,1)} %bitcast.86, f32[512,1024]{1,0:T(8,128)} %bitcast_add_fusion.x, f32[7,1,1024]{2,1,0:T(1,128)} %reshape.152.g, ...), custom_call_target="tpu_custom_call" | custom-call | flops 3221225472 | bytes 10485760 | tf_op jit(solution)/shard_map/pallas_call | solution.py:1237
  610.4 1.9 fusion.2
  612.3 1.1 pad.25
  613.3 0.7 concatenate.18
  614.3 0.7 select_bitcast_fusion
  615.0 300.2 %shard_map.446.sums.refs_1_ = f32[36,32,1024]{2,1,0:T(8,128)} custom-call(bf16[1,512,1024]{2,1,0:T(8,128)(2,1)} %bitcast.98, bf16[1,512,1024]{2,1,0:T(8,128)(2,1)} %shard_map.418.a.refs_1_, bf16[1,512,1024]{2,1,0:T(8,128)(2,1)} %bitcast.99, bf16[1,512,1024]{2,1,0:T(8,128)(2,1)} %shard_map.428.a.refs_3_, bf16[1,512,1024]{2,1,0:T(8,128)(2,1)} %bitcast.100, ...), custom_call_target="tpu_custom_call" | custom-call | tf_op jit(solution)/shard_map/pallas_call | solution.py:539
  915.3 8.1 fusion.text.refs_2_
  923.4 15.7 %shard_map.448 = (f32[8,128]{1,0:T(8,128)S(1)}, f32[8,128]{1,0:T(8,128)S(1)}) custom-call(f32[36,32,1024]{2,1,0:T(8,128)S(1)} %copy-done.2, f32[500,1024]{1,0:T(8,128)S(1)} %fusion.text.refs_2_, f32[32,8,128]{2,1,0:T(8,128)S(1)} %bitcast.64), custom_call_target="tpu_custom_call" | custom-call | tf_op jit(solution)/shard_map/pallas_call | solution.py:1144
  940.9 19.9 %shard_map.449 = (f32[3,32,3072]{2,1,0:T(8,128)}, f32[3,32,1024]{2,1,0:T(8,128)}, f32[2,32,4096]{2,1,0:T(8,128)}, f32[2,128,1024]{2,1,0:T(8,128)}, f32[7,32]{1,0...) custom-call(f32[8,128]{1,0:T(8,128)} %copy-done.8, ...), custom_call_target="tpu_custom_call" | custom-call | tf_op jit(solution)/shard_map/pallas_call | solution.py:1164
  (67 shorter events, 4.0 us)
Async XLA Ops:
  7.2 358.3 %copy-start = (s32[2]{0:T(128)S(1)}, s32[2]{0:T(128)}, u32[]{:S(2)}) copy-start(s32[2]{0:T(128)} %param.28) | copy-start | bytes 28
  7.2 428.3 %all-gather.3.cloned.1.call-start = ((), (), s32[]{:S(2)}) async-start(), calls=%async_computation | async-start | bytes 8650752 | tf_op jit(solution)/shard_map/all_gather | solution.py:1673
  9.1 906.2 %all-gather.5.cloned.1.call-start = ((), (), s32[]{:S(2)}) async-start(), calls=%async_computation.1 | async-start | bytes 8650752 | tf_op jit(solution)/shard_map/all_gather | solution.py:1707
  13.3 1.2 copy-start.4
  14.5 1.2 copy-start.5
  15.7 1.2 copy-start.6
  17.0 1.0 copy-start.7
  340.9 0.6 copy-start.11
  355.9 8.9 copy-start.15
  355.9 10.6 %copy-start.12 = (s32[2,256]{1,0:T(2,128)S(1)}, s32[2,256]{1,0:T(2,128)}, u32[]{:S(2)}) copy-start(s32[2,256]{1,0:T(2,128)} %param.27) | copy-start | bytes 6148
  448.5 16.1 %copy-start.14 = (s32[1,2,2,128]{3,1,2,0:T(2,128)S(1)}, s32[1,2,2,128]{3,1,2,0:T(2,128)}, u32[]{:S(2)}) copy-start(s32[1,2,2,128]{3,1,2,0:T(2,128)} %copy.64) | copy-start | bytes 6148
  464.5 10.8 %copy-start.9 = (f32[512,8192]{1,0:T(8,128)S(1)}, f32[512,8192]{1,0:T(8,128)}, u32[]{:S(2)}) copy-start(f32[512,8192]{1,0:T(8,128)} %get-tuple-element.160) | copy-start | bytes 50331652
  480.6 3.3 copy-start.10
  563.0 8.4 copy-start.13
  599.3 14.0 %copy-start.16 = (f32[1,1024]{1,0:T(1,128)S(1)}, f32[1,1024]{1,0:T(1,128)}, u32[]{:S(2)}) copy-start(f32[1,1024]{1,0:T(1,128)} %get-tuple-element.127) | copy-start | bytes 12292
  599.3 14.0 %copy-start.17 = (f32[1,1024]{1,0:T(1,128)S(1)}, f32[1,1024]{1,0:T(1,128)}, u32[]{:S(2)}) copy-start(f32[1,1024]{1,0:T(1,128)} %get-tuple-element.126) | copy-start | bytes 12292
  599.3 14.0 %copy-start.18 = (f32[1,1024]{1,0:T(1,128)S(1)}, f32[1,1024]{1,0:T(1,128)}, u32[]{:S(2)}) copy-start(f32[1,1024]{1,0:T(1,128)} %get-tuple-element.123) | copy-start | bytes 12292
  599.3 14.0 %copy-start.19 = (f32[1,1024]{1,0:T(1,128)S(1)}, f32[1,1024]{1,0:T(1,128)}, u32[]{:S(2)}) copy-start(f32[1,1024]{1,0:T(1,128)} %get-tuple-element.122) | copy-start | bytes 12292
  599.3 14.0 %copy-start.20 = (f32[1,1024]{1,0:T(1,128)S(1)}, f32[1,1024]{1,0:T(1,128)}, u32[]{:S(2)}) copy-start(f32[1,1024]{1,0:T(1,128)} %get-tuple-element.121) | copy-start | bytes 12292
  599.3 14.0 %copy-start.21 = (f32[1,1024]{1,0:T(1,128)S(1)}, f32[1,1024]{1,0:T(1,128)}, u32[]{:S(2)}) copy-start(f32[1,1024]{1,0:T(1,128)} %get-tuple-element.125) | copy-start | bytes 12292
  915.3 8.1 copy-start.2
  923.4 15.8 %copy-start.3 = (f32[500,1024]{1,0:T(8,128)}, f32[500,1024]{1,0:T(8,128)S(1)}, u32[]{:S(2)}) copy-start(f32[500,1024]{1,0:T(8,128)S(1)} %fusion.text.refs_2_) | copy-start | bytes 6144004
  939.1 1.8 copy-start.8
  940.3 20.5 %copy-start.1 = (s32[2]{0:T(128)S(1)}, s32[2]{0:T(128)}, u32[]{:S(2)}) copy-start(s32[2]{0:T(128)} %param.28) | copy-start | bytes 28
Sparse Core Ops, SparseCore 0:
  11.7 108.0 all-gather.2
  571.6 84.8 all-gather.4

commit v7 on v6

--- a/solution.py
+++ b/solution.py
@@ -812,7 +812,8 @@
     scratch, semaphores = sum_refs[:9], sum_refs[9:]
     own_slots, depth = scratch[0].shape[0], scratch[1].shape[0]
 
-    look_ups, text_first = 8, 9
+    small_turn, look_ups = 9, 8
+    text_first = small_turn + look_ups
 
     def look_up(part):
         owned_rows = text_table.shape[0]
@@ -869,11 +870,11 @@
     code_rows[...] = jnp.zeros_like(code_rows)
 
     def loop_step(j, carry):
-        @pl.when(j == 1)
+        @pl.when(j == small_turn)
         def _():
             each(lambda i: small_copy(i).wait())
 
-        pl.when((j >= 1) & (j < 1 + look_ups))(lambda: look_up(j - 1))
+        pl.when((j >= small_turn) & (j < text_first))(lambda: look_up(j - small_turn))
         for place in reversed(range(n_stages)):
             k = j - place * LAG
             turn = k - text_first

time: 978 us -> 985 us (level)
  no operation moved by 1% of the time
where the time goes in v7:
time: 985 us; the launch traced here: 976 us
  Pallas kernels  872 us (89%)
  matrix products  37.9 us (4%)
  other arithmetic  30.5 us (3%)
  local copies, waits for them, and re-layouts  19.9 us (2%)
  between operations  14.9 us (2%)
    pallas_call x1, Pallas kernels, spread(): pl.pallas_call(partial(spread_kernel, tables, count, Z, token_count), out...  331 us
    pallas_call x1, Pallas kernels, sum_products(): pl.pallas_call(partial(sum_kernel, Z, counts), out_shape=jax.ShapeDtypeSt...  299 us
    pallas_call x24, Pallas kernels, steps(): pl.pallas_call(kernel, grid=(count,), in_specs=in_specs, out_specs=out_sp...  155 us
    pallas_call x3, Pallas kernels, attention_back(): pl.pallas_call(kernel, grid=grid, in_specs=[*specs, pl.BlockSpec((rows //...  30.7 us
    pallas_call x3, Pallas kernels, attention(): pl.pallas_call(kernel, grid=grid, in_specs=[*specs, *marks], out_specs=pa...  19.9 us
    pallas_call x1, Pallas kernels, update(): pl.pallas_call(update_kernel, out_shape=shapes * 3, in_specs=[in_vmem] *...  19.9 us
  transfers between devices with their start and end apart: 2, of which 0 were waited for; matrix products, arithmetic and copies ran while one was open for 2% of the time, Pallas kernels for 77%

profile of v7, /device:TPU:0, one launch (start us, length us, event | category | flops | bytes accessed | tf_op | source)
XLA Modules:
  0.0 975.5 jit_solution(17800932101190884601)
XLA Ops:
  7.3 1.8 slice.58
  9.1 1.7 convert_element_type.55
  10.8 0.8 reshape.142
  11.6 0.8 pad_bitcast_fusion
  12.6 0.7 convert_bitcast_fusion
  13.3 1.2 copy-done.4
  14.5 1.2 copy-done.5
  15.7 1.2 copy-done.6
  17.0 1.0 copy-done.7
  18.0 331.5 %shard_map.416 = (bf16[4,2,1024,1024]{3,2,1,0:T(8,128)(2,1)}, bf16[24,4,4,2,32,1024]{5,4,3,2,1,0:T(8,128)(2,1)}, f32[4,32,1024]{2,1,0:T(8,128)S(1)}, f32[32,8,128]{2,1,0:T(8,128)S(1)}, f32[512,1024]{1,0:T(8,128)}) custom-call(f32[1024,256]{1,0:T(8,128)S(1)} %copy-done.5, f32[3,32,3072]{2,1,0:T(8,128)} %refs_4_.1, f32[3,32,1024]{2,1,0:T(8,128)S(1)} %copy-done.7, ...), custom_call_target="tpu_custom_call" | custom-call | tf_op jit(solution)/shard_map/pallas_call | solution.py:933
  349.5 0.6 copy-done.11
  350.2 0.7 reshape.152.g
  350.9 1.9 fusion.4
  352.9 3.3 bitcast_add_fusion.x
  356.2 8.3 shard_map.417
  364.4 8.9 shard_map.418.a.refs_1_
  373.3 0.7 copy.53.rest_0_
  374.1 0.9 copy.63
  375.6 0.9 fusion.6
  376.5 0.9 maximum_add_fusion.x
  377.4 5.3 shard_map.421
  382.7 5.0 shard_map.422.a.refs_14_
  387.7 3.1 shard_map.423.x
  390.8 6.8 shard_map.424
  397.6 6.1 shard_map.425.x
  403.8 2.0 shard_map.426.x
  405.7 3.5 shard_map.427.k.v
  409.2 5.1 shard_map.419.x
  414.3 4.8 shard_map.420
  419.2 6.0 shard_map.428.a.refs_3_
  425.2 5.1 shard_map.429.x
  430.3 13.7 %shard_map.430 = (bf16[512,1024]{1,0:T(8,128)(2,1)}, bf16[4,512,1024]{2,1,0:T(8,128)(2,1)}, bf16[4,512,1024]{2,1,0:T(8,128)(2,1)}) custom-call(f32[512,1024]{1,0:T(8,128)} %shard_map.429.x, f32[7,1,1024]{2,1,0:T(1,128)} %reshape.152.g, bf16[24,1024,1024]{2,1,0:T(8,128)(2,1)} %bitcast.76), custom_call_target="tpu_custom_call" | custom-call | flops 4294967296 | bytes 12582912 | tf_op jit(solution)/shard_map/pallas_call | solution.py:1238
  444.1 9.9 %shard_map.431.x = f32[512,1024]{1,0:T(8,128)} custom-call(f32[512,1024]{1,0:T(8,128)} %shard_map.429.x, bf16[4,512,1024]{2,1,0:T(8,128)(2,1)} %get-tuple-element.98.a.refs_5_, bf16[4,1024,1024]{2,1,0:T(8,128)(2,1)} %all-gather.3.cloned.1.call-done.w.down), custom_call_target="tpu_custom_call" | custom-call | flops 4294967296 | bytes 12582912 | tf_op jit(solution)/shard_map/pallas_call | solution.py:1238
  453.9 3.1 shard_map.432.refs_24_
  457.1 16.1 %fusion.11 = (f32[512]{0:T(512)S(1)}, f32[512,8192]{1,0:T(8,128)}) fusion(bf16[512,1024]{1,0:T(8,128)(2,1)} %shard_map.432.refs_24_, bf16[8192,1024]{1,0:T(8,128)(2,1)} %bitcast.117), kind=kOutput, calls=%fused_computation.38 | convolution fusion | flops 8594128896 | bytes 34605056 | tf_op jit(solution)/shard_map/dot_general | solution.py:1209
  473.1 10.2 %multiply_reduce_fusion = (f32[512]{0:T(512)S(1)}, f32[512]{0:T(512)S(1)}) fusion(f32[512,8192]{1,0:T(8,128)} %get-tuple-element.160, s32[512]{0:T(512)S(1)} %bitcast.111, f32[512]{0:T(512)S(1)} %get-tuple-element.159), kind=kLoop, calls=%fused_computation | loop fusion | flops 25164800 | bytes 16785408 | tf_op jit(solution)/shard_map/reduce_sum | solution.py:1691
  483.9 5.2 multiply_convert_fusion.refs_22_
  489.2 3.2 copy-done.10
  492.4 13.7 %fusion.12.d = f32[512,1024]{1,0:T(8,128)} fusion(bf16[512,8192]{1,0:T(8,128)(2,1)S(1)} %multiply_convert_fusion.refs_22_, bf16[8192,1024]{1,0:T(8,128)(2,1)} %bitcast.118), kind=kOutput, calls=%fused_computation.39 | convolution fusion | flops 8589934592 | bytes 27262976 | tf_op jit(solution)/shard_map/dot_general | solution.py:1199
  506.2 5.2 shard_map.433
  511.4 18.5 %shard_map.434 = (bf16[4,512,1024]{2,1,0:T(8,128)(2,1)}, f32[512,1024]{1,0:T(8,128)}, bf16[512,1024]{1,0:T(8,128)(2,1)}, f32[1,1024]{1,0:T(1,128)}) custom-call(bf16[512,1024]{1,0:T(8,128)(2,1)} %get-tuple-element.101.d, bf16[4,512,1024]{2,1,0:T(8,128)(2,1)} %get-tuple-element.102.s, bf16[24,1024,1024]{2,1,0:T(8,128)(2,1)} %bitcast.77, ...), custom_call_target="tpu_custom_call" | custom-call | flops 8589934592 | bytes 16777216 | tf_op jit(solution)/shard_map/pallas_call | solution.py:1238
  529.9 4.2 shard_map.435.d
  534.1 9.3 shard_map.436
  543.4 4.2 shard_map.440.d
  547.6 2.6 shard_map.441
  550.2 11.8 %shard_map.442 = (bf16[4,128,1024]{2,1,0:T(8,128)(2,1)}, f32[128,1024]{1,0:T(8,128)}, bf16[128,1024]{1,0:T(8,128)(2,1)}, f32[1,1024]{1,0:T(1,128)}) custom-call(bf16[128,1024]{1,0:T(8,128)(2,1)} %get-tuple-element.112.d, bf16[4,128,1024]{2,1,0:T(8,128)(2,1)} %get-tuple-element.113.s, bf16[24,1024,1024]{2,1,0:T(8,128)(2,1)} %bitcast.80, ...), custom_call_target="tpu_custom_call" | custom-call | flops 2147483648 | bytes 10485760 | tf_op jit(solution)/shard_map/pallas_call | solution.py:1238
  562.0 3.2 shard_map.443.d
  565.2 6.4 shard_map.444.refs_18_.d
  571.6 6.6 shard_map.447
  578.2 1.8 multiply_convert_fusion.1
  580.1 0.9 copy.66
  580.9 0.7 fusion.9
  581.6 6.9 shard_map.437
  588.6 4.2 shard_map.438.d
  592.8 15.0 %shard_map.439.d.refs_6_ = bf16[3,512,1024]{2,1,0:T(8,128)(2,1)} custom-call(bf16[3,512,1024]{2,1,0:T(8,128)(2,1)} %get-tuple-element.91.q.k.v, bf16[3,512,1024]{2,1,0:T(8,128)(2,1)} %get-tuple-element.91.q.k.v, bf16[3,512,1024]{2,1,0:T(8,128)(2,1)} %get-tuple-element.91.q.k.v, bf16[512,1024]{1,0:T(8,128)(2,1)} %shard_map.438.d), custom_call_target="tpu_custom_call" | custom-call | tf_op jit(solution)/shard_map/pallas_call | solution.py:1525
  607.8 11.0 %shard_map.445 = (f32[512,1024]{1,0:T(8,128)}, bf16[512,1024]{1,0:T(8,128)(2,1)}, f32[1,1024]{1,0:T(1,128)}) custom-call(bf16[3,512,1024]{2,1,0:T(8,128)(2,1)} %shard_map.439.d.refs_6_, bf16[24,1024,1024]{2,1,0:T(8,128)(2,1)} %bitcast.86, f32[512,1024]{1,0:T(8,128)} %bitcast_add_fusion.x, f32[7,1,1024]{2,1,0:T(1,128)} %reshape.152.g, ...), custom_call_target="tpu_custom_call" | custom-call | flops 3221225472 | bytes 10485760 | tf_op jit(solution)/shard_map/pallas_call | solution.py:1238
  618.9 1.9 fusion.2
  620.8 1.1 pad.25
  621.8 0.7 concatenate.18
  622.8 0.7 select_bitcast_fusion
  623.5 299.2 %shard_map.446.sums.refs_1_ = f32[36,32,1024]{2,1,0:T(8,128)} custom-call(bf16[1,512,1024]{2,1,0:T(8,128)(2,1)} %bitcast.98, bf16[1,512,1024]{2,1,0:T(8,128)(2,1)} %shard_map.418.a.refs_1_, bf16[1,512,1024]{2,1,0:T(8,128)(2,1)} %bitcast.99, bf16[1,512,1024]{2,1,0:T(8,128)(2,1)} %shard_map.428.a.refs_3_, bf16[1,512,1024]{2,1,0:T(8,128)(2,1)} %bitcast.100, ...), custom_call_target="tpu_custom_call" | custom-call | tf_op jit(solution)/shard_map/pallas_call | solution.py:539
  922.7 8.1 fusion.text.refs_2_
  930.8 15.6 %shard_map.448 = (f32[8,128]{1,0:T(8,128)S(1)}, f32[8,128]{1,0:T(8,128)S(1)}) custom-call(f32[36,32,1024]{2,1,0:T(8,128)S(1)} %copy-done.2, f32[500,1024]{1,0:T(8,128)S(1)} %fusion.text.refs_2_, f32[32,8,128]{2,1,0:T(8,128)S(1)} %bitcast.64), custom_call_target="tpu_custom_call" | custom-call | tf_op jit(solution)/shard_map/pallas_call | solution.py:1145
  948.3 19.9 %shard_map.449 = (f32[3,32,3072]{2,1,0:T(8,128)}, f32[3,32,1024]{2,1,0:T(8,128)}, f32[2,32,4096]{2,1,0:T(8,128)}, f32[2,128,1024]{2,1,0:T(8,128)}, f32[7,32]{1,0...) custom-call(f32[8,128]{1,0:T(8,128)} %copy-done.8, ...), custom_call_target="tpu_custom_call" | custom-call | tf_op jit(solution)/shard_map/pallas_call | solution.py:1165
  (67 shorter events, 4.0 us)
Async XLA Ops:
  7.2 366.9 %copy-start = (s32[2]{0:T(128)S(1)}, s32[2]{0:T(128)}, u32[]{:S(2)}) copy-start(s32[2]{0:T(128)} %param.28) | copy-start | bytes 28
  7.2 436.8 %all-gather.3.cloned.1.call-start = ((), (), s32[]{:S(2)}) async-start(), calls=%async_computation | async-start | bytes 8650752 | tf_op jit(solution)/shard_map/all_gather | solution.py:1674
  9.1 913.7 %all-gather.5.cloned.1.call-start = ((), (), s32[]{:S(2)}) async-start(), calls=%async_computation.1 | async-start | bytes 8650752 | tf_op jit(solution)/shard_map/all_gather | solution.py:1708
  13.3 1.2 copy-start.4
  14.5 1.2 copy-start.5
  15.7 1.2 copy-start.6
  17.0 1.0 copy-start.7
  349.5 0.6 copy-start.11
  364.4 8.9 copy-start.15
  364.4 10.6 %copy-start.12 = (s32[2,256]{1,0:T(2,128)S(1)}, s32[2,256]{1,0:T(2,128)}, u32[]{:S(2)}) copy-start(s32[2,256]{1,0:T(2,128)} %param.27) | copy-start | bytes 6148
  457.1 16.1 %copy-start.14 = (s32[1,2,2,128]{3,1,2,0:T(2,128)S(1)}, s32[1,2,2,128]{3,1,2,0:T(2,128)}, u32[]{:S(2)}) copy-start(s32[1,2,2,128]{3,1,2,0:T(2,128)} %copy.64) | copy-start | bytes 6148
  473.1 10.8 %copy-start.9 = (f32[512,8192]{1,0:T(8,128)S(1)}, f32[512,8192]{1,0:T(8,128)}, u32[]{:S(2)}) copy-start(f32[512,8192]{1,0:T(8,128)} %get-tuple-element.160) | copy-start | bytes 50331652
  489.2 3.3 copy-start.10
  571.6 8.4 copy-start.13
  607.8 14.0 %copy-start.16 = (f32[1,1024]{1,0:T(1,128)S(1)}, f32[1,1024]{1,0:T(1,128)}, u32[]{:S(2)}) copy-start(f32[1,1024]{1,0:T(1,128)} %get-tuple-element.127) | copy-start | bytes 12292
  607.8 14.0 %copy-start.17 = (f32[1,1024]{1,0:T(1,128)S(1)}, f32[1,1024]{1,0:T(1,128)}, u32[]{:S(2)}) copy-start(f32[1,1024]{1,0:T(1,128)} %get-tuple-element.126) | copy-start | bytes 12292
  607.8 14.0 %copy-start.18 = (f32[1,1024]{1,0:T(1,128)S(1)}, f32[1,1024]{1,0:T(1,128)}, u32[]{:S(2)}) copy-start(f32[1,1024]{1,0:T(1,128)} %get-tuple-element.123) | copy-start | bytes 12292
  607.8 14.0 %copy-start.19 = (f32[1,1024]{1,0:T(1,128)S(1)}, f32[1,1024]{1,0:T(1,128)}, u32[]{:S(2)}) copy-start(f32[1,1024]{1,0:T(1,128)} %get-tuple-element.122) | copy-start | bytes 12292
  607.8 14.0 %copy-start.20 = (f32[1,1024]{1,0:T(1,128)S(1)}, f32[1,1024]{1,0:T(1,128)}, u32[]{:S(2)}) copy-start(f32[1,1024]{1,0:T(1,128)} %get-tuple-element.121) | copy-start | bytes 12292
  607.8 14.0 %copy-start.21 = (f32[1,1024]{1,0:T(1,128)S(1)}, f32[1,1024]{1,0:T(1,128)}, u32[]{:S(2)}) copy-start(f32[1,1024]{1,0:T(1,128)} %get-tuple-element.125) | copy-start | bytes 12292
  922.7 8.1 copy-start.2
  930.8 15.7 %copy-start.3 = (f32[500,1024]{1,0:T(8,128)}, f32[500,1024]{1,0:T(8,128)S(1)}, u32[]{:S(2)}) copy-start(f32[500,1024]{1,0:T(8,128)S(1)} %fusion.text.refs_2_) | copy-start | bytes 6144004
  946.5 1.8 copy-start.8
  947.7 20.5 %copy-start.1 = (s32[2]{0:T(128)S(1)}, s32[2]{0:T(128)}, u32[]{:S(2)}) copy-start(s32[2]{0:T(128)} %param.28) | copy-start | bytes 28
Sparse Core Ops, SparseCore 0:
  11.7 110.2 all-gather.2
  580.1 79.3 all-gather.4
